TPU v7x, 512 devices: a whole 4x4x16 slice. The times are simulated.
512 devices in a mesh: head: 2 (over y_hi), outer: 8 (over x, core), inner: 32 (over y_lo, z).
Axes of the slice: x: 4, y: 4 (y_hi: 2, y_lo: 2; y = y_hi * 2 + y_lo), z: 16, core: 2. Of those that a mesh axis runs over, the one named last changes fastest.
Arguments:
- query: bfloat16 [32768, 32, 128], P(('outer', 'inner'), 'head'), may hold values from -100 to 100
- grad_out: bfloat16 [32768, 32, 128], P(('outer', 'inner'), 'head'), may hold values from -60 to 60
- out_forward: bfloat16 [32768, 32, 128], P(('outer', 'inner'), 'head'), may hold values from -4 to 4
- k_codes: int32 [32768, 4, 128], P(('outer', 'inner'), 'head'), may hold values from 0 to 15
- k_scale: float32 [4, 128], P('head'), may hold values from 0.15 to 0.45
- k_offset: float32 [4, 128], P('head'), may hold values from 0.975 to 3.825, as said below
- v_codes: int32 [32768, 4, 128], P(('outer', 'inner'), 'head'), may hold values from 0 to 15
- v_scale: float32 [4, 128], P('head'), may hold values from 0.15 to 0.45
- v_offset: float32 [4, 128], P('head'), may hold values from 1.5 to 2.5
Outputs:
- query_grad: bfloat16 [32768, 32, 128], P(('outer', 'inner'), 'head')
- key_grad: bfloat16 [32768, 4, 128], P(('outer', 'inner'), 'head')
- value_grad: bfloat16 [32768, 4, 128], P(('outer', 'inner'), 'head')
- quant_grads: float32 [4, 4, 128], P(None, 'head')
Inputs may be any that keep to these rules, and one draw needn't show every extreme that they name: `k_offset`: each channel's offset lies between 6.5 and 8.5 times its step.
All inputs are finite; a program needn't handle non-finite values.
Results may differ from a plain program's by a relative error of at most 0.04.
Values may be sent and summed in bfloat16 or wider, within the bound.
No kernel may reach another device: no remote copies, remote signals or barrier semaphores. Data moves between devices by JAX's collectives and lax.ppermute only.
A program may use at most 64 MiB of HBM per device.

v0:
```python
import math

import jax
import jax.numpy as jnp
from jax import lax
from jax.sharding import PartitionSpec as P

WIN = 512


clip_limit = 16.0
rope_base = 500000.0


def from_behind(value, axis, by):
    length = lax.axis_size(axis)
    return lax.ppermute(value, axis, [(i, (i + by) % length) for i in range(length)])


def shifted(value, axis, steps):
    count = lax.axis_size(axis)
    leading, last = (max(0, -steps), min(count, count - steps))
    return lax.ppermute(value, axis, [(source, source + steps) for source in range(leading, last)])


def rope_tables(positions, head_size):
    freqs = rope_base ** (-jnp.arange(0, head_size, 2, dtype=jnp.float32) / head_size)
    angles = positions.astype(jnp.float32)[:, None] * freqs[None, :]
    angles = jnp.concatenate([angles, angles], axis=-1)
    return (jnp.cos(angles)[:, None, :], jnp.sin(angles)[:, None, :])


def rotate(values, cosines, sines):
    half = values.shape[-1] // 2
    turned = jnp.concatenate([-values[..., half:], values[..., :half]], axis=-1)
    return values * cosines + turned * sines


def rotate_back(grads, cosines, sines):
    half = grads.shape[-1] // 2
    scaled = grads * sines
    turned = jnp.concatenate([scaled[..., half:], -scaled[..., :half]], axis=-1)
    return grads * cosines + turned


def hadamard_table(order):
    index = jnp.arange(order, dtype=jnp.int32)
    common = jnp.bitwise_and(index[:, None], index[None, :])
    parity = jnp.zeros((order, order), jnp.int32)
    for level in range(order.bit_length() - 1):
        parity = parity + jnp.bitwise_and(jnp.right_shift(common, level), 1)
    signs = 1 - 2 * (parity % 2)
    return signs.astype(jnp.float32) / math.sqrt(order)


def move_keys(stacked, distance):
    inner_part = from_behind(stacked, "inner", distance)
    outer_part = shifted(inner_part, "outer", 1)
    return jnp.where(lax.axis_index("inner") < distance, outer_part, inner_part)


def move_grads(stacked, distance):
    inner_part = from_behind(stacked.astype(jnp.bfloat16), "inner", distance).astype(stacked.dtype)
    direction = 1 if distance > 0 else -1
    outer_part = from_behind(inner_part.astype(jnp.bfloat16), "outer", direction).astype(
        inner_part.dtype
    )
    if distance > 0:
        crossing = lax.axis_index("inner") < distance
    else:
        crossing = lax.axis_index("inner") >= lax.axis_size("inner") + distance
    return jnp.where(crossing, outer_part, inner_part)


def body(query, grad_out, out_forward, k_codes, k_scale, k_offset, v_codes, v_scale, v_offset):
    block_rows, query_heads, head_size = query.shape
    kv_heads = k_codes.shape[1]
    group = query_heads // kv_heads
    reach = WIN // block_rows
    scale = 1.0 / math.sqrt(head_size)
    device_block = lax.axis_index("outer") * lax.axis_size("inner") + lax.axis_index("inner")
    positions = device_block * block_rows + jnp.arange(block_rows, dtype=jnp.int32)
    cosines, sines = rope_tables(positions, head_size)
    key_codes = k_codes.astype(jnp.float32)
    value_codes = v_codes.astype(jnp.float32)
    key_fq = rotate(k_scale[None] * key_codes - k_offset[None], cosines, sines).astype(jnp.bfloat16)
    hadamard = hadamard_table(head_size)
    value_deq = v_scale[None] * value_codes - v_offset[None]
    value_fq = jnp.einsum(
        "tkd,de->tke", value_deq, hadamard, precision=lax.Precision.HIGHEST
    ).astype(jnp.bfloat16)
    queries = query.reshape(block_rows, kv_heads, group, head_size)
    upstream_rows = grad_out.reshape(block_rows, kv_heads, group, head_size)
    delta = jnp.sum(grad_out.astype(jnp.float32) * out_forward.astype(jnp.float32), axis=-1)
    delta = jnp.transpose(delta.reshape(block_rows, kv_heads, group), (1, 2, 0))
    own = jnp.stack([key_fq, value_fq])
    blocks = [own]
    for distance in range(1, reach + 1):
        blocks.append(move_keys(blocks[-1], 1))
    row_index = jnp.arange(block_rows, dtype=jnp.int32)[:, None]
    col_index = jnp.arange(block_rows, dtype=jnp.int32)[None, :]
    masks = []
    for distance in range(reach + 1):
        gap = distance * block_rows + row_index - col_index
        masks.append((gap >= 0) & (gap < WIN) & (device_block >= distance))

    def block_scores(distance):
        return (
            jnp.einsum(
                "tkgd,ukd->kgtu", queries, blocks[distance][0], preferred_element_type=jnp.float32
            )
            * scale
        )

    first = block_scores(0)
    top = jnp.max(jnp.where(masks[0], first, -jnp.inf), axis=-1)
    total = jnp.sum(jnp.where(masks[0], jnp.exp(first - top[..., None]), 0.0), axis=-1)
    for distance in range(1, reach + 1):
        scores = block_scores(distance)
        raised = jnp.maximum(top, jnp.max(jnp.where(masks[distance], scores, -jnp.inf), axis=-1))
        total = total * jnp.exp(top - raised) + jnp.sum(
            jnp.where(masks[distance], jnp.exp(scores - raised[..., None]), 0.0), axis=-1
        )
        top = raised
    log_total = top + jnp.log(total)
    query_acc = jnp.zeros((block_rows, kv_heads, group, head_size), jnp.float32)
    carried = None
    collected = None
    for distance in range(reach + 1):
        scores = block_scores(distance)
        weights = jnp.where(masks[distance], jnp.exp(scores - log_total[..., None]), 0.0)
        weights_low = weights.astype(jnp.bfloat16)
        upstream = jnp.einsum(
            "tkgd,ukd->kgtu", upstream_rows, blocks[distance][1], preferred_element_type=jnp.float32
        )
        score_grad = (weights * (upstream - delta[..., None])).astype(jnp.bfloat16)
        query_acc = query_acc + jnp.einsum(
            "kgtu,ukd->tkgd", score_grad, blocks[distance][0], preferred_element_type=jnp.float32
        )
        key_part = (
            jnp.einsum("kgtu,tkgd->ukd", score_grad, queries, preferred_element_type=jnp.float32)
            * scale
        )
        value_part = jnp.einsum(
            "kgtu,tkgd->ukd", weights_low, upstream_rows, preferred_element_type=jnp.float32
        )
        part = jnp.stack([key_part, value_part])
        carried = part if distance == 0 else move_grads(carried, 1) + part
    collected = move_grads(carried, -reach)
    key_deq_grad = rotate_back(collected[0], cosines, sines)
    value_deq_grad = jnp.einsum(
        "tke,de->tkd", collected[1], hadamard, precision=lax.Precision.HIGHEST
    )
    key_grad = jnp.where((k_codes > 0) & (k_codes < 15), key_deq_grad, 0.0).astype(jnp.bfloat16)
    value_grad = jnp.where((v_codes > 0) & (v_codes < 15), value_deq_grad, 0.0).astype(jnp.bfloat16)
    local_terms = jnp.stack(
        [
            jnp.sum(key_deq_grad * key_codes, axis=0),
            -jnp.sum(key_deq_grad, axis=0),
            jnp.sum(value_deq_grad * value_codes, axis=0),
            -jnp.sum(value_deq_grad, axis=0),
        ]
    )
    summed = lax.psum(local_terms, ("outer", "inner"))
    squares = lax.psum(jnp.sum(summed * summed), "head")
    quant_grads = summed * jnp.minimum(1.0, clip_limit / jnp.sqrt(squares + 1e-06))
    query_grad = (
        (query_acc * scale).reshape(block_rows, query_heads, head_size).astype(jnp.bfloat16)
    )
    return (query_grad, key_grad, value_grad, quant_grads)


def solution(mesh):
    placed = (
        P(("outer", "inner"), "head", None),
        P(("outer", "inner"), "head", None),
        P(("outer", "inner"), "head", None),
        P(("outer", "inner"), "head", None),
        P("head", None),
        P("head", None),
        P(("outer", "inner"), "head", None),
        P("head", None),
        P("head", None),
    )
    return jax.shard_map(
        body,
        mesh=mesh,
        in_specs=placed,
        out_specs=(
            P(("outer", "inner"), "head", None),
            P(("outer", "inner"), "head", None),
            P(("outer", "inner"), "head", None),
            P(None, "head", None),
        ),
        check_vma=False,
    )
```

profile of v0, /device:TPU:48, one launch (start us, length us, event | category | flops | bytes accessed | tf_op | source)
XLA Modules:
  0.0 713.2 jit_solution(5240560702354841233)
XLA Ops:
  1.1 0.5 copy-done.1
  1.8 0.8 copy-done.4
  2.6 0.3 convolution_convert_fusion
  3.0 0.5 copy-done.5
  3.6 3.8 collective-permute-start
  8.2 2.5 collective-permute-done
  10.7 1.9 collective-permute-start.1
  13.2 3.8 collective-permute-start.2
  17.2 10.3 %collective-permute-done.2 = bf16[2,128,2,128]{3,1,2,0:T(8,128)(2,1)S(1)} collective-permute-done((bf16[2,128,2,128]{3,1,2,0:T(8,128)(2,1)S(1)}, bf16[2,128,2,128]{3,1,2,0:T(8,128)(2,1)S(1)}, u32[]{:S(2)}, u32[]{:S(2)}) %collective-permute-start.2) | collective-permute-done | bytes 131104 | tf_op jit(solution)/shard_map/ppermute | solution.py:17
  27.5 4.7 collective-permute-start.3
  32.2 0.3 multiply_reduce_fusion
  32.7 1.9 collective-permute-start.4
  34.8 7.5 %collective-permute-done.4 = bf16[2,128,2,128]{3,1,2,0:T(8,128)(2,1)S(1)} collective-permute-done((bf16[2,128,2,128]{3,1,2,0:T(8,128)(2,1)S(1)}, bf16[2,128,2,128]{3,1,2,0:T(8,128)(2,1)S(1)}, u32[]{:S(2)}, u32[]{:S(2)}) %collective-permute-start.4) | collective-permute-done | bytes 131104 | tf_op jit(solution)/shard_map/ppermute | solution.py:17
  42.2 5.6 collective-permute-start.5
  48.1 0.6 collective-permute-done.5
  48.8 1.9 collective-permute-start.6
  51.1 6.4 collective-permute-done.6
  57.5 5.7 collective-permute-start.7
  63.5 0.6 collective-permute-done.7
  64.5 0.4 select_reduce_fusion
  64.9 0.4 select_reduce_fusion.2
  65.4 0.3 fusion.35
  65.7 0.3 convolution_bitcast_fusion.11
  66.1 0.5 copy-done.6
  66.6 0.4 fusion.23
  67.0 0.4 fusion.22
  67.3 0.4 fusion.21
  67.7 0.4 fusion.20
  68.1 0.4 fusion.19
  68.8 0.3 fusion.81
  69.2 1.9 collective-permute-start.8
  71.1 0.3 convolution_add_fusion.1
  71.5 0.3 convolution_bitcast_fusion.9
  71.8 6.1 collective-permute-done.8
  77.9 3.7 collective-permute-start.9
  81.8 2.5 collective-permute-done.9
  84.4 1.9 collective-permute-start.10
  86.4 0.3 convolution_bitcast_fusion.7
  86.7 6.4 collective-permute-done.10
  93.1 1.8 collective-permute-start.11
  95.3 3.5 collective-permute-done.11
  98.8 1.9 collective-permute-start.12
  100.7 0.3 convolution_bitcast_fusion.5
  101.0 7.3 %collective-permute-done.12 = bf16[2,128,2,128]{3,1,2,0:T(8,128)(2,1)S(1)} collective-permute-done((bf16[2,128,2,128]{3,1,2,0:T(8,128)(2,1)S(1)}, bf16[2,128,2,128]{3,1,2,0:T(8,128)(2,1)S(1)}, u32[]{:S(2)}, u32[]{:S(2)}) %collective-permute-start.12) | collective-permute-done | bytes 131104 | tf_op jit(solution)/shard_map/ppermute | solution.py:17
  108.4 0.6 collective-permute-start.13
  109.3 4.7 collective-permute-done.13
  114.0 1.9 collective-permute-start.14
  115.9 0.3 fusion.109
  116.3 7.1 collective-permute-done.14
  123.7 5.3 collective-permute-done.15
  129.0 1.9 collective-permute-start.16
  131.0 0.3 fusion.108
  131.3 13.4 %collective-permute-done.16 = bf16[2,128,2,128]{3,1,2,0:T(8,128)(2,1)S(1)} collective-permute-done((bf16[2,128,2,128]{3,1,2,0:T(8,128)(2,1)S(1)}, bf16[2,128,2,128]{3,1,2,0:T(8,128)(2,1)S(1)}, u32[]{:S(2)}, u32[]{:S(2)}) %collective-permute-start.16) | collective-permute-done | bytes 131104 | tf_op jit(solution)/shard_map/ppermute | solution.py:17
  144.7 1.2 collective-permute-start.17
  145.9 0.4 fusion.18
  146.3 1.2 copy.144
  147.5 0.9 collective-permute-done.17
  148.5 0.3 select_convert_fusion
  149.1 553.7 %psum.14 = f32[4,2,128]{2,1,0:T(2,128)S(1)} all-reduce(f32[4,2,128]{2,1,0:T(2,128)S(1)} %pad_maximum_fusion.3), channel_id=1, replica_groups=mesh['head'=2,'outer'=8,'inner'=32] {'outer','inner'}, use_global_device_ids=true, to_apply=%region_15.16 | all-reduce | flops 1024 | bytes 8192 | tf_op jit(solution)/shard_map/psum | solution.py:164
  702.8 0.6 multiply_reduce_fusion.3
  703.4 0.7 copy.146
  704.1 7.1 psum.15
  711.9 0.7 copy.145
  712.6 0.6 broadcast_multiply_fusion.1
  (75 shorter events, 5.8 us)
Async XLA Ops:
  0.6 7.1 copy-start
  0.7 1.0 copy-start.1
  0.8 0.9 copy-start.7
  0.8 0.9 copy-start.8
  1.7 0.9 copy-start.4
  1.7 0.9 copy-start.9
  1.7 0.9 copy-start.10
  2.9 0.6 copy-start.5
  3.6 7.1 collective-permute-start
  7.7 24.5 %copy-start.3 = (bf16[128,16,128]{2,1,0:T(8,128)(2,1)S(1)}, bf16[128,16,128]{2,1,0:T(8,128)(2,1)}, u32[]{:S(2)}) copy-start(bf16[128,16,128]{2,1,0:T(8,128)(2,1)} %param.10) | copy-start | bytes 1572868
  8.0 24.1 %copy-start.2 = (bf16[128,16,128]{2,1,0:T(8,128)(2,1)S(1)}, bf16[128,16,128]{2,1,0:T(8,128)(2,1)}, u32[]{:S(2)}) copy-start(bf16[128,16,128]{2,1,0:T(8,128)(2,1)} %param.11) | copy-start | bytes 1572868
  10.7 2.4 collective-permute-start.1
  13.2 14.3 %collective-permute-start.2 = (bf16[2,128,2,128]{3,1,2,0:T(8,128)(2,1)S(1)}, bf16[2,128,2,128]{3,1,2,0:T(8,128)(2,1)S(1)}, u32[]{:S(2)}, u32[]{:S(2)}) collective-permute-start(bf16[2,128,2,128]{3,1,2,0:T(8,128)(2,1)S(1)} %broadcast_select_fusion.3), channel_id=1, source_target_pairs={{0,1},{1,2},{2,3},{3,4},{4,5},{5,6},{6,7},{7,8},{8,9},{9,10},{10,1... | collective-permute-start | bytes 393224 | tf_op jit(solution)/shard_map/ppermute | solution.py:17
  27.5 5.1 collective-permute-start.3
  32.7 9.6 %collective-permute-start.4 = (bf16[2,128,2,128]{3,1,2,0:T(8,128)(2,1)S(1)}, bf16[2,128,2,128]{3,1,2,0:T(8,128)(2,1)S(1)}, u32[]{:S(2)}, u32[]{:S(2)}) collective-permute-start(bf16[2,128,2,128]{3,1,2,0:T(8,128)(2,1)S(1)} %broadcast_select_fusion.2), channel_id=1, source_target_pairs={{0,1},{1,2},{2,3},{3,4},{4,5},{5,6},{6,7},{7,8},{8,9},{9,10},{10,1... | collective-permute-start | bytes 393224 | tf_op jit(solution)/shard_map/ppermute | solution.py:17
  42.2 6.5 collective-permute-start.5
  48.8 8.7 %collective-permute-start.6 = (bf16[2,128,2,128]{3,1,2,0:T(8,128)(2,1)S(1)}, bf16[2,128,2,128]{3,1,2,0:T(8,128)(2,1)S(1)}, u32[]{:S(2)}, u32[]{:S(2)}) collective-permute-start(bf16[2,128,2,128]{3,1,2,0:T(8,128)(2,1)S(1)} %broadcast_select_fusion.1), channel_id=1, source_target_pairs={{0,1},{1,2},{2,3},{3,4},{4,5},{5,6},{6,7},{7,8},{8,9},{9,10},{10,1... | collective-permute-start | bytes 393224 | tf_op jit(solution)/shard_map/ppermute | solution.py:17
  57.5 6.7 collective-permute-start.7
  65.7 0.8 copy-start.6
  69.2 8.7 %collective-permute-start.8 = (bf16[2,128,2,128]{3,1,2,0:T(8,128)(2,1)S(1)}, bf16[2,128,2,128]{3,1,2,0:T(8,128)(2,1)S(1)}, u32[]{:S(2)}, u32[]{:S(2)}) collective-permute-start(bf16[2,128,2,128]{3,1,2,0:T(8,128)(2,1)S(1)} %pad_maximum_fusion.1), channel_id=1, source_target_pairs={{0,1},{1,2},{2,3},{3,4},{4,5},{5,6},{6,7},{7,8},{8,9},{9,10},{10,1... | collective-permute-start | bytes 393224 | tf_op jit(solution)/shard_map/ppermute | solution.py:17
  77.9 6.5 collective-permute-start.9
  84.4 8.7 %collective-permute-start.10 = (bf16[2,128,2,128]{3,1,2,0:T(8,128)(2,1)S(1)}, bf16[2,128,2,128]{3,1,2,0:T(8,128)(2,1)S(1)}, u32[]{:S(2)}, u32[]{:S(2)}) collective-permute-start(bf16[2,128,2,128]{3,1,2,0:T(8,128)(2,1)S(1)} %fusion.62), channel_id=1, source_target_pairs={{0,1},{1,2},{2,3},{3,4},{4,5},{5,6},{6,7},{7,8},{8,9},{9,10},{10,1... | collective-permute-start | bytes 393224 | tf_op jit(solution)/shard_map/ppermute | solution.py:17
  93.1 5.6 collective-permute-start.11
  98.8 9.6 %collective-permute-start.12 = (bf16[2,128,2,128]{3,1,2,0:T(8,128)(2,1)S(1)}, bf16[2,128,2,128]{3,1,2,0:T(8,128)(2,1)S(1)}, u32[]{:S(2)}, u32[]{:S(2)}) collective-permute-start(bf16[2,128,2,128]{3,1,2,0:T(8,128)(2,1)S(1)} %fusion.63), channel_id=1, source_target_pairs={{0,1},{1,2},{2,3},{3,4},{4,5},{5,6},{6,7},{7,8},{8,9},{9,10},{10,1... | collective-permute-start | bytes 393224 | tf_op jit(solution)/shard_map/ppermute | solution.py:17
  108.4 5.6 collective-permute-start.13
  114.0 9.4 %collective-permute-start.14 = (bf16[2,128,2,128]{3,1,2,0:T(8,128)(2,1)S(1)}, bf16[2,128,2,128]{3,1,2,0:T(8,128)(2,1)S(1)}, u32[]{:S(2)}, u32[]{:S(2)}) collective-permute-start(bf16[2,128,2,128]{3,1,2,0:T(8,128)(2,1)S(1)} %fusion.64), channel_id=1, source_target_pairs={{0,1},{1,2},{2,3},{3,4},{4,5},{5,6},{6,7},{7,8},{8,9},{9,10},{10,1... | collective-permute-start | bytes 393224 | tf_op jit(solution)/shard_map/ppermute | solution.py:17
  123.4 5.6 collective-permute-start.15
  129.0 15.6 %collective-permute-start.16 = (bf16[2,128,2,128]{3,1,2,0:T(8,128)(2,1)S(1)}, bf16[2,128,2,128]{3,1,2,0:T(8,128)(2,1)S(1)}, u32[]{:S(2)}, u32[]{:S(2)}) collective-permute-start(bf16[2,128,2,128]{3,1,2,0:T(8,128)(2,1)S(1)} %fusion.65), channel_id=1, source_target_pairs={{0,28},{1,29},{2,30},{3,31},{4,0},{5,1},{6,2},{7,3},{8,4},{9,5},{1... | collective-permute-start | bytes 393224 | tf_op jit(solution)/shard_map/ppermute | solution.py:17
  144.7 3.8 collective-permute-start.17
where the time goes:
time: 714 us; the launch traced here: 713 us
  blocking collectives  561 us (79%)
  waiting for transfers between devices  85.2 us (12%)
  starting transfers between devices  46.3 us (6%)
  matrix products  9.1 us (1%)
    psum x1, blocking collectives, body(): summed = lax.psum(local_terms, ('outer', 'inner'))  554 us
    ppermute x14, waiting for transfers between devices, from_behind(): lax.ppermute(value, axis, [(i, (i + by) % length) for i in range(length)])  83.9 us
    ppermute x14, starting transfers between devices, from_behind(): lax.ppermute(value, axis, [(i, (i + by) % length) for i in range(length)])  28.5 us
    ppermute x4, starting transfers between devices, shifted(): lax.ppermute(value, axis, [(source, source + steps) for source in range(l...  17.8 us
  transfers between devices with their start and end apart: 18, of which 17 were waited for; matrix products, arithmetic and copies ran while one was open for 1% of the time, Pallas kernels for 0%

commit v1 on v0

v1 whole, which is shorter than its diff:
```python
import math

import jax
import jax.numpy as jnp
from jax import lax
from jax.sharding import Mesh, PartitionSpec as P

WIN = 512
clip_limit = 16.0
rope_base = 500000.0
TOK = ("x", "core", "ylo", "z")
FLAT = ("head", "x", "core", "ylo")


def shift(value, by):
    count = 1
    for axis in TOK:
        count *= lax.axis_size(axis)
    pairs = [(i, i + by) for i in range(count) if 0 <= i + by < count]
    return lax.ppermute(value, TOK, pairs)


def gather_all(value, axes):
    count = 1
    for axis in (axes,) if isinstance(axes, str) else axes:
        count *= lax.axis_size(axis)
    spread = jnp.broadcast_to(value[None], (count,) + value.shape)
    return lax.all_to_all(spread, axes, 0, 0)


def rope_tables(positions, head_size):
    freqs = rope_base ** (-jnp.arange(0, head_size, 2, dtype=jnp.float32) / head_size)
    angles = positions.astype(jnp.float32)[:, None] * freqs[None, :]
    angles = jnp.concatenate([angles, angles], axis=-1)
    return (jnp.cos(angles)[:, None, :], jnp.sin(angles)[:, None, :])


def rotate(values, cosines, sines):
    half = values.shape[-1] // 2
    turned = jnp.concatenate([-values[..., half:], values[..., :half]], axis=-1)
    return values * cosines + turned * sines


def rotate_back(grads, cosines, sines):
    half = grads.shape[-1] // 2
    scaled = grads * sines
    turned = jnp.concatenate([scaled[..., half:], -scaled[..., :half]], axis=-1)
    return grads * cosines + turned


def hadamard_table(order):
    index = jnp.arange(order, dtype=jnp.int32)
    common = jnp.bitwise_and(index[:, None], index[None, :])
    parity = jnp.zeros((order, order), jnp.int32)
    for level in range(order.bit_length() - 1):
        parity = parity + jnp.bitwise_and(jnp.right_shift(common, level), 1)
    signs = 1 - 2 * (parity % 2)
    return signs.astype(jnp.float32) / math.sqrt(order)


def body(query, grad_out, out_forward, k_codes, k_scale, k_offset, v_codes, v_scale, v_offset):
    block_rows, query_heads, head_size = query.shape
    kv_heads = k_codes.shape[1]
    group = query_heads // kv_heads
    reach = WIN // block_rows
    scale = 1.0 / math.sqrt(head_size)
    device_block = jnp.int32(0)
    for axis in TOK:
        device_block = device_block * lax.axis_size(axis) + lax.axis_index(axis)
    hadamard = hadamard_table(head_size)

    own = jnp.stack([k_codes, v_codes]).astype(jnp.bfloat16)
    one = shift(own, 1)
    two = shift(own, 2)
    far = shift(jnp.stack([one, two]), 2)
    codes = [own, one, two, far[0], far[1]]

    tables = []
    for distance in range(reach + 1):
        first_row = (device_block - distance) * block_rows
        tables.append(rope_tables(first_row + jnp.arange(block_rows, dtype=jnp.int32), head_size))

    def key_block(distance):
        deq = k_scale[None] * codes[distance][0].astype(jnp.float32) - k_offset[None]
        return rotate(deq, *tables[distance]).astype(jnp.bfloat16)

    def value_block(distance):
        deq = v_scale[None] * codes[distance][1].astype(jnp.float32) - v_offset[None]
        return jnp.einsum("tkd,de->tke", deq, hadamard, precision=lax.Precision.HIGHEST).astype(
            jnp.bfloat16
        )

    keys = [key_block(distance) for distance in range(reach + 1)]
    values = [value_block(distance) for distance in range(reach + 1)]
    queries = query.reshape(block_rows, kv_heads, group, head_size)
    upstream_rows = grad_out.reshape(block_rows, kv_heads, group, head_size)
    delta = jnp.sum(grad_out.astype(jnp.float32) * out_forward.astype(jnp.float32), axis=-1)
    delta = jnp.transpose(delta.reshape(block_rows, kv_heads, group), (1, 2, 0))
    row_index = jnp.arange(block_rows, dtype=jnp.int32)[:, None]
    col_index = jnp.arange(block_rows, dtype=jnp.int32)[None, :]
    masks = []
    for distance in range(reach + 1):
        gap = distance * block_rows + row_index - col_index
        masks.append((gap >= 0) & (gap < WIN) & (device_block >= distance))

    def block_scores(distance):
        return (
            jnp.einsum("tkgd,ukd->kgtu", queries, keys[distance], preferred_element_type=jnp.float32)
            * scale
        )

    first = block_scores(0)
    top = jnp.max(jnp.where(masks[0], first, -jnp.inf), axis=-1)
    total = jnp.sum(jnp.where(masks[0], jnp.exp(first - top[..., None]), 0.0), axis=-1)
    for distance in range(1, reach + 1):
        scores = block_scores(distance)
        raised = jnp.maximum(top, jnp.max(jnp.where(masks[distance], scores, -jnp.inf), axis=-1))
        total = total * jnp.exp(top - raised) + jnp.sum(
            jnp.where(masks[distance], jnp.exp(scores - raised[..., None]), 0.0), axis=-1
        )
        top = raised
    log_total = top + jnp.log(total)
    query_acc = jnp.zeros((block_rows, kv_heads, group, head_size), jnp.float32)
    parts = [None] * (reach + 1)
    local_terms = 0.0
    for distance in reversed(range(reach + 1)):
        scores = block_scores(distance)
        weights = jnp.where(masks[distance], jnp.exp(scores - log_total[..., None]), 0.0)
        weights_low = weights.astype(jnp.bfloat16)
        upstream = jnp.einsum(
            "tkgd,ukd->kgtu", upstream_rows, values[distance], preferred_element_type=jnp.float32
        )
        score_grad = (weights * (upstream - delta[..., None])).astype(jnp.bfloat16)
        query_acc = query_acc + jnp.einsum(
            "kgtu,ukd->tkgd", score_grad, keys[distance], preferred_element_type=jnp.float32
        )
        key_part = (
            jnp.einsum("kgtu,tkgd->ukd", score_grad, queries, preferred_element_type=jnp.float32)
            * scale
        )
        value_part = jnp.einsum(
            "kgtu,tkgd->ukd", weights_low, upstream_rows, preferred_element_type=jnp.float32
        )
        parts[distance] = jnp.stack([key_part, value_part])
        key_deq_part = rotate_back(key_part, *tables[distance])
        value_deq_part = jnp.einsum(
            "tke,de->tkd", value_part, hadamard, precision=lax.Precision.HIGHEST
        )
        local_terms = local_terms + jnp.stack(
            [
                jnp.sum(key_deq_part * codes[distance][0].astype(jnp.float32), axis=0),
                -jnp.sum(key_deq_part, axis=0),
                jnp.sum(value_deq_part * codes[distance][1].astype(jnp.float32), axis=0),
                -jnp.sum(value_deq_part, axis=0),
            ]
        )

    back = shift(jnp.stack([parts[3], parts[4]]).astype(jnp.bfloat16), -2)
    column = jnp.sum(gather_all(local_terms, "z"), axis=0)
    near = (parts[1] + back[0].astype(jnp.float32)).astype(jnp.bfloat16)
    next_near = (parts[2] + back[1].astype(jnp.float32)).astype(jnp.bfloat16)
    near = shift(near, -1)
    next_near = shift(next_near, -2)
    columns = gather_all(column, FLAT)
    columns = jnp.sum(columns.reshape((lax.axis_size("head"), -1) + column.shape), axis=1)
    squares = jnp.sum(columns * columns)
    summed = lax.dynamic_index_in_dim(columns, lax.axis_index("head"), 0, keepdims=False)
    quant_grads = summed * jnp.minimum(1.0, clip_limit / jnp.sqrt(squares + 1e-06))

    collected = parts[0] + near.astype(jnp.float32) + next_near.astype(jnp.float32)
    key_deq_grad = rotate_back(collected[0], *tables[0])
    value_deq_grad = jnp.einsum(
        "tke,de->tkd", collected[1], hadamard, precision=lax.Precision.HIGHEST
    )
    key_grad = jnp.where((k_codes > 0) & (k_codes < 15), key_deq_grad, 0.0).astype(jnp.bfloat16)
    value_grad = jnp.where((v_codes > 0) & (v_codes < 15), value_deq_grad, 0.0).astype(jnp.bfloat16)
    query_grad = (
        (query_acc * scale).reshape(block_rows, query_heads, head_size).astype(jnp.bfloat16)
    )
    return (query_grad, key_grad, value_grad, quant_grads)


def solution(mesh):
    sizes = (mesh.shape["head"], mesh.shape["outer"] // 2, 2, 2, mesh.shape["inner"] // 2)
    split = Mesh(mesh.devices.reshape(sizes), ("head",) + TOK)
    rows = P(TOK, "head", None)
    steps = P("head", None)
    return jax.shard_map(
        body,
        mesh=split,
        in_specs=(rows, rows, rows, rows, steps, steps, rows, steps, steps),
        out_specs=(rows, rows, rows, P(None, "head", None)),
        check_vma=False,
    )
```

time: 714 us -> 138 us (0.19)
  the two profiles are of different devices: /device:TPU:48 before, /device:TPU:1 now
where the time goes in v1:
time: 138 us; the launch traced here: 136 us
  starting transfers between devices  50.7 us (37%)
  local copies, waits for them, and re-layouts  32.2 us (23%)
  other arithmetic  18.5 us (13%)
  matrix products  17.8 us (13%)
  waiting for transfers between devices  14.5 us (11%)
  between operations  2.65 us (2%)
    ppermute x6, starting transfers between devices, shift(): return lax.ppermute(value, TOK, pairs)  33 us
    unnamed x153, local copies, waits for them, and re-layouts  20.3 us
    all_to_all x2, starting transfers between devices, gather_all(): return lax.all_to_all(spread, axes, 0, 0)  17.7 us
    ppermute x6, waiting for transfers between devices, shift(): return lax.ppermute(value, TOK, pairs)  14.5 us
    dot_general x5, matrix products, body(): jnp.einsum('kgtu,tkgd->ukd', weights_low, upstream_rows, preferred_elemen...  3.93 us
    mul x5, local copies, waits for them, and re-layouts, rotate_back(): scaled = grads * sines  3.61 us
    mul x5, local copies, waits for them, and re-layouts, rotate_back(): return grads * cosines + turned  3.58 us
    dot_general x5, matrix products, body(): jnp.einsum('tke,de->tkd', value_part, hadamard, precision=lax.Precision.H...  3.34 us
  transfers between devices with their start and end apart: 8, of which 3 were waited for; matrix products, arithmetic and copies ran while one was open for 15% of the time, Pallas kernels for 0%

profile of v1, /device:TPU:1, one launch (start us, length us, event | category | flops | bytes accessed | tf_op | source)
XLA Modules:
  0.0 136.3 jit_solution(16902028122266241711)
XLA Ops:
  0.6 1.0 copy.464
  1.7 0.9 copy-done.52
  3.4 0.7 pad_maximum_fusion.2
  4.0 5.7 %collective-permute-start.1 = (bf16[2,128,2,128]{1,3,2,0:T(8,128)(2,1)}, bf16[2,128,2,128]{1,3,2,0:T(8,128)(2,1)S(1)}, u32[]{:S(2)}, u32[]{:S(2)}) collective-permute-start(bf16[2,128,2,128]{1,3,2,0:T(8,128)(2,1)} %pad_maximum_fusion.2), channel_id=1, source_target_pairs={{0,2},{1,3},{2,4},{3,5},{4,6},{5,7},{6,8},{7,9},{8,10},{9,11},{10,... | collective-permute-start | bytes 393224 | tf_op jit(solution)/shard_map/ppermute | solution.py:20
  9.8 3.5 %collective-permute-start = (bf16[2,128,2,128]{1,3,2,0:T(8,128)(2,1)}, bf16[2,128,2,128]{1,3,2,0:T(8,128)(2,1)S(1)}, u32[]{:S(2)}, u32[]{:S(2)}) collective-permute-start(bf16[2,128,2,128]{1,3,2,0:T(8,128)(2,1)} %pad_maximum_fusion.2), channel_id=1, source_target_pairs={{0,1},{1,2},{2,3},{3,4},{4,5},{5,6},{6,7},{7,8},{8,9},{9,10},{10,1... | collective-permute-start | bytes 393224 | tf_op jit(solution)/shard_map/ppermute | solution.py:20
  15.5 0.7 copy.532
  16.2 0.7 copy.533
  17.7 0.7 copy.548
  18.6 0.7 copy.549
  19.5 0.7 copy.545
  20.3 0.7 copy.544
  22.0 0.7 copy.540
  22.7 0.7 copy.541
  23.8 0.7 copy.537
  24.6 0.7 copy.536
  25.3 0.7 copy-done.72
  26.6 6.2 %collective-permute-start.2 = (bf16[2,2,128,2,128]{2,4,3,1,0:T(8,128)(2,1)S(1)}, bf16[2,2,128,2,128]{2,4,3,1,0:T(8,128)(2,1)S(1)}, u32[]{:S(2)}, u32[]{:S(2)}) collective-permute-start(bf16[2,2,128,2,128]{2,4,3,1,0:T(8,128)(2,1)S(1)} %pad_maximum_fusion), channel_id=1, source_target_pairs={{0,2},{1,3},{2,4},{3,5},{4,6},{5,7},{6,8},{7,9},{8,10},{9,11},{10,... | collective-permute-start | bytes 786440 | tf_op jit(solution)/shard_map/ppermute | solution.py:20
  33.9 11.7 %collective-permute-done.2 = bf16[2,2,128,2,128]{2,4,3,1,0:T(8,128)(2,1)S(1)} collective-permute-done((bf16[2,2,128,2,128]{2,4,3,1,0:T(8,128)(2,1)S(1)}, bf16[2,2,128,2,128]{2,4,3,1,0:T(8,128)(2,1)S(1)}, u32[]{:S(2)}, u32[]{:S(2)}) %collective-permute-start.2) | collective-permute-done | bytes 262176 | tf_op jit(solution)/shard_map/ppermute | solution.py:20
  49.6 0.6 convert_bitcast_fusion
  50.3 1.0 fusion.376
  51.7 0.6 convert_bitcast_fusion.1
  52.4 1.1 fusion.377
  53.4 1.0 fusion.37
  54.5 1.0 fusion.35
  55.5 1.1 fusion.33
  61.1 0.9 convolution_bitcast_fusion.5
  62.5 0.9 convolution_bitcast_fusion.10
  64.6 1.0 copy.539
  65.8 0.7 copy-done.45
  66.5 0.6 multiply_bitcast_fusion.3
  67.2 0.8 copy-done.44
  68.0 0.6 multiply_bitcast_fusion.4
  69.8 0.6 negate_bitcast_fusion.7
  71.4 0.6 negate_bitcast_fusion
  72.1 0.8 copy-done.5
  72.9 0.7 fusion.63
  74.2 0.6 negate_bitcast_fusion.2
  74.9 0.8 copy-done.56
  76.8 0.7 copy-done.38
  77.6 0.8 copy-done.15
  79.3 0.7 multiply_bitcast_fusion.1
  80.0 0.9 copy-done.11
  81.1 0.7 copy-done.2
  81.8 0.7 multiply_bitcast_fusion.2
  82.5 0.9 copy-done.9
  84.3 0.6 broadcast_in_dim.62
  85.0 9.6 %all-to-all-start = ((f32[16,4,2,128]{3,2,1,0:T(2,128)}), f32[16,4,2,128]{3,2,1,0:T(2,128)}, u32[]{:S(2)}, u32[]{:S(2)}) async-start(f32[16,4,2,128]{3,2,1,0:T(2,128)} %broadcast_in_dim.62), calls=%async_computation | async-start | bytes 131072 | tf_op jit(solution)/shard_map/all_to_all | solution.py:28
  94.6 0.8 copy-done.41
  95.5 0.7 pad_maximum_fusion.1
  96.2 9.0 %collective-permute-start.3 = (bf16[2,2,128,2,128]{2,4,3,1,0:T(8,128)(2,1)}, bf16[2,2,128,2,128]{2,4,3,1,0:T(8,128)(2,1)}, u32[]{:S(2)}, u32[]{:S(2)}) collective-permute-start(bf16[2,2,128,2,128]{2,4,3,1,0:T(8,128)(2,1)} %pad_maximum_fusion.1), channel_id=1, source_target_pairs={{2,0},{3,1},{4,2},{5,3},{6,4},{7,5},{8,6},{9,7},{10,8},{11,9},{12,... | collective-permute-start | bytes 786440 | tf_op jit(solution)/shard_map/ppermute | solution.py:20
  106.7 0.7 copy-done.1
  107.8 1.2 copy.555
  108.9 0.9 reduce_sum.287
  109.8 0.7 broadcast_in_dim.63
  110.5 8.2 %all-to-all-start.1 = ((f32[32,4,2,128]{3,2,1,0:T(2,128)}), f32[32,4,2,128]{3,2,1,0:T(2,128)S(1)}, u32[]{:S(2)}, u32[]{:S(2)}) async-start(f32[32,4,2,128]{3,2,1,0:T(2,128)} %broadcast_in_dim.63), calls=%async_computation.1 | async-start | bytes 262144 | tf_op jit(solution)/shard_map/all_to_all | solution.py:28
  118.7 1.0 fusion.57
  119.8 4.5 %collective-permute-start.4 = (bf16[2,128,2,128]{1,3,2,0:T(8,128)(2,1)S(1)}, bf16[2,128,2,128]{1,3,2,0:T(8,128)(2,1)S(1)}, u32[]{:S(2)}, u32[]{:S(2)}) collective-permute-start(bf16[2,128,2,128]{1,3,2,0:T(8,128)(2,1)S(1)} %get-tuple-element.54), channel_id=1, source_target_pairs={{1,0},{2,1},{3,2},{4,3},{5,4},{6,5},{7,6},{8,7},{9,8},{10,9},{11,1... | collective-permute-start | bytes 393224 | tf_op jit(solution)/shard_map/ppermute | solution.py:20
  124.3 4.0 %collective-permute-start.5 = (bf16[2,128,2,128]{1,3,2,0:T(8,128)(2,1)S(1)}, bf16[2,128,2,128]{1,3,2,0:T(8,128)(2,1)S(1)}, u32[]{:S(2)}, u32[]{:S(2)}) collective-permute-start(bf16[2,128,2,128]{1,3,2,0:T(8,128)(2,1)S(1)} %get-tuple-element.55), channel_id=1, source_target_pairs={{2,0},{3,1},{4,2},{5,3},{6,4},{7,5},{8,6},{9,7},{10,8},{11,9},{12,... | collective-permute-start | bytes 393224 | tf_op jit(solution)/shard_map/ppermute | solution.py:20
  128.3 0.6 multiply_reduce_fusion.1
  129.6 0.6 multiply_bitcast_fusion.8
  130.2 2.7 %collective-permute-done.5 = bf16[2,128,2,128]{1,3,2,0:T(8,128)(2,1)S(1)} collective-permute-done((bf16[2,128,2,128]{1,3,2,0:T(8,128)(2,1)S(1)}, bf16[2,128,2,128]{1,3,2,0:T(8,128)(2,1)S(1)}, u32[]{:S(2)}, u32[]{:S(2)}) %collective-permute-start.5) | collective-permute-done | bytes 131104 | tf_op jit(solution)/shard_map/ppermute | solution.py:20
  133.9 0.8 copy.557
  134.7 0.9 copy-done.7
  135.6 0.8 copy.556
  (254 shorter events, 26.2 us)
Async XLA Ops:
  1.6 23.6 %copy-start.4 = (s32[128,2,128]{0,2,1:T(8,128)}, s32[128,2,128]{0,2,1:T(8,128)S(1)}, u32[]{:S(2)}) copy-start(s32[128,2,128]{0,2,1:T(8,128)S(1)} %copy.464) | copy-start | bytes 393220
  1.6 1.0 copy-start.52
  1.7 1.0 copy-start.60
  1.7 1.0 copy-start.61
  2.6 11.9 %copy-start.30 = (bf16[128,16,128]{2,1,0:T(8,128)(2,1)S(1)}, bf16[128,16,128]{2,1,0:T(8,128)(2,1)}, u32[]{:S(2)}) copy-start(bf16[128,16,128]{2,1,0:T(8,128)(2,1)} %param.10) | copy-start | bytes 1572868
  2.7 11.8 %copy-start.28 = (bf16[128,16,128]{2,1,0:T(8,128)(2,1)S(1)}, bf16[128,16,128]{2,1,0:T(8,128)(2,1)}, u32[]{:S(2)}) copy-start(bf16[128,16,128]{2,1,0:T(8,128)(2,1)} %param.11) | copy-start | bytes 1572868
  3.4 42.2 %copy-start.14 = (bf16[128,2,128]{0,2,1:T(8,128)(2,1)}, bf16[128,2,128]{0,2,1:T(8,128)(2,1)S(1)}, u32[]{:S(2)}) copy-start(bf16[128,2,128]{0,2,1:T(8,128)(2,1)S(1)} %get-tuple-element.49) | copy-start | bytes 196612
  4.0 22.4 %collective-permute-start.1 = (bf16[2,128,2,128]{1,3,2,0:T(8,128)(2,1)}, bf16[2,128,2,128]{1,3,2,0:T(8,128)(2,1)S(1)}, u32[]{:S(2)}, u32[]{:S(2)}) collective-permute-start(bf16[2,128,2,128]{1,3,2,0:T(8,128)(2,1)} %pad_maximum_fusion.2), channel_id=1, source_target_pairs={{0,2},{1,3},{2,4},{3,5},{4,6},{5,7},{6,8},{7,9},{8,10},{9,11},{10,... | collective-permute-start | bytes 393224 | tf_op jit(solution)/shard_map/ppermute | solution.py:20
  9.8 16.8 %collective-permute-start = (bf16[2,128,2,128]{1,3,2,0:T(8,128)(2,1)}, bf16[2,128,2,128]{1,3,2,0:T(8,128)(2,1)S(1)}, u32[]{:S(2)}, u32[]{:S(2)}) collective-permute-start(bf16[2,128,2,128]{1,3,2,0:T(8,128)(2,1)} %pad_maximum_fusion.2), channel_id=1, source_target_pairs={{0,1},{1,2},{2,3},{3,4},{4,5},{5,6},{6,7},{7,8},{8,9},{9,10},{10,1... | collective-permute-start | bytes 393224 | tf_op jit(solution)/shard_map/ppermute | solution.py:20
  14.1 40.3 %copy-start.48 = (pred[128,128]{0,1:T(8,128)(4,1)}, pred[128,128]{0,1:T(8,128)(4,1)S(1)}, u32[]{:S(2)}) copy-start(pred[128,128]{0,1:T(8,128)(4,1)S(1)} %copy.475) | copy-start | bytes 49156
  14.5 41.0 %copy-start.50 = (pred[128,128]{0,1:T(8,128)(4,1)}, pred[128,128]{0,1:T(8,128)(4,1)S(1)}, u32[]{:S(2)}) copy-start(pred[128,128]{0,1:T(8,128)(4,1)S(1)} %copy.470) | copy-start | bytes 49156
  15.0 44.1 %copy-start.62 = (f32[128,16]{0,1:T(8,128)}, f32[128,16]{0,1:T(8,128)S(1)}, u32[]{:S(2)}) copy-start(f32[128,16]{0,1:T(8,128)S(1)} %copy.492) | copy-start | bytes 24580
  17.7 3.3 %copy-start.29 = (bf16[128,16,128]{2,1,0:T(8,128)(2,1)S(1)}, bf16[128,16,128]{2,1,0:T(8,128)(2,1)}, u32[]{:S(2)}) copy-start(bf16[128,16,128]{2,1,0:T(8,128)(2,1)} %param.9) | copy-start | bytes 1572868
  18.5 27.1 %copy-start.18 = (f32[128,128]{0,1:T(8,128)}, f32[128,128]{0,1:T(8,128)S(1)}, u32[]{:S(2)}) copy-start(f32[128,128]{0,1:T(8,128)S(1)} %copy.472) | copy-start | bytes 196612
  18.6 27.0 %copy-start.20 = (f32[128,128]{0,1:T(8,128)}, f32[128,128]{0,1:T(8,128)S(1)}, u32[]{:S(2)}) copy-start(f32[128,128]{0,1:T(8,128)S(1)} %copy.471) | copy-start | bytes 196612
  26.5 19.2 %copy-start.8 = (bf16[2,128,2,128]{1,3,2,0:T(8,128)(2,1)}, bf16[2,128,2,128]{1,3,2,0:T(8,128)(2,1)S(1)}, u32[]{:S(2)}) copy-start(bf16[2,128,2,128]{1,3,2,0:T(8,128)(2,1)S(1)} %collective-permute-done.1) | copy-start | bytes 393220
  26.6 19.3 %copy-start.10 = (bf16[2,128,2,128]{1,3,2,0:T(8,128)(2,1)}, bf16[2,128,2,128]{1,3,2,0:T(8,128)(2,1)S(1)}, u32[]{:S(2)}) copy-start(bf16[2,128,2,128]{1,3,2,0:T(8,128)(2,1)S(1)} %collective-permute-done) | copy-start | bytes 393220
  26.6 19.0 %collective-permute-start.2 = (bf16[2,2,128,2,128]{2,4,3,1,0:T(8,128)(2,1)S(1)}, bf16[2,2,128,2,128]{2,4,3,1,0:T(8,128)(2,1)S(1)}, u32[]{:S(2)}, u32[]{:S(2)}) collective-permute-start(bf16[2,2,128,2,128]{2,4,3,1,0:T(8,128)(2,1)S(1)} %pad_maximum_fusion), channel_id=1, source_target_pairs={{0,2},{1,3},{2,4},{3,5},{4,6},{5,7},{6,8},{7,9},{8,10},{9,11},{10,... | collective-permute-start | bytes 786440 | tf_op jit(solution)/shard_map/ppermute | solution.py:20
  45.6 13.0 %copy-start.12 = (bf16[2,2,128,2,128]{2,4,3,1,0:T(8,128)(2,1)}, bf16[2,2,128,2,128]{2,4,3,1,0:T(8,128)(2,1)S(1)}, u32[]{:S(2)}) copy-start(bf16[2,2,128,2,128]{2,4,3,1,0:T(8,128)(2,1)S(1)} %collective-permute-done.2) | copy-start | bytes 786436
  45.8 1.6 %copy-start.26 = (bf16[128,2,128,1]{0,2,3,1:T(8,128)(2,1)}, bf16[128,2,128,1]{0,2,3,1:T(8,128)(2,1)S(1)}, u32[]{:S(2)}) copy-start(bf16[128,2,128,1]{0,2,3,1:T(8,128)(2,1)S(1)} %get-tuple-element.110) | copy-start | bytes 196612
  45.8 2.0 %copy-start.16 = (bf16[128,2,128,1]{0,2,3,1:T(8,128)(2,1)}, bf16[128,2,128,1]{0,2,3,1:T(8,128)(2,1)S(1)}, u32[]{:S(2)}) copy-start(bf16[128,2,128,1]{0,2,3,1:T(8,128)(2,1)S(1)} %get-tuple-element.111) | copy-start | bytes 196612
  46.1 1.0 copy-start.22
  61.1 1.0 copy-start.31
  61.1 1.0 copy-start.49
  62.5 0.9 copy-start.51
  64.6 1.0 copy-start.53
  65.7 0.8 copy-start.45
  68.0 1.0 copy-start.13
  68.6 0.9 copy-start.39
  68.6 0.9 copy-start.40
  69.5 1.5 %copy-start.54 = (f32[2,128,128,1]{1,2,3,0:T(8,128)S(1)}, f32[2,128,128,1]{1,2,3,0:T(8,128)}, u32[]{:S(2)}) copy-start(f32[2,128,128,1]{1,2,3,0:T(8,128)} %fusion.33) | copy-start | bytes 393220
  72.0 0.9 copy-start.5
  72.9 0.9 copy-start.58
  74.8 0.9 copy-start.56
  77.5 0.8 copy-start.15
  77.6 0.9 copy-start.43
  78.4 0.9 copy-start.3
  78.4 0.9 copy-start.37
  80.0 0.9 copy-start.11
  80.0 0.9 copy-start.35
  80.9 0.9 copy-start.2
  80.9 0.9 copy-start.36
  82.5 0.9 copy-start.9
  82.5 0.9 copy-start.34
  85.0 9.6 %copy-start.42 = (bf16[1,128,2,128]{1,3,2,0:T(8,128)(2,1)S(1)}, bf16[1,128,2,128]{1,3,2,0:T(8,128)(2,1)}, u32[]{:S(2)}) copy-start(bf16[1,128,2,128]{1,3,2,0:T(8,128)(2,1)} %convert_bitcast_fusion.1) | copy-start | bytes 196612
  85.0 9.6 %copy-start.46 = (bf16[1,128,2,128]{1,3,2,0:T(8,128)(2,1)S(1)}, bf16[1,128,2,128]{1,3,2,0:T(8,128)(2,1)}, u32[]{:S(2)}) copy-start(bf16[1,128,2,128]{1,3,2,0:T(8,128)(2,1)} %get-tuple-element.75) | copy-start | bytes 196612
  85.0 24.0 %all-to-all-start = ((f32[16,4,2,128]{3,2,1,0:T(2,128)}), f32[16,4,2,128]{3,2,1,0:T(2,128)}, u32[]{:S(2)}, u32[]{:S(2)}) async-start(f32[16,4,2,128]{3,2,1,0:T(2,128)} %broadcast_in_dim.62), calls=%async_computation | async-start | bytes 131072 | tf_op jit(solution)/shard_map/all_to_all | solution.py:28
  94.6 0.8 copy-start.41
  94.6 0.9 copy-start.47
  95.5 9.8 %copy-start.25 = (bf16[128,2,128,1]{0,2,3,1:T(8,128)(2,1)S(1)}, bf16[128,2,128,1]{0,2,3,1:T(8,128)(2,1)}, u32[]{:S(2)}) copy-start(bf16[128,2,128,1]{0,2,3,1:T(8,128)(2,1)} %copy-done.24) | copy-start | bytes 196612
  96.2 9.3 %copy-start.27 = (bf16[128,2,128,1]{0,2,3,1:T(8,128)(2,1)S(1)}, bf16[128,2,128,1]{0,2,3,1:T(8,128)(2,1)}, u32[]{:S(2)}) copy-start(bf16[128,2,128,1]{0,2,3,1:T(8,128)(2,1)} %copy-done.26) | copy-start | bytes 196612
  96.2 22.5 %collective-permute-start.3 = (bf16[2,2,128,2,128]{2,4,3,1,0:T(8,128)(2,1)}, bf16[2,2,128,2,128]{2,4,3,1,0:T(8,128)(2,1)}, u32[]{:S(2)}, u32[]{:S(2)}) collective-permute-start(bf16[2,2,128,2,128]{2,4,3,1,0:T(8,128)(2,1)} %pad_maximum_fusion.1), channel_id=1, source_target_pairs={{2,0},{3,1},{4,2},{5,3},{6,4},{7,5},{8,6},{9,7},{10,8},{11,9},{12,... | collective-permute-start | bytes 786440 | tf_op jit(solution)/shard_map/ppermute | solution.py:20
  106.4 1.0 copy-start.1
  106.4 1.0 copy-start.17
  107.7 11.0 %copy-start.57 = (f32[2,128,128,1]{1,2,3,0:T(8,128)S(1)}, f32[2,128,128,1]{1,2,3,0:T(8,128)}, u32[]{:S(2)}) copy-start(f32[2,128,128,1]{1,2,3,0:T(8,128)} %fusion.37) | copy-start | bytes 393220
  107.7 11.0 %copy-start.59 = (f32[2,128,128,1]{1,2,3,0:T(8,128)S(1)}, f32[2,128,128,1]{1,2,3,0:T(8,128)}, u32[]{:S(2)}) copy-start(f32[2,128,128,1]{1,2,3,0:T(8,128)} %fusion.35) | copy-start | bytes 393220
  110.5 8.2 %copy-start.32 = (f32[1,128,2,128]{1,3,2,0:T(8,128)S(1)}, f32[1,128,2,128]{1,3,2,0:T(8,128)}, u32[]{:S(2)}) copy-start(f32[1,128,2,128]{1,3,2,0:T(8,128)} %get-tuple-element.63) | copy-start | bytes 393220
  110.5 8.2 %copy-start.33 = (f32[1,128,2,128]{1,3,2,0:T(8,128)S(1)}, f32[1,128,2,128]{1,3,2,0:T(8,128)}, u32[]{:S(2)}) copy-start(f32[1,128,2,128]{1,3,2,0:T(8,128)} %get-tuple-element.67) | copy-start | bytes 393220
  110.5 17.8 %all-to-all-start.1 = ((f32[32,4,2,128]{3,2,1,0:T(2,128)}), f32[32,4,2,128]{3,2,1,0:T(2,128)S(1)}, u32[]{:S(2)}, u32[]{:S(2)}) async-start(f32[32,4,2,128]{3,2,1,0:T(2,128)} %broadcast_in_dim.63), calls=%async_computation.1 | async-start | bytes 262144 | tf_op jit(solution)/shard_map/all_to_all | solution.py:28
  119.8 13.2 %copy-start.55 = (f32[2,128,128,1]{1,2,3,0:T(8,128)S(1)}, f32[2,128,128,1]{1,2,3,0:T(8,128)}, u32[]{:S(2)}) copy-start(f32[2,128,128,1]{1,2,3,0:T(8,128)} %fusion.33) | copy-start | bytes 393220
  119.8 10.5 %collective-permute-start.4 = (bf16[2,128,2,128]{1,3,2,0:T(8,128)(2,1)S(1)}, bf16[2,128,2,128]{1,3,2,0:T(8,128)(2,1)S(1)}, u32[]{:S(2)}, u32[]{:S(2)}) collective-permute-start(bf16[2,128,2,128]{1,3,2,0:T(8,128)(2,1)S(1)} %get-tuple-element.54), channel_id=1, source_target_pairs={{1,0},{2,1},{3,2},{4,3},{5,4},{6,5},{7,6},{8,7},{9,8},{10,9},{11,1... | collective-permute-start | bytes 393224 | tf_op jit(solution)/shard_map/ppermute | solution.py:20
  124.3 8.7 %collective-permute-start.5 = (bf16[2,128,2,128]{1,3,2,0:T(8,128)(2,1)S(1)}, bf16[2,128,2,128]{1,3,2,0:T(8,128)(2,1)S(1)}, u32[]{:S(2)}, u32[]{:S(2)}) collective-permute-start(bf16[2,128,2,128]{1,3,2,0:T(8,128)(2,1)S(1)} %get-tuple-element.55), channel_id=1, source_target_pairs={{2,0},{3,1},{4,2},{5,3},{6,4},{7,5},{8,6},{9,7},{10,8},{11,9},{12,... | collective-permute-start | bytes 393224 | tf_op jit(solution)/shard_map/ppermute | solution.py:20
  134.6 0.9 copy-start.7
  134.6 0.9 copy-start.21
  (18 other events, 12.9 us)

commit v2 on v1

v2 whole, which is shorter than its diff:
```python
import math

import jax
import jax.numpy as jnp
from jax import lax
from jax.experimental import pallas as pl
from jax.experimental.pallas import tpu as pltpu
from jax.sharding import Mesh, PartitionSpec as P

WIN = 512
ROWS = 128
HEAD = 128
QUERY_HEADS = 16
KV_HEADS = 2
BLOCKS = WIN // ROWS + 1
SPAN = BLOCKS * ROWS
WIDE = KV_HEADS * HEAD
CHUNK = 32
COLS = CHUNK * QUERY_HEADS
REACH = WIN + CHUNK
CHUNKS = ROWS // CHUNK
SCALE = 1.0 / math.sqrt(HEAD)
FLOOR = -3.0e38
clip_limit = 16.0
rope_base = 500000.0
TOK = ("x", "core", "ylo", "z")
FLAT = ("head", "x", "core", "ylo")
F32 = jnp.float32
BF16 = jnp.bfloat16


def shift(value, by):
    count = 1
    for axis in TOK:
        count *= lax.axis_size(axis)
    pairs = [(i, i + by) for i in range(count) if 0 <= i + by < count]
    return lax.ppermute(value, TOK, pairs)


def axis_count(axes):
    count = 1
    for axis in axes:
        count *= lax.axis_size(axis)
    return count


def split_two(value):
    high = value.astype(BF16)
    return high, (value - high.astype(F32)).astype(BF16)


def split_three(value):
    high = value.astype(BF16)
    rest = value - high.astype(F32)
    middle = rest.astype(BF16)
    return high, middle, (rest - middle.astype(F32)).astype(BF16)


def matmul(left, right):
    return jnp.dot(left, right, preferred_element_type=F32)


def matmul_nt(left, right):
    return lax.dot_general(left, right, (((1,), (1,)), ((), ())), preferred_element_type=F32)


def head_cols(head):
    return slice(head * HEAD, (head + 1) * HEAD)


def pack_kernel(key_ref, value_ref, out_ref):
    for head in range(KV_HEADS):
        picked = pl.ds(head, ROWS, stride=KV_HEADS)
        out_ref[:, head_cols(head)] = key_ref[picked, :].astype(F32).astype(BF16)
        out_ref[:, head_cols(KV_HEADS + head)] = value_ref[picked, :].astype(F32).astype(BF16)


def delta_kernel(grad_ref, forward_ref, out_ref):
    ones = jnp.ones((8, HEAD), BF16)
    product = grad_ref[...].astype(F32) * forward_ref[...].astype(F32)
    total = 0.0
    for piece in split_three(product):
        total = total + matmul_nt(ones, piece)
    out_ref[...] = total


def widen(rows, low):
    zero = jnp.zeros_like(rows)
    return jnp.concatenate([jnp.where(low, rows, zero), jnp.where(low, zero, rows)], axis=1)


def main_kernel(
    place_ref,
    query_ref,
    grad_ref,
    delta_ref,
    code4,
    code3,
    code2,
    code1,
    code0,
    cos_ref,
    sin_ref,
    steps_ref,
    had_ref,
    far4_ref,
    far3_ref,
    mid2_ref,
    near1_ref,
    own0_ref,
    query_out,
    raw_ref,
    keys,
    keys_t,
    values,
    wide_q,
    wide_g,
    scores,
    grads,
    key_acc,
    value_acc,
):
    code_refs = (code4, code3, code2, code1, code0)
    hadamard = had_ref[...]
    for block in range(BLOCKS):
        rows = slice(block * ROWS, (block + 1) * ROWS)
        cosines, sines = cos_ref[rows, :], sin_ref[rows, :]
        for head in range(KV_HEADS):
            cols = head_cols(head)
            code = code_refs[block][:, cols].astype(F32)
            deq = steps_ref[0:1, cols] * code - steps_ref[1:2, cols]
            turned = deq * cosines + pltpu.roll(deq, HEAD // 2, 1) * sines
            keys[rows, cols] = turned.astype(BF16)
            keys_t[cols, rows] = turned.T.astype(BF16)
            code = code_refs[block][:, head_cols(KV_HEADS + head)].astype(F32)
            deq = steps_ref[2:3, cols] * code - steps_ref[3:4, cols]
            total = 0.0
            for piece in split_three(deq):
                total = total + matmul(piece, hadamard)
            values[rows, cols] = (total * SCALE).astype(BF16)
    low = lax.broadcasted_iota(jnp.int32, (COLS, HEAD), 0) % QUERY_HEADS < QUERY_HEADS // KV_HEADS
    edge_row = lax.broadcasted_iota(jnp.int32, (CHUNK, COLS), 0)
    edge_token = lax.broadcasted_iota(jnp.int32, (CHUNK, COLS), 1) // QUERY_HEADS
    for chunk in range(CHUNKS):
        picked = slice(chunk * COLS, (chunk + 1) * COLS)
        span = slice(chunk * CHUNK, chunk * CHUNK + REACH)
        wide_q[picked, :] = widen(query_ref[picked, :], low)
        wide_g[picked, :] = widen(grad_ref[picked, :], low)
        score = matmul_nt(keys[span, :], wide_q[picked, :])
        scores[chunk, :CHUNK, :] = jnp.where(edge_row > edge_token, score[:CHUNK], FLOOR)
        scores[chunk, CHUNK:WIN, :] = score[CHUNK:WIN]
        scores[chunk, WIN:, :] = jnp.where(edge_row <= edge_token, score[WIN:], FLOOR)

    missing = WIN - place_ref[0] * ROWS

    @pl.when(missing > 0)
    def _():
        row = lax.broadcasted_iota(jnp.int32, (REACH, COLS), 0)
        for chunk in range(CHUNKS):
            scores[chunk] = jnp.where(row + chunk * CHUNK < missing, FLOOR, scores[chunk])

    key_acc[...] = jnp.zeros_like(key_acc)
    value_acc[...] = jnp.zeros_like(value_acc)
    grads[...] = jnp.zeros_like(grads)
    low_lane = (
        lax.broadcasted_iota(jnp.int32, (HEAD, COLS), 1) % QUERY_HEADS < QUERY_HEADS // KV_HEADS
    )
    for chunk in range(CHUNKS):
        picked = slice(chunk * COLS, (chunk + 1) * COLS)
        span = slice(chunk * CHUNK, chunk * CHUNK + REACH)
        score = scores[chunk]
        top = jnp.max(score, axis=0, keepdims=True)
        weights = jnp.exp((score - top) * SCALE)
        weights = weights * (1.0 / jnp.sum(weights, axis=0, keepdims=True))
        upstream = matmul_nt(values[span, :], wide_g[picked, :])
        grad = (weights * (upstream - delta_ref[0:1, picked])).astype(BF16)
        grads[chunk, span, :] = grad
        value_acc[span, :] += matmul(weights.astype(BF16), wide_g[picked, :])
        key_acc[span, :] += matmul(grad, wide_q[picked, :])
        both = matmul(keys_t[...], grads[chunk])
        query_grad = jnp.where(low_lane, both[:HEAD], both[HEAD:]) * SCALE
        query_out[picked, :] = query_grad.T.astype(BF16)

    outs = (far4_ref, far3_ref, mid2_ref, near1_ref, own0_ref)
    for head in range(KV_HEADS):
        cols = head_cols(head)
        value_cols = head_cols(KV_HEADS + head)
        sums = [0.0, 0.0, 0.0, 0.0]
        for block in range(BLOCKS):
            rows = slice(block * ROWS, (block + 1) * ROWS)
            part = key_acc[rows, cols] * SCALE
            part = part * cos_ref[rows, :] - pltpu.roll(part, HEAD // 2, 1) * sin_ref[rows, :]
            outs[block][:, cols] = part.astype(outs[block].dtype)
            code = code_refs[block][:, cols].astype(F32)
            sums[0] = sums[0] + jnp.sum(part * code, axis=0, keepdims=True)
            sums[1] = sums[1] - jnp.sum(part, axis=0, keepdims=True)
            total = 0.0
            for piece in split_three(value_acc[rows, cols]):
                total = total + matmul(piece, hadamard)
            part = total * SCALE
            outs[block][:, value_cols] = part.astype(outs[block].dtype)
            code = code_refs[block][:, value_cols].astype(F32)
            sums[2] = sums[2] + jnp.sum(part * code, axis=0, keepdims=True)
            sums[3] = sums[3] - jnp.sum(part, axis=0, keepdims=True)
        for term in range(4):
            row = term * KV_HEADS + head
            for copy in range(raw_ref.shape[0]):
                raw_ref[copy, row : row + 1, :] = sums[term]


def spread_kernel(in_ref, out_ref):
    total = jnp.sum(in_ref[...], axis=0)
    out_ref[...] = jnp.broadcast_to(total[None], out_ref.shape)


def finish_kernel(
    place_ref, all_ref, own_ref, near_ref, mid_ref, code_ref, key_out, value_out, quant_out, rows_ref
):
    per_head = all_ref.shape[0] // 2
    first = jnp.sum(all_ref[:per_head], axis=0)
    second = jnp.sum(all_ref[per_head:], axis=0)
    squares = jnp.sum(first * first + second * second, keepdims=True)
    mine = jnp.where(place_ref[1] == 0, first, second)
    quant_out[...] = mine * jnp.minimum(1.0, clip_limit / jnp.sqrt(squares + 1e-06))
    total = own_ref[...] + near_ref[...].astype(F32) + mid_ref[...].astype(F32)
    code = code_ref[...].astype(F32)
    total = jnp.where((code > 0.0) & (code < 15.0), total, 0.0)
    for kind, out in enumerate((key_out, value_out)):
        for head in range(KV_HEADS):
            rows_ref[pl.ds(head, ROWS, stride=KV_HEADS), :] = total[
                :, head_cols(kind * KV_HEADS + head)
            ]
        out[...] = rows_ref[...].astype(BF16)


def call(kernel, outs, scratch=(), scalars=0, inputs=0, limit=32, cost=None):
    specs = [pl.BlockSpec(memory_space=pltpu.SMEM)] * scalars
    specs = specs + [pl.BlockSpec(memory_space=pltpu.VMEM)] * inputs
    return pl.pallas_call(
        kernel,
        out_shape=[jax.ShapeDtypeStruct(shape, dtype) for shape, dtype in outs],
        in_specs=specs,
        out_specs=[pl.BlockSpec(memory_space=pltpu.VMEM)] * len(outs),
        scratch_shapes=[pltpu.VMEM(shape, dtype) for shape, dtype in scratch],
        compiler_params=pltpu.CompilerParams(vmem_limit_bytes=limit * 1024 * 1024),
        cost_estimate=cost,
    )


def rope_tables(positions, head_size):
    freqs = rope_base ** (-jnp.arange(0, head_size, 2, dtype=jnp.float32) / head_size)
    angles = positions.astype(jnp.float32)[:, None] * freqs[None, :]
    cosines, sines = jnp.cos(angles), jnp.sin(angles)
    return (
        jnp.concatenate([cosines, cosines], axis=-1),
        jnp.concatenate([-sines, sines], axis=-1),
    )


def hadamard_signs(order):
    index = jnp.arange(order, dtype=jnp.int32)
    common = jnp.bitwise_and(index[:, None], index[None, :])
    parity = jnp.zeros((order, order), jnp.int32)
    for level in range(order.bit_length() - 1):
        parity = parity + jnp.bitwise_and(jnp.right_shift(common, level), 1)
    return (1 - 2 * (parity % 2)).astype(BF16)


def body(query, grad_out, out_forward, k_codes, k_scale, k_offset, v_codes, v_scale, v_offset):
    device_block = jnp.int32(0)
    for axis in TOK:
        device_block = device_block * lax.axis_size(axis) + lax.axis_index(axis)
    place = jnp.stack([device_block, lax.axis_index("head")]).astype(jnp.int32)
    flat_codes = (KV_HEADS * ROWS, HEAD)
    flat_rows = (QUERY_HEADS * ROWS, HEAD)
    pack = (ROWS, 2 * WIDE)

    (own,) = call(pack_kernel, [(pack, BF16)], inputs=2)(
        k_codes.reshape(flat_codes), v_codes.reshape(flat_codes)
    )
    two = shift(own, 2)
    one = shift(own, 1)
    queries = query.reshape(flat_rows)
    upstream_rows = grad_out.reshape(flat_rows)
    (delta,) = call(delta_kernel, [((8, QUERY_HEADS * ROWS), F32)], inputs=2)(
        upstream_rows, out_forward.reshape(flat_rows)
    )
    first_row = device_block * ROWS - WIN
    cosines, sines = rope_tables(first_row + jnp.arange(SPAN, dtype=jnp.int32), HEAD)
    steps = jnp.stack([k_scale, k_offset, v_scale, v_offset]).reshape(4, WIDE)
    hadamard = hadamard_signs(HEAD)
    four = shift(two, 2)
    three = shift(two, 1)

    column = axis_count(("z",))
    far4, far3, mid2, near1, own0, query_grad, raw = call(
        main_kernel,
        [
            (pack, BF16),
            (pack, BF16),
            (pack, F32),
            (pack, BF16),
            (pack, F32),
            (flat_rows, BF16),
            ((column, 4 * KV_HEADS, HEAD), F32),
        ],
        scratch=[
            ((SPAN, WIDE), BF16),
            ((WIDE, SPAN), BF16),
            ((SPAN, WIDE), BF16),
            ((QUERY_HEADS * ROWS, WIDE), BF16),
            ((QUERY_HEADS * ROWS, WIDE), BF16),
            ((CHUNKS, REACH, COLS), F32),
            ((CHUNKS, SPAN, COLS), BF16),
            ((SPAN, WIDE), F32),
            ((SPAN, WIDE), F32),
        ],
        scalars=1,
        inputs=12,
    )(place, queries, upstream_rows, delta, four, three, two, one, own, cosines, sines, steps, hadamard)

    from4 = shift(far4, -2)
    from3 = shift(far3, -1)
    from1 = shift(near1, -1)
    raw = lax.all_to_all(raw, "z", 0, 0)
    (raw,) = call(
        spread_kernel, [((axis_count(FLAT), 4 * KV_HEADS, HEAD), F32)], inputs=1
    )(raw)
    mid = (mid2 + from4.astype(F32) + from3.astype(F32)).astype(BF16)
    from2 = shift(mid, -2)
    raw = lax.all_to_all(raw, FLAT, 0, 0)
    key_grad, value_grad, quant = call(
        finish_kernel,
        [(flat_codes, BF16), (flat_codes, BF16), ((4 * KV_HEADS, HEAD), F32)],
        scratch=[(flat_codes, F32)],
        scalars=1,
        inputs=5,
    )(place, raw, own0, from1, from2, own)
    return (
        query_grad.reshape(ROWS, QUERY_HEADS, HEAD),
        key_grad.reshape(ROWS, KV_HEADS, HEAD),
        value_grad.reshape(ROWS, KV_HEADS, HEAD),
        quant.reshape(4, KV_HEADS, HEAD),
    )


def solution(mesh):
    sizes = (mesh.shape["head"], mesh.shape["outer"] // 2, 2, 2, mesh.shape["inner"] // 2)
    split = Mesh(mesh.devices.reshape(sizes), ("head",) + TOK)
    rows = P(TOK, "head", None)
    steps = P("head", None)
    return jax.shard_map(
        body,
        mesh=split,
        in_specs=(rows, rows, rows, rows, steps, steps, rows, steps, steps),
        out_specs=(rows, rows, rows, P(None, "head", None)),
        check_vma=False,
    )
```

time: 138 us -> 89.3 us (0.65)
  local copies, waits for them, and re-layouts: 32.2 us -> 1.84 us
  matrix products: 17.8 us -> 0 us
  other arithmetic: 18.5 us -> 1.71 us
  waiting for transfers between devices: 14.5 us -> 28.1 us
  Pallas kernels: 0 us -> 9.49 us
  starting transfers between devices: 50.7 us -> 46.8 us
  between operations: 2.65 us -> 0.91 us
    unnamed x153 -> x18, local copies, waits for them, and re-layouts: 20.3 us -> 1.84 us
    dot_general x36 -> x0, matrix products: 17.8 us -> none  [the longest x5 3.93 us: body(): jnp.einsum('kgtu,tkgd->ukd', weights_low, upstream_rows, preferred_elemen...]
    pallas_call x0 -> x5, Pallas kernels: none -> 9.49 us  [the longest x1 6.78 us: body(): call(main_kernel, [(pack, BF16), (pack, BF16), (pack, F32), (pack, BF16),...]
    all_to_all x2, waiting for transfers between devices: 0.01 us -> 8.31 us  [the longest x1 7.55 us: body(): raw = lax.all_to_all(raw, FLAT, 0, 0)]
    mul x10 -> x0, local copies, waits for them, and re-layouts: 7.19 us -> none  [the longest x5 3.61 us: rotate_back(): scaled = grads * sines]
    ppermute x6 -> x8, waiting for transfers between devices: 14.5 us -> 19.7 us  [shift(): return lax.ppermute(value, TOK, pairs)]
    all_to_all x2, starting transfers between devices: 17.7 us -> 12.6 us  [the longest x1 9.05 us: body(): raw = lax.all_to_all(raw, FLAT, 0, 0)]
    mul x11 -> x0, other arithmetic: 4.82 us -> none  [the longest x6 2.64 us: rotate_back(): scaled = grads * sines]
  transfers between devices with their start and end apart: 8 -> 10, of which waited for: 3 -> 5; matrix products, arithmetic and copies ran while one was open for 15% -> 2% of each run, Pallas kernels for 0% -> 1%
where the time goes in v2:
time: 89.3 us; the launch traced here: 88.8 us
  starting transfers between devices  46.8 us (52%)
  waiting for transfers between devices  28.1 us (31%)
  Pallas kernels  9.49 us (11%)
  local copies, waits for them, and re-layouts  1.84 us (2%)
  other arithmetic  1.71 us (2%)
  between operations  0.91 us (1%)
    ppermute x8, starting transfers between devices, shift(): return lax.ppermute(value, TOK, pairs)  34.2 us
    ppermute x8, waiting for transfers between devices, shift(): return lax.ppermute(value, TOK, pairs)  19.7 us
    all_to_all x1, starting transfers between devices, body(): raw = lax.all_to_all(raw, FLAT, 0, 0)  9.05 us
    all_to_all x1, waiting for transfers between devices, body(): raw = lax.all_to_all(raw, FLAT, 0, 0)  7.55 us
    pallas_call x1, Pallas kernels, body(): call(main_kernel, [(pack, BF16), (pack, BF16), (pack, F32), (pack, BF16),...  6.78 us
    all_to_all x1, starting transfers between devices, body(): raw = lax.all_to_all(raw, 'z', 0, 0)  3.51 us
    unnamed x18, local copies, waits for them, and re-layouts  1.84 us
  transfers between devices with their start and end apart: 10, of which 5 were waited for; matrix products, arithmetic and copies ran while one was open for 2% of the time, Pallas kernels for 1%

profile of v2, /device:TPU:1, one launch (start us, length us, event | category | flops | bytes accessed | tf_op | source)
XLA Modules:
  0.0 88.8 jit_solution(15655459321020880316)
XLA Ops:
  0.6 0.0 copy-start.3
  0.6 0.9 %copy-done.3 = s32[128,2,128]{2,1,0:T(2,128)S(1)} copy-done((s32[128,2,128]{2,1,0:T(2,128)S(1)}, s32[128,2,128]{2,1,0:T(2,128)}, u32[]{:S(2)}) %copy-start.3) | copy-done | bytes 131096
  1.5 0.0 copy-start.4
  1.5 0.9 %copy-done.4 = s32[128,2,128]{2,1,0:T(2,128)S(1)} copy-done((s32[128,2,128]{2,1,0:T(2,128)S(1)}, s32[128,2,128]{2,1,0:T(2,128)}, u32[]{:S(2)}) %copy-start.4) | copy-done | bytes 131096
  2.5 4.4 %collective-permute-start.3 = (bf16[128,512]{1,0:T(8,128)(2,1)S(1)}, bf16[128,512]{1,0:T(8,128)(2,1)S(1)}, u32[]{:S(2)}, u32[]{:S(2)}) collective-permute-start(bf16[128,512]{1,0:T(8,128)(2,1)S(1)} %shard_map.121.code0.code_ref), channel_id=1, source_target_pairs={{0,1},{1,2},{2,3},{3,4},{4,5},{5,6},{6,7},{7,8},{8,9},{9,10},{10,1... | collective-permute-start | bytes 393224 | tf_op jit(solution)/shard_map/ppermute | solution.py:37
  6.9 4.9 %collective-permute-start = (bf16[128,512]{1,0:T(8,128)(2,1)S(1)}, bf16[128,512]{1,0:T(8,128)(2,1)S(1)}, u32[]{:S(2)}, u32[]{:S(2)}) collective-permute-start(bf16[128,512]{1,0:T(8,128)(2,1)S(1)} %shard_map.121.code0.code_ref), channel_id=1, source_target_pairs={{0,2},{1,3},{2,4},{3,5},{4,6},{5,7},{6,8},{7,9},{8,10},{9,11},{10,... | collective-permute-start | bytes 393224 | tf_op jit(solution)/shard_map/ppermute | solution.py:37
  11.8 0.0 copy-start.5
  11.8 0.0 copy-start.6
  11.8 0.0 copy-start.7
  11.8 0.0 copy-start.8
  11.9 0.0 copy-start
  11.9 0.0 copy-start.1
  11.9 1.2 %fusion = (f32[640,64]{1,0:T(8,128)S(1)}, f32[640,64]{1,0:T(8,128)S(1)}, f32[640,64]{1,0:T(8,128)S(1)}) fusion(f32[64]{0:T(128)S(1)} %multiply_power_fusion, f32[640]{0:T(1024)S(1)} %add_convert_fusion.1), kind=kLoop, calls=%fused_computation.5 | loop fusion | flops 81920 | bytes 494336 | tf_op jit(solution)/shard_map/neg | solution.py:256
  13.1 0.0 copy-done.5
  13.1 0.0 copy-done.6
  13.1 0.0 copy-done.7
  13.1 0.0 copy-done.8
  13.2 0.1 fusion.4.had_ref
  13.3 11.7 %collective-permute-done.code2 = bf16[128,512]{1,0:T(8,128)(2,1)S(1)} collective-permute-done((bf16[128,512]{1,0:T(8,128)(2,1)S(1)}, bf16[128,512]{1,0:T(8,128)(2,1)S(1)}, u32[]{:S(2)}, u32[]{:S(2)}) %collective-permute-start) | collective-permute-done | bytes 131104 | tf_op jit(solution)/shard_map/ppermute | solution.py:37
  24.9 2.7 %collective-permute-start.2 = (bf16[128,512]{1,0:T(8,128)(2,1)S(1)}, bf16[128,512]{1,0:T(8,128)(2,1)S(1)}, u32[]{:S(2)}, u32[]{:S(2)}) collective-permute-start(bf16[128,512]{1,0:T(8,128)(2,1)S(1)} %collective-permute-done.code2), channel_id=1, source_target_pairs={{0,1},{1,2},{2,3},{3,4},{4,5},{5,6},{6,7},{7,8},{8,9},{9,10},{10,1... | collective-permute-start | bytes 393224 | tf_op jit(solution)/shard_map/ppermute | solution.py:37
  27.7 1.9 %collective-permute-start.1 = (bf16[128,512]{1,0:T(8,128)(2,1)S(1)}, bf16[128,512]{1,0:T(8,128)(2,1)S(1)}, u32[]{:S(2)}, u32[]{:S(2)}) collective-permute-start(bf16[128,512]{1,0:T(8,128)(2,1)S(1)} %collective-permute-done.code2), channel_id=1, source_target_pairs={{0,2},{1,3},{2,4},{3,5},{4,6},{5,7},{6,8},{7,9},{8,10},{9,11},{10,... | collective-permute-start | bytes 393224 | tf_op jit(solution)/shard_map/ppermute | solution.py:37
  29.6 0.1 pad_add_fusion.place_ref
  29.7 0.0 copy-done
  29.7 0.0 copy-done.1
  29.7 0.6 shard_map.120.delta_ref
  30.3 0.0 copy-start.2
  30.3 0.3 pad_maximum_fusion
  30.5 0.0 collective-permute-done.3.code1
  30.6 5.4 %collective-permute-done.2.code3 = bf16[128,512]{1,0:T(8,128)(2,1)S(1)} collective-permute-done((bf16[128,512]{1,0:T(8,128)(2,1)S(1)}, bf16[128,512]{1,0:T(8,128)(2,1)S(1)}, u32[]{:S(2)}, u32[]{:S(2)}) %collective-permute-start.2) | collective-permute-done | bytes 131104 | tf_op jit(solution)/shard_map/ppermute | solution.py:37
  35.9 2.7 %collective-permute-done.1.code4 = bf16[128,512]{1,0:T(8,128)(2,1)S(1)} collective-permute-done((bf16[128,512]{1,0:T(8,128)(2,1)S(1)}, bf16[128,512]{1,0:T(8,128)(2,1)S(1)}, u32[]{:S(2)}, u32[]{:S(2)}) %collective-permute-start.1) | collective-permute-done | bytes 131104 | tf_op jit(solution)/shard_map/ppermute | solution.py:37
  38.6 0.0 copy-done.2
  38.6 6.8 %shard_map.122 = (bf16[128,512]{1,0:T(8,128)(2,1)S(1)}, bf16[128,512]{1,0:T(8,128)(2,1)S(1)}, f32[128,512]{1,0:T(8,128)S(1)}, bf16[128,512]{1,0:T(8,128)(2,1)S(1...) custom-call(s32[2]{0:T(128)S(1)} %pad_add_fusion.place_ref, ...), custom_call_target="tpu_custom_call" | custom-call | tf_op jit(solution)/shard_map/pallas_call | solution.py:296
  45.4 3.2 %collective-permute-start.5 = (bf16[128,512]{1,0:T(8,128)(2,1)S(1)}, bf16[128,512]{1,0:T(8,128)(2,1)S(1)}, u32[]{:S(2)}, u32[]{:S(2)}) collective-permute-start(bf16[128,512]{1,0:T(8,128)(2,1)S(1)} %get-tuple-element.19), channel_id=1, source_target_pairs={{2,0},{3,1},{4,2},{5,3},{6,4},{7,5},{8,6},{9,7},{10,8},{11,9},{12,... | collective-permute-start | bytes 393224 | tf_op jit(solution)/shard_map/ppermute | solution.py:37
  48.6 6.3 %collective-permute-start.6 = (bf16[128,512]{1,0:T(8,128)(2,1)S(1)}, bf16[128,512]{1,0:T(8,128)(2,1)S(1)}, u32[]{:S(2)}, u32[]{:S(2)}) collective-permute-start(bf16[128,512]{1,0:T(8,128)(2,1)S(1)} %get-tuple-element.20), channel_id=1, source_target_pairs={{1,0},{2,1},{3,2},{4,3},{5,4},{6,5},{7,6},{8,7},{9,8},{10,9},{11,1... | collective-permute-start | bytes 393224 | tf_op jit(solution)/shard_map/ppermute | solution.py:37
  55.0 3.5 %all-to-all-start = ((f32[16,8,128]{2,1,0:T(8,128)}), f32[16,8,128]{2,1,0:T(8,128)S(1)}, u32[]{:S(2)}, u32[]{:S(2)}) async-start(f32[16,8,128]{2,1,0:T(8,128)} %get-tuple-element.15), calls=%async_computation | async-start | bytes 131072 | tf_op jit(solution)/shard_map/all_to_all | solution.py:325
  58.5 6.5 %collective-permute-start.4 = (bf16[128,512]{1,0:T(8,128)(2,1)S(1)}, bf16[128,512]{1,0:T(8,128)(2,1)S(1)}, u32[]{:S(2)}, u32[]{:S(2)}) collective-permute-start(bf16[128,512]{1,0:T(8,128)(2,1)S(1)} %get-tuple-element.17), channel_id=1, source_target_pairs={{1,0},{2,1},{3,2},{4,3},{5,4},{6,5},{7,6},{8,7},{9,8},{10,9},{11,1... | collective-permute-start | bytes 393224 | tf_op jit(solution)/shard_map/ppermute | solution.py:37
  65.0 0.0 collective-permute-done.5
  65.0 0.0 collective-permute-done.6
  65.0 4.3 %collective-permute-start.7 = (bf16[128,512]{1,0:T(8,128)(2,1)S(1)}, bf16[128,512]{1,0:T(8,128)(2,1)S(1)}, u32[]{:S(2)}, u32[]{:S(2)}) collective-permute-start(bf16[128,512]{1,0:T(8,128)(2,1)S(1)} %add_convert_fusion), channel_id=1, source_target_pairs={{2,0},{3,1},{4,2},{5,3},{6,4},{7,5},{8,6},{9,7},{10,8},{11,9},{12,... | collective-permute-start | bytes 393224 | tf_op jit(solution)/shard_map/ppermute | solution.py:37
  69.3 0.8 all-to-all-done.in_ref
  70.1 0.7 shard_map.123
  70.8 9.1 %all-to-all-start.1 = ((f32[32,8,128]{2,1,0:T(8,128)}), f32[32,8,128]{2,1,0:T(8,128)S(1)}, u32[]{:S(2)}, u32[]{:S(2)}) async-start(f32[32,8,128]{2,1,0:T(8,128)} %shard_map.123), calls=%async_computation.1 | async-start | bytes 262144 | tf_op jit(solution)/shard_map/all_to_all | solution.py:331
  79.8 0.0 collective-permute-done.4.near_ref
  79.8 0.0 collective-permute-done.7.mid_ref
  79.8 7.5 %all-to-all-done.1.all_ref = f32[32,8,128]{2,1,0:T(8,128)S(1)} async-done(((f32[32,8,128]{2,1,0:T(8,128)}), f32[32,8,128]{2,1,0:T(8,128)S(1)}, u32[]{:S(2)}, u32[]{:S(2)}) %all-to-all-start.1) | async-done | bytes 131104 | tf_op jit(solution)/shard_map/all_to_all | solution.py:331
  87.4 1.4 %shard_map.124 = (bf16[256,128]{1,0:T(8,128)(2,1)}, bf16[256,128]{1,0:T(8,128)(2,1)}, f32[8,128]{1,0:T(8,128)}) custom-call(s32[2]{0:T(128)S(1)} %pad_add_fusion.place_ref, f32[32,8,128]{2,1,0:T(8,128)S(1)} %all-to-all-done.1.all_ref, f32[128,512]{1,0:T(8,128)S(1)} %get-tuple-element.16.own_ref, bf16[128,512]{1,0:T(8,128)(2,1)S(1)} %collective-permute-done.4.near_ref, ...), custom_call_target="tpu_custom_call" | custom-call | tf_op jit(solution)/shard_map/pallas_call | solution.py:332
  (5 shorter events, 0.1 us)
Async XLA Ops:
  0.6 0.9 %copy-start.3 = (s32[128,2,128]{2,1,0:T(2,128)S(1)}, s32[128,2,128]{2,1,0:T(2,128)}, u32[]{:S(2)}) copy-start(s32[128,2,128]{2,1,0:T(2,128)} %param.12) | copy-start | bytes 393220
  1.5 0.9 %copy-start.4 = (s32[128,2,128]{2,1,0:T(2,128)S(1)}, s32[128,2,128]{2,1,0:T(2,128)}, u32[]{:S(2)}) copy-start(s32[128,2,128]{2,1,0:T(2,128)} %param.15) | copy-start | bytes 393220
  2.5 28.1 %collective-permute-start.3 = (bf16[128,512]{1,0:T(8,128)(2,1)S(1)}, bf16[128,512]{1,0:T(8,128)(2,1)S(1)}, u32[]{:S(2)}, u32[]{:S(2)}) collective-permute-start(bf16[128,512]{1,0:T(8,128)(2,1)S(1)} %shard_map.121.code0.code_ref), channel_id=1, source_target_pairs={{0,1},{1,2},{2,3},{3,4},{4,5},{5,6},{6,7},{7,8},{8,9},{9,10},{10,1... | collective-permute-start | bytes 393224 | tf_op jit(solution)/shard_map/ppermute | solution.py:37
  6.9 18.1 %collective-permute-start = (bf16[128,512]{1,0:T(8,128)(2,1)S(1)}, bf16[128,512]{1,0:T(8,128)(2,1)S(1)}, u32[]{:S(2)}, u32[]{:S(2)}) collective-permute-start(bf16[128,512]{1,0:T(8,128)(2,1)S(1)} %shard_map.121.code0.code_ref), channel_id=1, source_target_pairs={{0,2},{1,3},{2,4},{3,5},{4,6},{5,7},{6,8},{7,9},{8,10},{9,11},{10,... | collective-permute-start | bytes 393224 | tf_op jit(solution)/shard_map/ppermute | solution.py:37
  11.8 1.3 %copy-start.5 = (f32[2,128]{1,0:T(2,128)S(1)}, f32[2,128]{1,0:T(2,128)}, u32[]{:S(2)}) copy-start(f32[2,128]{1,0:T(2,128)} %param.17) | copy-start | bytes 3076
  11.8 1.3 %copy-start.6 = (f32[2,128]{1,0:T(2,128)S(1)}, f32[2,128]{1,0:T(2,128)}, u32[]{:S(2)}) copy-start(f32[2,128]{1,0:T(2,128)} %param.16) | copy-start | bytes 3076
  11.8 1.3 %copy-start.7 = (f32[2,128]{1,0:T(2,128)S(1)}, f32[2,128]{1,0:T(2,128)}, u32[]{:S(2)}) copy-start(f32[2,128]{1,0:T(2,128)} %param.14) | copy-start | bytes 3076
  11.8 1.3 %copy-start.8 = (f32[2,128]{1,0:T(2,128)S(1)}, f32[2,128]{1,0:T(2,128)}, u32[]{:S(2)}) copy-start(f32[2,128]{1,0:T(2,128)} %param.13) | copy-start | bytes 3076
  11.9 17.8 %copy-start = (bf16[128,16,128]{2,1,0:T(8,128)(2,1)S(1)}, bf16[128,16,128]{2,1,0:T(8,128)(2,1)}, u32[]{:S(2)}) copy-start(bf16[128,16,128]{2,1,0:T(8,128)(2,1)} %param.10) | copy-start | bytes 1572868
  11.9 17.8 %copy-start.1 = (bf16[128,16,128]{2,1,0:T(8,128)(2,1)S(1)}, bf16[128,16,128]{2,1,0:T(8,128)(2,1)}, u32[]{:S(2)}) copy-start(bf16[128,16,128]{2,1,0:T(8,128)(2,1)} %param.11) | copy-start | bytes 1572868
  24.9 11.0 %collective-permute-start.2 = (bf16[128,512]{1,0:T(8,128)(2,1)S(1)}, bf16[128,512]{1,0:T(8,128)(2,1)S(1)}, u32[]{:S(2)}, u32[]{:S(2)}) collective-permute-start(bf16[128,512]{1,0:T(8,128)(2,1)S(1)} %collective-permute-done.code2), channel_id=1, source_target_pairs={{0,1},{1,2},{2,3},{3,4},{4,5},{5,6},{6,7},{7,8},{8,9},{9,10},{10,1... | collective-permute-start | bytes 393224 | tf_op jit(solution)/shard_map/ppermute | solution.py:37
  27.7 10.9 %collective-permute-start.1 = (bf16[128,512]{1,0:T(8,128)(2,1)S(1)}, bf16[128,512]{1,0:T(8,128)(2,1)S(1)}, u32[]{:S(2)}, u32[]{:S(2)}) collective-permute-start(bf16[128,512]{1,0:T(8,128)(2,1)S(1)} %collective-permute-done.code2), channel_id=1, source_target_pairs={{0,2},{1,3},{2,4},{3,5},{4,6},{5,7},{6,8},{7,9},{8,10},{9,11},{10,... | collective-permute-start | bytes 393224 | tf_op jit(solution)/shard_map/ppermute | solution.py:37
  30.3 8.3 %copy-start.2 = (bf16[128,16,128]{2,1,0:T(8,128)(2,1)S(1)}, bf16[128,16,128]{2,1,0:T(8,128)(2,1)}, u32[]{:S(2)}) copy-start(bf16[128,16,128]{2,1,0:T(8,128)(2,1)} %param.9) | copy-start | bytes 1572868
  45.4 19.6 %collective-permute-start.5 = (bf16[128,512]{1,0:T(8,128)(2,1)S(1)}, bf16[128,512]{1,0:T(8,128)(2,1)S(1)}, u32[]{:S(2)}, u32[]{:S(2)}) collective-permute-start(bf16[128,512]{1,0:T(8,128)(2,1)S(1)} %get-tuple-element.19), channel_id=1, source_target_pairs={{2,0},{3,1},{4,2},{5,3},{6,4},{7,5},{8,6},{9,7},{10,8},{11,9},{12,... | collective-permute-start | bytes 393224 | tf_op jit(solution)/shard_map/ppermute | solution.py:37
  48.6 16.4 %collective-permute-start.6 = (bf16[128,512]{1,0:T(8,128)(2,1)S(1)}, bf16[128,512]{1,0:T(8,128)(2,1)S(1)}, u32[]{:S(2)}, u32[]{:S(2)}) collective-permute-start(bf16[128,512]{1,0:T(8,128)(2,1)S(1)} %get-tuple-element.20), channel_id=1, source_target_pairs={{1,0},{2,1},{3,2},{4,3},{5,4},{6,5},{7,6},{8,7},{9,8},{10,9},{11,1... | collective-permute-start | bytes 393224 | tf_op jit(solution)/shard_map/ppermute | solution.py:37
  55.0 15.1 %all-to-all-start = ((f32[16,8,128]{2,1,0:T(8,128)}), f32[16,8,128]{2,1,0:T(8,128)S(1)}, u32[]{:S(2)}, u32[]{:S(2)}) async-start(f32[16,8,128]{2,1,0:T(8,128)} %get-tuple-element.15), calls=%async_computation | async-start | bytes 131072 | tf_op jit(solution)/shard_map/all_to_all | solution.py:325
  58.5 21.3 %collective-permute-start.4 = (bf16[128,512]{1,0:T(8,128)(2,1)S(1)}, bf16[128,512]{1,0:T(8,128)(2,1)S(1)}, u32[]{:S(2)}, u32[]{:S(2)}) collective-permute-start(bf16[128,512]{1,0:T(8,128)(2,1)S(1)} %get-tuple-element.17), channel_id=1, source_target_pairs={{1,0},{2,1},{3,2},{4,3},{5,4},{6,5},{7,6},{8,7},{9,8},{10,9},{11,1... | collective-permute-start | bytes 393224 | tf_op jit(solution)/shard_map/ppermute | solution.py:37
  65.0 14.8 %collective-permute-start.7 = (bf16[128,512]{1,0:T(8,128)(2,1)S(1)}, bf16[128,512]{1,0:T(8,128)(2,1)S(1)}, u32[]{:S(2)}, u32[]{:S(2)}) collective-permute-start(bf16[128,512]{1,0:T(8,128)(2,1)S(1)} %add_convert_fusion), channel_id=1, source_target_pairs={{2,0},{3,1},{4,2},{5,3},{6,4},{7,5},{8,6},{9,7},{10,8},{11,9},{12,... | collective-permute-start | bytes 393224 | tf_op jit(solution)/shard_map/ppermute | solution.py:37
  70.8 16.6 %all-to-all-start.1 = ((f32[32,8,128]{2,1,0:T(8,128)}), f32[32,8,128]{2,1,0:T(8,128)S(1)}, u32[]{:S(2)}, u32[]{:S(2)}) async-start(f32[32,8,128]{2,1,0:T(8,128)} %shard_map.123), calls=%async_computation.1 | async-start | bytes 262144 | tf_op jit(solution)/shard_map/all_to_all | solution.py:331

commit v3 on v2

v3 whole, which is shorter than its diff:
```python
import math

import jax
import jax.numpy as jnp
from jax import lax
from jax.experimental import pallas as pl
from jax.experimental.pallas import tpu as pltpu
from jax.sharding import Mesh, PartitionSpec as P

WIN = 512
ROWS = 128
HEAD = 128
QUERY_HEADS = 16
KV_HEADS = 2
BLOCKS = WIN // ROWS + 1
SPAN = BLOCKS * ROWS
WIDE = KV_HEADS * HEAD
CHUNK = 32
COLS = CHUNK * QUERY_HEADS
CHUNKS = ROWS // CHUNK
FAR_BLOCKS = 2
PIECES = 4
FINISH_FLOPS = None
MIDDLE_FLOPS = 3 * 10**9
FAR_ROWS = FAR_BLOCKS * ROWS
NEAR_ROWS = SPAN - FAR_ROWS
SCALE = 1.0 / math.sqrt(HEAD)
FLOOR = -3.0e38
clip_limit = 16.0
rope_base = 500000.0
TOK = ("x", "core", "ylo", "z")
FLAT = ("head", "x", "core", "ylo")
F32 = jnp.float32
BF16 = jnp.bfloat16


def shift(value, by):
    count = 1
    for axis in TOK:
        count *= lax.axis_size(axis)
    pairs = [(i, i + by) for i in range(count) if 0 <= i + by < count]
    return lax.ppermute(value, TOK, pairs)


def axis_count(axes):
    count = 1
    for axis in axes:
        count *= lax.axis_size(axis)
    return count


def split_two(value):
    high = value.astype(BF16)
    return high, (value - high.astype(F32)).astype(BF16)


def split_three(value):
    high = value.astype(BF16)
    rest = value - high.astype(F32)
    middle = rest.astype(BF16)
    return high, middle, (rest - middle.astype(F32)).astype(BF16)


def matmul(left, right):
    return jnp.dot(left, right, preferred_element_type=F32)


def matmul_nt(left, right):
    return lax.dot_general(left, right, (((1,), (1,)), ((), ())), preferred_element_type=F32)


def head_cols(head):
    return slice(head * HEAD, (head + 1) * HEAD)


def pack_kernel(key_hbm, value_hbm, out_ref, rows_ref, sems):
    copies = []
    step = KV_HEADS * ROWS // PIECES
    for kind, source in enumerate((key_hbm, value_hbm)):
        for piece in range(PIECES):
            rows = pl.ds(piece * step, step)
            copies.append(
                pltpu.make_async_copy(
                    source.at[rows], rows_ref.at[kind, rows], sems.at[kind * PIECES + piece]
                )
            )
            copies[-1].start()
    for kind in range(2):
        for piece in range(PIECES):
            copies[kind * PIECES + piece].wait()
        for head in range(KV_HEADS):
            code = rows_ref[kind, pl.ds(head, ROWS, stride=KV_HEADS), :].astype(F32)
            out_ref[:, head_cols(kind * KV_HEADS + head)] = code.astype(BF16)


def widen(rows, low):
    zero = jnp.zeros_like(rows)
    return jnp.concatenate([jnp.where(low, rows, zero), jnp.where(low, zero, rows)], axis=1)


def dequantize(code_ref, tables, block, steps_ref, hadamard):
    rows = slice(block * ROWS, (block + 1) * ROWS)
    cos_ref, sin_ref = tables
    cosines, sines = cos_ref[rows, :], sin_ref[rows, :]
    keys, values = [], []
    for head in range(KV_HEADS):
        cols = head_cols(head)
        code = code_ref[:, cols].astype(F32)
        deq = steps_ref[0:1, cols] * code - steps_ref[1:2, cols]
        keys.append(deq * cosines + pltpu.roll(deq, HEAD // 2, 1) * sines)
        code = code_ref[:, head_cols(KV_HEADS + head)].astype(F32)
        deq = steps_ref[2:3, cols] * code - steps_ref[3:4, cols]
        total = 0.0
        for piece in split_three(deq):
            total = total + matmul(piece, hadamard)
        values.append((total * SCALE).astype(BF16))
    return keys, values


def store_block(dequantized, row, keys, keys_t, values):
    rows = slice(row, row + ROWS)
    for head in range(KV_HEADS):
        cols = head_cols(head)
        keys[rows, cols] = dequantized[0][head].astype(BF16)
        keys_t[cols, rows] = dequantized[0][head].T.astype(BF16)
        values[rows, cols] = dequantized[1][head]


def near_kernel(
    place_ref,
    query_ref,
    grad_ref,
    forward_ref,
    code2,
    code1,
    code0,
    cos_ref,
    sin_ref,
    steps_ref,
    had_ref,
    wide_q,
    wide_g,
    keys_t,
    near_p,
    near_u,
    stats,
    keys,
    values,
    scores,
):
    hadamard = had_ref[...]
    tables = (cos_ref, sin_ref)
    for block, code_ref in enumerate((code2, code1, code0)):
        made = dequantize(code_ref, tables, FAR_BLOCKS + block, steps_ref, hadamard)
        store_block(made, block * ROWS, keys, keys_t, values)
    low = lax.broadcasted_iota(jnp.int32, (COLS, HEAD), 0) % QUERY_HEADS < QUERY_HEADS // KV_HEADS
    edge_row = lax.broadcasted_iota(jnp.int32, (CHUNK, COLS), 0)
    edge_token = lax.broadcasted_iota(jnp.int32, (CHUNK, COLS), 1) // QUERY_HEADS
    for chunk in range(CHUNKS):
        picked = slice(chunk * COLS, (chunk + 1) * COLS)
        count = NEAR_ROWS - ROWS + (chunk + 1) * CHUNK
        wide_q[picked, :] = widen(query_ref[picked, :], low)
        wide_g[picked, :] = widen(grad_ref[picked, :], low)
        score = matmul_nt(keys[:count, :], wide_q[picked, :])
        last = count - CHUNK
        scores[chunk, :last, :] = score[:last]
        scores[chunk, last:count, :] = jnp.where(edge_row <= edge_token, score[last:], FLOOR)

    missing = (BLOCKS - FAR_BLOCKS - 1 - place_ref[0]) * ROWS

    @pl.when(missing > 0)
    def _():
        row = lax.broadcasted_iota(jnp.int32, (NEAR_ROWS, COLS), 0)
        for chunk in range(CHUNKS):
            scores[chunk] = jnp.where(row < missing, FLOOR, scores[chunk])

    ones = jnp.ones((8, HEAD), BF16)
    for chunk in range(CHUNKS):
        picked = slice(chunk * COLS, (chunk + 1) * COLS)
        count = NEAR_ROWS - ROWS + (chunk + 1) * CHUNK
        delta = 0.0
        for piece in split_three(
            grad_ref[picked, :].astype(F32) * forward_ref[picked, :].astype(F32)
        ):
            delta = delta + matmul_nt(ones, piece)
        score = scores[chunk, :count, :]
        top = jnp.max(score, axis=0, keepdims=True)
        weights = jnp.exp((score - top) * SCALE)
        near_p[chunk, :count, :] = weights
        stats[0:1, picked] = top
        stats[1:2, picked] = jnp.sum(weights, axis=0, keepdims=True)
        stats[2:3, picked] = delta[0:1]
        near_u[chunk, :count, :] = matmul_nt(values[:count, :], wide_g[picked, :]) - delta[0:1]


def far_kernel(
    place_ref,
    code4,
    code3,
    code2,
    code1,
    code0,
    cos_ref,
    sin_ref,
    steps_ref,
    had_ref,
    wide_q,
    wide_g,
    near_p,
    near_u,
    stats,
    near_t,
    raw_ref,
    four_out,
    odd_out,
    parts,
    query_hbm,
    keys,
    keys_t,
    values,
    scores,
    lows,
    key_acc,
    value_acc,
    grads,
    query_out,
    sems,
):
    hadamard = had_ref[...]
    tables = (cos_ref, sin_ref)
    for block, code_ref in enumerate((code4, code3)):
        made = dequantize(code_ref, tables, block, steps_ref, hadamard)
        store_block(made, block * ROWS, keys, keys_t, values)
    edge_row = lax.broadcasted_iota(jnp.int32, (CHUNK, COLS), 0)
    edge_token = lax.broadcasted_iota(jnp.int32, (CHUNK, COLS), 1) // QUERY_HEADS
    for chunk in range(CHUNKS):
        picked = slice(chunk * COLS, (chunk + 1) * COLS)
        first = chunk * CHUNK
        score = matmul_nt(keys[first:, :], wide_q[picked, :])
        scores[chunk, first : first + CHUNK, :] = jnp.where(
            edge_row > edge_token, score[:CHUNK], FLOOR
        )
        scores[chunk, first + CHUNK :, :] = score[CHUNK:]

    missing = WIN - place_ref[0] * ROWS

    @pl.when(missing > 0)
    def _():
        row = lax.broadcasted_iota(jnp.int32, (FAR_ROWS, COLS), 0)
        for chunk in range(CHUNKS):
            scores[chunk] = jnp.where(row < missing, FLOOR, scores[chunk])

    key_acc[...] = jnp.zeros_like(key_acc)
    value_acc[...] = jnp.zeros_like(value_acc)
    grads[...] = jnp.zeros_like(grads)
    low_lane = (
        lax.broadcasted_iota(jnp.int32, (HEAD, COLS), 1) % QUERY_HEADS < QUERY_HEADS // KV_HEADS
    )
    copies = []
    for chunk in range(CHUNKS):
        picked = slice(chunk * COLS, (chunk + 1) * COLS)
        first = chunk * CHUNK
        count = NEAR_ROWS - ROWS + (chunk + 1) * CHUNK
        last = FAR_ROWS + count
        score = scores[chunk, first:, :]
        near_top = stats[0:1, picked]
        top = jnp.maximum(near_top, jnp.max(score, axis=0, keepdims=True))
        far = jnp.exp((score - top) * SCALE)
        kept = jnp.exp((near_top - top) * SCALE)
        inverse = 1.0 / (stats[1:2, picked] * kept + jnp.sum(far, axis=0, keepdims=True))
        far = far * inverse
        near = near_p[chunk, :count, :] * (kept * inverse)
        upstream = matmul_nt(values[first:, :], wide_g[picked, :]) - stats[2:3, picked]
        lows[chunk, first:FAR_ROWS, :] = far.astype(BF16)
        lows[chunk, FAR_ROWS:last, :] = near.astype(BF16)
        grads[chunk, first:FAR_ROWS, :] = (far * upstream).astype(BF16)
        grads[chunk, FAR_ROWS:last, :] = (near * near_u[chunk, :count, :]).astype(BF16)
        value_acc[first:last, :] += matmul(lows[chunk, first:last, :], wide_g[picked, :])
        key_acc[first:last, :] += matmul(grads[chunk, first:last, :], wide_q[picked, :])
        both = matmul(keys_t[...], grads[chunk, :FAR_ROWS, :])
        both = both + matmul(near_t[...], grads[chunk, FAR_ROWS:, :])
        query_grad = jnp.where(low_lane, both[:HEAD], both[HEAD:]) * SCALE
        query_out[picked, :] = query_grad.T.astype(BF16)
        rows = pl.ds(chunk * COLS, COLS)
        copies.append(
            pltpu.make_async_copy(query_out.at[rows], query_hbm.at[rows], sems.at[chunk])
        )
        copies[-1].start()

    code_refs = (code4, code3, code2, code1, code0)
    outs = (
        four_out,
        odd_out.at[:ROWS],
        parts.at[:ROWS],
        odd_out.at[ROWS:],
        parts.at[ROWS:],
    )
    for head in range(KV_HEADS):
        cols = head_cols(head)
        value_cols = head_cols(KV_HEADS + head)
        sums = [0.0, 0.0, 0.0, 0.0]
        for block in range(BLOCKS):
            rows = slice(block * ROWS, (block + 1) * ROWS)
            out = outs[block]
            part = key_acc[rows, cols] * SCALE
            part = part * cos_ref[rows, :] - pltpu.roll(part, HEAD // 2, 1) * sin_ref[rows, :]
            out[:, cols] = part.astype(out.dtype)
            code = code_refs[block][:, cols].astype(F32)
            sums[0] = sums[0] + jnp.sum(part * code, axis=0, keepdims=True)
            sums[1] = sums[1] - jnp.sum(part, axis=0, keepdims=True)
            total = 0.0
            for piece in split_two(value_acc[rows, cols]):
                total = total + matmul(piece, hadamard)
            part = total * SCALE
            out[:, value_cols] = part.astype(out.dtype)
            code = code_refs[block][:, value_cols].astype(F32)
            sums[2] = sums[2] + jnp.sum(part * code, axis=0, keepdims=True)
            sums[3] = sums[3] - jnp.sum(part, axis=0, keepdims=True)
        for term in range(4):
            row = term * KV_HEADS + head
            for copy in range(raw_ref.shape[0]):
                raw_ref[copy, row : row + 1, :] = sums[term]
    for copy in copies:
        copy.wait()


def middle_kernel(parts, four_ref, odd_ref, mid_ref):
    total = parts[:ROWS, :] + four_ref[...].astype(F32) + odd_ref[:ROWS, :].astype(F32)
    mid_ref[...] = total.astype(BF16)


def spread_kernel(in_ref, raw_ref):
    per_head = in_ref.shape[0] // 2
    terms = 4 * KV_HEADS
    for head in range(2):
        total = jnp.sum(in_ref[head * per_head : (head + 1) * per_head], axis=0)
        shape = (raw_ref.shape[0], terms, HEAD)
        raw_ref[:, head * terms : (head + 1) * terms, :] = jnp.broadcast_to(total[None], shape)


def clip_kernel(first_ref, all_ref, quant_out):
    total = jnp.sum(all_ref[...], axis=0)
    squares = jnp.sum(total * total, keepdims=True)
    mine = jnp.where(first_ref[...] > 0.0, total[: 4 * KV_HEADS], total[4 * KV_HEADS :])
    quant_out[...] = mine * jnp.minimum(1.0, clip_limit / jnp.sqrt(squares + 1e-06))


def finish_kernel(first_ref, parts, odd_ref, mid_ref, code_ref, key_out, value_out, first_out, rows_ref):
    first_out[...] = first_ref[...]
    near = odd_ref[ROWS:, :].astype(F32)
    total = parts[ROWS:, :] + near + mid_ref[...].astype(F32)
    code = code_ref[...].astype(F32)
    total = jnp.where((code > 0.0) & (code < 15.0), total, 0.0)
    for kind, out in enumerate((key_out, value_out)):
        for head in range(KV_HEADS):
            rows_ref[kind, pl.ds(head, ROWS, stride=KV_HEADS), :] = total[
                :, head_cols(kind * KV_HEADS + head)
            ]
        out[...] = rows_ref[kind].astype(BF16)


def call(
    kernel, outs, scratch=(), scalars=0, inputs=(), hbm_outs=(), copies=0, limit=24, flops=None
):
    place = {"s": pltpu.SMEM, "v": pltpu.VMEM, "h": pl.ANY}
    specs = [pl.BlockSpec(memory_space=place[kind]) for kind in "s" * scalars + inputs]
    out_specs = [pl.BlockSpec(memory_space=pltpu.VMEM)] * len(outs)
    out_specs = out_specs + [pl.BlockSpec(memory_space=pltpu.HBM)] * len(hbm_outs)
    outs = list(outs) + list(hbm_outs)
    scratch_shapes = [pltpu.VMEM(shape, dtype) for shape, dtype in scratch]
    if copies:
        scratch_shapes.append(pltpu.SemaphoreType.DMA((copies,)))
    params, cost = {}, None
    if flops:
        cost = pl.CostEstimate(flops=flops, bytes_accessed=0, transcendentals=0)
    if limit:
        params["vmem_limit_bytes"] = limit * 1024 * 1024
    return pl.pallas_call(
        kernel,
        out_shape=[jax.ShapeDtypeStruct(shape, dtype) for shape, dtype in outs],
        in_specs=specs,
        out_specs=out_specs,
        scratch_shapes=scratch_shapes,
        compiler_params=pltpu.CompilerParams(**params),
        cost_estimate=cost,
    )


def rope_tables(positions, head_size):
    freqs = rope_base ** (-jnp.arange(0, head_size, 2, dtype=jnp.float32) / head_size)
    angles = positions.astype(jnp.float32)[:, None] * freqs[None, :]
    cosines, sines = jnp.cos(angles), jnp.sin(angles)
    return (
        jnp.concatenate([cosines, cosines], axis=-1),
        jnp.concatenate([-sines, sines], axis=-1),
    )


def hadamard_signs(order):
    index = jnp.arange(order, dtype=jnp.int32)
    common = jnp.bitwise_and(index[:, None], index[None, :])
    parity = jnp.zeros((order, order), jnp.int32)
    for level in range(order.bit_length() - 1):
        parity = parity + jnp.bitwise_and(jnp.right_shift(common, level), 1)
    return (1 - 2 * (parity % 2)).astype(BF16)


def body(query, grad_out, out_forward, k_codes, k_scale, k_offset, v_codes, v_scale, v_offset):
    device_block = jnp.int32(0)
    for axis in TOK:
        device_block = device_block * lax.axis_size(axis) + lax.axis_index(axis)
    place = device_block.astype(jnp.int32).reshape(1)
    flat_codes = (KV_HEADS * ROWS, HEAD)
    flat_rows = (QUERY_HEADS * ROWS, HEAD)
    pack = (ROWS, 2 * WIDE)

    (own,) = call(
        pack_kernel, [(pack, BF16)], [((2,) + flat_codes, jnp.int32)], inputs="hh", copies=2 * PIECES, limit=0
    )(k_codes.reshape(flat_codes), v_codes.reshape(flat_codes))
    two = shift(own, 2)
    one = shift(own, 1)
    queries = query.reshape(flat_rows)
    upstream_rows = grad_out.reshape(flat_rows)
    first_row = device_block * ROWS - WIN
    cosines, sines = rope_tables(first_row + jnp.arange(SPAN, dtype=jnp.int32), HEAD)
    steps = jnp.stack([k_scale, k_offset, v_scale, v_offset]).reshape(4, WIDE)
    hadamard = hadamard_signs(HEAD)
    four = shift(two, 2)
    three = shift(two, 1)

    wide = (QUERY_HEADS * ROWS, WIDE)
    near_pairs = (CHUNKS, NEAR_ROWS, COLS)
    wide_q, wide_g, near_t, near_p, near_u, stats = call(
        near_kernel,
        [
            (wide, BF16),
            (wide, BF16),
            ((WIDE, NEAR_ROWS), BF16),
            (near_pairs, F32),
            (near_pairs, F32),
            ((8, QUERY_HEADS * ROWS), F32),
        ],
        scratch=[
            ((NEAR_ROWS, WIDE), BF16),
            ((NEAR_ROWS, WIDE), BF16),
            (near_pairs, F32),
        ],
        scalars=1,
        inputs="v" * 10,
    )(
        place,
        queries,
        upstream_rows,
        out_forward.reshape(flat_rows),
        two,
        one,
        own,
        cosines,
        sines,
        steps,
        hadamard,
    )
    raw, four_part, odd_part, parts, query_grad = call(
        far_kernel,
        [
            ((axis_count(FLAT), 4 * KV_HEADS, HEAD), F32),
            (pack, BF16),
            ((2 * ROWS, 2 * WIDE), BF16),
            ((2 * ROWS, 2 * WIDE), F32),
        ],
        scratch=[
            ((FAR_ROWS, WIDE), BF16),
            ((WIDE, FAR_ROWS), BF16),
            ((FAR_ROWS, WIDE), BF16),
            ((CHUNKS, FAR_ROWS, COLS), F32),
            ((CHUNKS, SPAN, COLS), BF16),
            ((SPAN, WIDE), F32),
            ((SPAN, WIDE), F32),
            ((CHUNKS, SPAN, COLS), BF16),
            (flat_rows, BF16),
        ],
        scalars=1,
        inputs="v" * 15,
        hbm_outs=[(flat_rows, BF16)],
        copies=CHUNKS,
    )(
        place,
        four,
        three,
        two,
        one,
        own,
        cosines,
        sines,
        steps,
        hadamard,
        wide_q,
        wide_g,
        near_p,
        near_u,
        stats,
        near_t,
    )
    four_part = shift(four_part, -2)
    odd_part = shift(odd_part, -1)
    raw = lax.all_to_all(raw, FLAT, 0, 0)
    columns = axis_count(("z",))
    (raw,) = call(spread_kernel, [((columns, 8 * KV_HEADS, HEAD), F32)], inputs="v")(raw)
    (mid,) = call(middle_kernel, [(pack, BF16)], inputs="vvv", flops=MIDDLE_FLOPS)(
        parts, four_part, odd_part
    )
    mid = shift(mid, -2)
    raw = lax.all_to_all(raw, "z", 0, 0)
    first = jnp.where(lax.axis_index("head") == 0, jnp.ones((4 * KV_HEADS, HEAD), F32), 0.0)
    key_grad, value_grad, first = call(
        finish_kernel,
        [(flat_codes, BF16)] * 2 + [((4 * KV_HEADS, HEAD), F32)],
        scratch=[((2,) + flat_codes, F32)],
        inputs="vvvvv",
        flops=FINISH_FLOPS,
    )(first, parts, odd_part, mid, own)
    (quant,) = call(clip_kernel, [((4 * KV_HEADS, HEAD), F32)], inputs="vv")(first, raw)
    return (
        query_grad.reshape(ROWS, QUERY_HEADS, HEAD),
        key_grad.reshape(ROWS, KV_HEADS, HEAD),
        value_grad.reshape(ROWS, KV_HEADS, HEAD),
        quant.reshape(4, KV_HEADS, HEAD),
    )


def solution(mesh):
    sizes = (mesh.shape["head"], mesh.shape["outer"] // 2, 2, 2, mesh.shape["inner"] // 2)
    split = Mesh(mesh.devices.reshape(sizes), ("head",) + TOK)
    rows = P(TOK, "head", None)
    steps = P("head", None)
    return jax.shard_map(
        body,
        mesh=split,
        in_specs=(rows, rows, rows, rows, steps, steps, rows, steps, steps),
        out_specs=(rows, rows, rows, P(None, "head", None)),
        check_vma=False,
    )
```

time: 89.3 us -> 84 us (0.941)
  starting transfers between devices: 46.8 us -> 42.4 us
  waiting for transfers between devices: 28.1 us -> 24.9 us
  Pallas kernels: 9.49 us -> 11.6 us
  local copies, waits for them, and re-layouts: 1.84 us -> 0.92 us
    ppermute x8 -> x7, starting transfers between devices: 34.2 us -> 27.8 us  [shift(): return lax.ppermute(value, TOK, pairs)]
    all_to_all x1, waiting for transfers between devices: 7.55 us -> 3.63 us  [body(): raw = lax.all_to_all(raw, FLAT, 0, 0)]
    all_to_all x1, starting transfers between devices: 3.51 us -> 7.18 us  [body(): raw = lax.all_to_all(raw, 'z', 0, 0)]
    pallas_call x5 -> x7, Pallas kernels: 9.49 us -> 11.6 us  [the longest x1 4.78 us: body(): call(far_kernel, [((axis_count(FLAT), 4 * KV_HEADS, HEAD), F32), (pack, B...]
    all_to_all x1, starting transfers between devices: 9.05 us -> 7.43 us  [body(): raw = lax.all_to_all(raw, FLAT, 0, 0)]
    ppermute x8 -> x7, waiting for transfers between devices: 19.7 us -> 21.2 us  [shift(): return lax.ppermute(value, TOK, pairs)]
    unnamed x18 -> x10, local copies, waits for them, and re-layouts: 1.84 us -> 0.91 us
  transfers between devices with their start and end apart: 10 -> 9, of which waited for: 5 -> 5; matrix products, arithmetic and copies ran while one was open for 2% -> 3% of each run, Pallas kernels for 1% -> 5%
where the time goes in v3:
time: 84 us; the launch traced here: 83 us
  starting transfers between devices  42.4 us (50%)
  waiting for transfers between devices  24.9 us (30%)
  Pallas kernels  11.6 us (14%)
  other arithmetic  2.3 us (3%)
  local copies, waits for them, and re-layouts  0.92 us (1%)
  between operations  0.88 us (1%)
    ppermute x7, starting transfers between devices, shift(): return lax.ppermute(value, TOK, pairs)  27.8 us
    ppermute x7, waiting for transfers between devices, shift(): return lax.ppermute(value, TOK, pairs)  21.2 us
    all_to_all x1, starting transfers between devices, body(): raw = lax.all_to_all(raw, FLAT, 0, 0)  7.43 us
    all_to_all x1, starting transfers between devices, body(): raw = lax.all_to_all(raw, 'z', 0, 0)  7.18 us
    pallas_call x1, Pallas kernels, body(): call(far_kernel, [((axis_count(FLAT), 4 * KV_HEADS, HEAD), F32), (pack, B...  4.78 us
    all_to_all x1, waiting for transfers between devices, body(): raw = lax.all_to_all(raw, FLAT, 0, 0)  3.63 us
    pallas_call x1, Pallas kernels, body(): call(near_kernel, [(wide, BF16), (wide, BF16), ((WIDE, NEAR_ROWS), BF16),...  2.8 us
    pallas_call x1, Pallas kernels, body(): call(pack_kernel, [(pack, BF16)], [((2,) + flat_codes, jnp.int32)], input...  1.71 us
  transfers between devices with their start and end apart: 9, of which 5 were waited for; matrix products, arithmetic and copies ran while one was open for 3% of the time, Pallas kernels for 5%

profile of v3, /device:TPU:1, one launch (start us, length us, event | category | flops | bytes accessed | tf_op | source)
XLA Modules:
  0.0 83.0 jit_solution(15601813847534854979)
XLA Ops:
  0.6 0.0 copy-start.2
  0.6 0.0 copy-start.3
  0.7 0.0 copy-start.4
  0.7 1.7 %shard_map.120.code0.code_ref = bf16[128,512]{1,0:T(8,128)(2,1)} custom-call(s32[256,128]{1,0:T(8,128)} %bitcast.17, s32[256,128]{1,0:T(8,128)} %bitcast.18), custom_call_target="tpu_custom_call" | custom-call | tf_op jit(solution)/shard_map/pallas_call | solution.py:417
  2.4 5.7 %collective-permute-start = (bf16[128,512]{1,0:T(8,128)(2,1)}, bf16[128,512]{1,0:T(8,128)(2,1)S(1)}, u32[]{:S(2)}, u32[]{:S(2)}) collective-permute-start(bf16[128,512]{1,0:T(8,128)(2,1)} %shard_map.120.code0.code_ref), channel_id=1, source_target_pairs={{0,2},{1,3},{2,4},{3,5},{4,6},{5,7},{6,8},{7,9},{8,10},{9,11},{10,... | collective-permute-start | bytes 393224 | tf_op jit(solution)/shard_map/ppermute | solution.py:42
  8.1 3.5 %collective-permute-start.3 = (bf16[128,512]{1,0:T(8,128)(2,1)}, bf16[128,512]{1,0:T(8,128)(2,1)S(1)}, u32[]{:S(2)}, u32[]{:S(2)}) collective-permute-start(bf16[128,512]{1,0:T(8,128)(2,1)} %shard_map.120.code0.code_ref), channel_id=1, source_target_pairs={{0,1},{1,2},{2,3},{3,4},{4,5},{5,6},{6,7},{7,8},{8,9},{9,10},{10,1... | collective-permute-start | bytes 393224 | tf_op jit(solution)/shard_map/ppermute | solution.py:42
  11.7 1.2 %fusion = (f32[640,64]{1,0:T(8,128)S(1)}, f32[640,64]{1,0:T(8,128)S(1)}, f32[640,64]{1,0:T(8,128)S(1)}) fusion(f32[64]{0:T(128)S(1)} %multiply_power_fusion, f32[640]{0:T(1024)S(1)} %add_convert_fusion), kind=kLoop, calls=%fused_computation.4 | loop fusion | flops 81920 | bytes 494336 | tf_op jit(solution)/shard_map/neg | solution.py:395
  12.9 0.1 fusion.4.had_ref
  13.0 8.6 %collective-permute-done.code2 = bf16[128,512]{1,0:T(8,128)(2,1)S(1)} collective-permute-done((bf16[128,512]{1,0:T(8,128)(2,1)}, bf16[128,512]{1,0:T(8,128)(2,1)S(1)}, u32[]{:S(2)}, u32[]{:S(2)}) %collective-permute-start) | collective-permute-done | bytes 131104 | tf_op jit(solution)/shard_map/ppermute | solution.py:42
  21.6 1.9 %collective-permute-start.1 = (bf16[128,512]{1,0:T(8,128)(2,1)S(1)}, bf16[128,512]{1,0:T(8,128)(2,1)S(1)}, u32[]{:S(2)}, u32[]{:S(2)}) collective-permute-start(bf16[128,512]{1,0:T(8,128)(2,1)S(1)} %collective-permute-done.code2), channel_id=1, source_target_pairs={{0,2},{1,3},{2,4},{3,5},{4,6},{5,7},{6,8},{7,9},{8,10},{9,11},{10,... | collective-permute-start | bytes 393224 | tf_op jit(solution)/shard_map/ppermute | solution.py:42
  23.5 4.1 %collective-permute-start.2 = (bf16[128,512]{1,0:T(8,128)(2,1)S(1)}, bf16[128,512]{1,0:T(8,128)(2,1)S(1)}, u32[]{:S(2)}, u32[]{:S(2)}) collective-permute-start(bf16[128,512]{1,0:T(8,128)(2,1)S(1)} %collective-permute-done.code2), channel_id=1, source_target_pairs={{0,1},{1,2},{2,3},{3,4},{4,5},{5,6},{6,7},{7,8},{8,9},{9,10},{10,1... | collective-permute-start | bytes 393224 | tf_op jit(solution)/shard_map/ppermute | solution.py:42
  27.7 0.7 pad_maximum_fusion.2.steps_ref
  28.4 0.2 pad_maximum_fusion
  28.6 0.0 collective-permute-done.3.code1
  28.6 0.0 copy-done.2
  28.7 0.0 copy-done.3
  28.7 0.0 copy-done.4
  28.7 0.0 copy-start
  28.7 0.9 %copy-done = bf16[128,512]{1,0:T(8,128)(2,1)S(1)} copy-done((bf16[128,512]{1,0:T(8,128)(2,1)S(1)}, bf16[128,512]{1,0:T(8,128)(2,1)}, u32[]{:S(2)}) %copy-start) | copy-done | bytes 131096
  29.6 2.8 %shard_map.121 = (bf16[2048,256]{1,0:T(8,128)(2,1)S(1)}, bf16[2048,256]{1,0:T(8,128)(2,1)S(1)}, bf16[256,384]{1,0:T(8,128)(2,1)S(1)}, f32[4,384,512]{2,1,0:T(8,1...) custom-call(s32[1]{0:T(128)} %bitcast.place_ref, bf16[2048,128]{1,0:T(8,128)(2,1)S(1)} %bitcast.14, ...), custom_call_target="tpu_custom_call" | custom-call | tf_op jit(solution)/shard_map/pallas_call | solution.py:433
  32.4 0.9 %collective-permute-done.1.code4 = bf16[128,512]{1,0:T(8,128)(2,1)S(1)} collective-permute-done((bf16[128,512]{1,0:T(8,128)(2,1)S(1)}, bf16[128,512]{1,0:T(8,128)(2,1)S(1)}, u32[]{:S(2)}, u32[]{:S(2)}) %collective-permute-start.1) | collective-permute-done | bytes 131104 | tf_op jit(solution)/shard_map/ppermute | solution.py:42
  33.3 4.5 %collective-permute-done.2.code3 = bf16[128,512]{1,0:T(8,128)(2,1)S(1)} collective-permute-done((bf16[128,512]{1,0:T(8,128)(2,1)S(1)}, bf16[128,512]{1,0:T(8,128)(2,1)S(1)}, u32[]{:S(2)}, u32[]{:S(2)}) %collective-permute-start.2) | collective-permute-done | bytes 131104 | tf_op jit(solution)/shard_map/ppermute | solution.py:42
  37.9 4.8 %shard_map.122 = (f32[32,8,128]{2,1,0:T(8,128)}, bf16[128,512]{1,0:T(8,128)(2,1)S(1)}, bf16[256,512]{1,0:T(8,128)(2,1)S(1)}, f32[256,512]{1,0:T(8,128)S(1)}, bf16[2048,128]{1,0:T(8,128)(2,1)}) custom-call(s32[1]{0:T(128)} %bitcast.place_ref, bf16[128,512]{1,0:T(8,128)(2,1)S(1)} %collective-permute-done.1.code4, ...), custom_call_target="tpu_custom_call" | custom-call | tf_op jit(solution)/shard_map/pallas_call | solution.py:463
  42.6 1.9 %collective-permute-start.4 = (bf16[256,512]{1,0:T(8,128)(2,1)S(1)}, bf16[256,512]{1,0:T(8,128)(2,1)S(1)}, u32[]{:S(2)}, u32[]{:S(2)}) collective-permute-start(bf16[256,512]{1,0:T(8,128)(2,1)S(1)} %get-tuple-element.26), channel_id=1, source_target_pairs={{1,0},{2,1},{3,2},{4,3},{5,4},{6,5},{7,6},{8,7},{9,8},{10,9},{11,1... | collective-permute-start | bytes 786440 | tf_op jit(solution)/shard_map/ppermute | solution.py:42
  44.6 7.4 %all-to-all-start = ((f32[32,8,128]{2,1,0:T(8,128)}), f32[32,8,128]{2,1,0:T(8,128)S(1)}, u32[]{:S(2)}, u32[]{:S(2)}) async-start(f32[32,8,128]{2,1,0:T(8,128)} %get-tuple-element.31), calls=%async_computation | async-start | bytes 262144 | tf_op jit(solution)/shard_map/all_to_all | solution.py:506
  52.0 3.9 %collective-permute-start.5 = (bf16[128,512]{1,0:T(8,128)(2,1)S(1)}, bf16[128,512]{1,0:T(8,128)(2,1)S(1)}, u32[]{:S(2)}, u32[]{:S(2)}) collective-permute-start(bf16[128,512]{1,0:T(8,128)(2,1)S(1)} %get-tuple-element.27), channel_id=1, source_target_pairs={{2,0},{3,1},{4,2},{5,3},{6,4},{7,5},{8,6},{9,7},{10,8},{11,9},{12,... | collective-permute-start | bytes 393224 | tf_op jit(solution)/shard_map/ppermute | solution.py:42
  56.0 3.6 %all-to-all-done.in_ref = f32[32,8,128]{2,1,0:T(8,128)S(1)} async-done(((f32[32,8,128]{2,1,0:T(8,128)}), f32[32,8,128]{2,1,0:T(8,128)S(1)}, u32[]{:S(2)}, u32[]{:S(2)}) %all-to-all-start) | async-done | bytes 131104 | tf_op jit(solution)/shard_map/all_to_all | solution.py:506
  59.6 0.7 shard_map.125
  60.3 7.2 %all-to-all-start.1 = ((f32[16,16,128]{2,1,0:T(8,128)}), f32[16,16,128]{2,1,0:T(8,128)S(1)}, u32[]{:S(2)}, u32[]{:S(2)}) async-start(f32[16,16,128]{2,1,0:T(8,128)} %shard_map.125), calls=%async_computation.1 | async-start | bytes 262144 | tf_op jit(solution)/shard_map/all_to_all | solution.py:513
  67.5 0.0 collective-permute-done.5.four_ref
  67.5 0.0 collective-permute-done.4.odd_ref
  67.5 0.0 copy-start.1
  67.5 6.7 %collective-permute-start.6 = (bf16[128,512]{1,0:T(8,128)(2,1)S(1)}, bf16[128,512]{1,0:T(8,128)(2,1)S(1)}, u32[]{:S(2)}, u32[]{:S(2)}) collective-permute-start(bf16[128,512]{1,0:T(8,128)(2,1)S(1)} %shard_map.123), channel_id=1, source_target_pairs={{2,0},{3,1},{4,2},{5,3},{6,4},{7,5},{8,6},{9,7},{10,8},{11,9},{12,... | collective-permute-start | bytes 393224 | tf_op jit(solution)/shard_map/ppermute | solution.py:42
  74.2 7.2 %collective-permute-done.6.mid_ref = bf16[128,512]{1,0:T(8,128)(2,1)S(1)} collective-permute-done((bf16[128,512]{1,0:T(8,128)(2,1)S(1)}, bf16[128,512]{1,0:T(8,128)(2,1)S(1)}, u32[]{:S(2)}, u32[]{:S(2)}) %collective-permute-start.6) | collective-permute-done | bytes 131104 | tf_op jit(solution)/shard_map/ppermute | solution.py:42
  81.4 0.0 copy-done.1
  81.4 0.8 shard_map.124
  82.2 0.0 all-to-all-done.1.all_ref
  82.2 0.7 shard_map.126
  (4 shorter events, 0.1 us)
Async XLA Ops:
  0.6 28.0 %copy-start.2 = (bf16[128,16,128]{2,1,0:T(8,128)(2,1)S(1)}, bf16[128,16,128]{2,1,0:T(8,128)(2,1)}, u32[]{:S(2)}) copy-start(bf16[128,16,128]{2,1,0:T(8,128)(2,1)} %param.9) | copy-start | bytes 1572868
  0.6 28.0 %copy-start.3 = (bf16[128,16,128]{2,1,0:T(8,128)(2,1)S(1)}, bf16[128,16,128]{2,1,0:T(8,128)(2,1)}, u32[]{:S(2)}) copy-start(bf16[128,16,128]{2,1,0:T(8,128)(2,1)} %param.10) | copy-start | bytes 1572868
  0.7 28.0 %copy-start.4 = (bf16[128,16,128]{2,1,0:T(8,128)(2,1)S(1)}, bf16[128,16,128]{2,1,0:T(8,128)(2,1)}, u32[]{:S(2)}) copy-start(bf16[128,16,128]{2,1,0:T(8,128)(2,1)} %param.11) | copy-start | bytes 1572868
  2.4 19.2 %collective-permute-start = (bf16[128,512]{1,0:T(8,128)(2,1)}, bf16[128,512]{1,0:T(8,128)(2,1)S(1)}, u32[]{:S(2)}, u32[]{:S(2)}) collective-permute-start(bf16[128,512]{1,0:T(8,128)(2,1)} %shard_map.120.code0.code_ref), channel_id=1, source_target_pairs={{0,2},{1,3},{2,4},{3,5},{4,6},{5,7},{6,8},{7,9},{8,10},{9,11},{10,... | collective-permute-start | bytes 393224 | tf_op jit(solution)/shard_map/ppermute | solution.py:42
  8.1 20.5 %collective-permute-start.3 = (bf16[128,512]{1,0:T(8,128)(2,1)}, bf16[128,512]{1,0:T(8,128)(2,1)S(1)}, u32[]{:S(2)}, u32[]{:S(2)}) collective-permute-start(bf16[128,512]{1,0:T(8,128)(2,1)} %shard_map.120.code0.code_ref), channel_id=1, source_target_pairs={{0,1},{1,2},{2,3},{3,4},{4,5},{5,6},{6,7},{7,8},{8,9},{9,10},{10,1... | collective-permute-start | bytes 393224 | tf_op jit(solution)/shard_map/ppermute | solution.py:42
  21.6 11.7 %collective-permute-start.1 = (bf16[128,512]{1,0:T(8,128)(2,1)S(1)}, bf16[128,512]{1,0:T(8,128)(2,1)S(1)}, u32[]{:S(2)}, u32[]{:S(2)}) collective-permute-start(bf16[128,512]{1,0:T(8,128)(2,1)S(1)} %collective-permute-done.code2), channel_id=1, source_target_pairs={{0,2},{1,3},{2,4},{3,5},{4,6},{5,7},{6,8},{7,9},{8,10},{9,11},{10,... | collective-permute-start | bytes 393224 | tf_op jit(solution)/shard_map/ppermute | solution.py:42
  23.5 14.3 %collective-permute-start.2 = (bf16[128,512]{1,0:T(8,128)(2,1)S(1)}, bf16[128,512]{1,0:T(8,128)(2,1)S(1)}, u32[]{:S(2)}, u32[]{:S(2)}) collective-permute-start(bf16[128,512]{1,0:T(8,128)(2,1)S(1)} %collective-permute-done.code2), channel_id=1, source_target_pairs={{0,1},{1,2},{2,3},{3,4},{4,5},{5,6},{6,7},{7,8},{8,9},{9,10},{10,1... | collective-permute-start | bytes 393224 | tf_op jit(solution)/shard_map/ppermute | solution.py:42
  28.7 0.9 %copy-start = (bf16[128,512]{1,0:T(8,128)(2,1)S(1)}, bf16[128,512]{1,0:T(8,128)(2,1)}, u32[]{:S(2)}) copy-start(bf16[128,512]{1,0:T(8,128)(2,1)} %shard_map.120.code0.code_ref) | copy-start | bytes 393220
  42.6 24.8 %collective-permute-start.4 = (bf16[256,512]{1,0:T(8,128)(2,1)S(1)}, bf16[256,512]{1,0:T(8,128)(2,1)S(1)}, u32[]{:S(2)}, u32[]{:S(2)}) collective-permute-start(bf16[256,512]{1,0:T(8,128)(2,1)S(1)} %get-tuple-element.26), channel_id=1, source_target_pairs={{1,0},{2,1},{3,2},{4,3},{5,4},{6,5},{7,6},{8,7},{9,8},{10,9},{11,1... | collective-permute-start | bytes 786440 | tf_op jit(solution)/shard_map/ppermute | solution.py:42
  44.6 15.0 %all-to-all-start = ((f32[32,8,128]{2,1,0:T(8,128)}), f32[32,8,128]{2,1,0:T(8,128)S(1)}, u32[]{:S(2)}, u32[]{:S(2)}) async-start(f32[32,8,128]{2,1,0:T(8,128)} %get-tuple-element.31), calls=%async_computation | async-start | bytes 262144 | tf_op jit(solution)/shard_map/all_to_all | solution.py:506
  52.0 15.4 %collective-permute-start.5 = (bf16[128,512]{1,0:T(8,128)(2,1)S(1)}, bf16[128,512]{1,0:T(8,128)(2,1)S(1)}, u32[]{:S(2)}, u32[]{:S(2)}) collective-permute-start(bf16[128,512]{1,0:T(8,128)(2,1)S(1)} %get-tuple-element.27), channel_id=1, source_target_pairs={{2,0},{3,1},{4,2},{5,3},{6,4},{7,5},{8,6},{9,7},{10,8},{11,9},{12,... | collective-permute-start | bytes 393224 | tf_op jit(solution)/shard_map/ppermute | solution.py:42
  60.3 21.9 %all-to-all-start.1 = ((f32[16,16,128]{2,1,0:T(8,128)}), f32[16,16,128]{2,1,0:T(8,128)S(1)}, u32[]{:S(2)}, u32[]{:S(2)}) async-start(f32[16,16,128]{2,1,0:T(8,128)} %shard_map.125), calls=%async_computation.1 | async-start | bytes 262144 | tf_op jit(solution)/shard_map/all_to_all | solution.py:513
  67.5 13.9 %copy-start.1 = (bf16[128,512]{1,0:T(8,128)(2,1)S(1)}, bf16[128,512]{1,0:T(8,128)(2,1)}, u32[]{:S(2)}) copy-start(bf16[128,512]{1,0:T(8,128)(2,1)} %shard_map.120.code0.code_ref) | copy-start | bytes 393220
  67.5 13.9 %collective-permute-start.6 = (bf16[128,512]{1,0:T(8,128)(2,1)S(1)}, bf16[128,512]{1,0:T(8,128)(2,1)S(1)}, u32[]{:S(2)}, u32[]{:S(2)}) collective-permute-start(bf16[128,512]{1,0:T(8,128)(2,1)S(1)} %shard_map.123), channel_id=1, source_target_pairs={{2,0},{3,1},{4,2},{5,3},{6,4},{7,5},{8,6},{9,7},{10,8},{11,9},{12,... | collective-permute-start | bytes 393224 | tf_op jit(solution)/shard_map/ppermute | solution.py:42

commit v4 on v3

--- a/solution.py
+++ b/solution.py
@@ -20,8 +20,10 @@
 CHUNKS = ROWS // CHUNK
 FAR_BLOCKS = 2
 PIECES = 4
+PACK_LIMIT = 0
 FINISH_FLOPS = None
-MIDDLE_FLOPS = 3 * 10**9
+ADD_FLOPS = None
+MIDDLE_FLOPS = 2 * 10**9
 FAR_ROWS = FAR_BLOCKS * ROWS
 NEAR_ROWS = SPAN - FAR_ROWS
 SCALE = 1.0 / math.sqrt(HEAD)
@@ -211,8 +213,7 @@
     stats,
     near_t,
     raw_ref,
-    four_out,
-    odd_out,
+    back_out,
     parts,
     query_hbm,
     keys,
@@ -288,13 +289,8 @@
         copies[-1].start()
 
     code_refs = (code4, code3, code2, code1, code0)
-    outs = (
-        four_out,
-        odd_out.at[:ROWS],
-        parts.at[:ROWS],
-        odd_out.at[ROWS:],
-        parts.at[ROWS:],
-    )
+    outs = [back_out.at[:ROWS], back_out.at[ROWS:]]
+    outs = outs + [parts.at[block * ROWS : (block + 1) * ROWS] for block in range(3)]
     for head in range(KV_HEADS):
         cols = head_cols(head)
         value_cols = head_cols(KV_HEADS + head)
@@ -324,9 +320,10 @@
         copy.wait()
 
 
-def middle_kernel(parts, four_ref, odd_ref, mid_ref):
-    total = parts[:ROWS, :] + four_ref[...].astype(F32) + odd_ref[:ROWS, :].astype(F32)
-    mid_ref[...] = total.astype(BF16)
+def middle_kernel(parts, back_ref, mid_ref, near_ref):
+    total = parts[: 2 * ROWS, :] + back_ref[...].astype(F32)
+    mid_ref[...] = total[:ROWS].astype(BF16)
+    near_ref[...] = total[ROWS:].astype(BF16)
 
 
 def spread_kernel(in_ref, raw_ref):
@@ -345,10 +342,13 @@
     quant_out[...] = mine * jnp.minimum(1.0, clip_limit / jnp.sqrt(squares + 1e-06))
 
 
-def finish_kernel(first_ref, parts, odd_ref, mid_ref, code_ref, key_out, value_out, first_out, rows_ref):
+def add_kernel(parts, mid_ref, sum_ref):
+    sum_ref[...] = parts[2 * ROWS :, :] + mid_ref[...].astype(F32)
+
+
+def finish_kernel(first_ref, sum_ref, near_ref, code_ref, key_out, value_out, first_out, rows_ref):
     first_out[...] = first_ref[...]
-    near = odd_ref[ROWS:, :].astype(F32)
-    total = parts[ROWS:, :] + near + mid_ref[...].astype(F32)
+    total = sum_ref[...] + near_ref[...].astype(F32)
     code = code_ref[...].astype(F32)
     total = jnp.where((code > 0.0) & (code < 15.0), total, 0.0)
     for kind, out in enumerate((key_out, value_out)):
@@ -371,7 +371,7 @@
     if copies:
         scratch_shapes.append(pltpu.SemaphoreType.DMA((copies,)))
     params, cost = {}, None
-    if flops:
+    if flops is not None:
         cost = pl.CostEstimate(flops=flops, bytes_accessed=0, transcendentals=0)
     if limit:
         params["vmem_limit_bytes"] = limit * 1024 * 1024
@@ -460,13 +460,12 @@
         steps,
         hadamard,
     )
-    raw, four_part, odd_part, parts, query_grad = call(
+    raw, back, parts, query_grad = call(
         far_kernel,
         [
             ((axis_count(FLAT), 4 * KV_HEADS, HEAD), F32),
-            (pack, BF16),
             ((2 * ROWS, 2 * WIDE), BF16),
-            ((2 * ROWS, 2 * WIDE), F32),
+            ((3 * ROWS, 2 * WIDE), F32),
         ],
         scratch=[
             ((FAR_ROWS, WIDE), BF16),
@@ -501,24 +500,23 @@
         stats,
         near_t,
     )
-    four_part = shift(four_part, -2)
-    odd_part = shift(odd_part, -1)
+    back = shift(back, -2)
     raw = lax.all_to_all(raw, FLAT, 0, 0)
     columns = axis_count(("z",))
     (raw,) = call(spread_kernel, [((columns, 8 * KV_HEADS, HEAD), F32)], inputs="v")(raw)
-    (mid,) = call(middle_kernel, [(pack, BF16)], inputs="vvv", flops=MIDDLE_FLOPS)(
-        parts, four_part, odd_part
-    )
+    mid, near = call(middle_kernel, [(pack, BF16)] * 2, inputs="vv", flops=MIDDLE_FLOPS)(parts, back)
     mid = shift(mid, -2)
+    near = shift(near, -1)
     raw = lax.all_to_all(raw, "z", 0, 0)
     first = jnp.where(lax.axis_index("head") == 0, jnp.ones((4 * KV_HEADS, HEAD), F32), 0.0)
+    (own_sum,) = call(add_kernel, [(pack, F32)], inputs="vv", flops=ADD_FLOPS)(parts, mid)
     key_grad, value_grad, first = call(
         finish_kernel,
         [(flat_codes, BF16)] * 2 + [((4 * KV_HEADS, HEAD), F32)],
         scratch=[((2,) + flat_codes, F32)],
-        inputs="vvvvv",
+        inputs="vvvv",
         flops=FINISH_FLOPS,
-    )(first, parts, odd_part, mid, own)
+    )(first, own_sum, near, own)
     (quant,) = call(clip_kernel, [((4 * KV_HEADS, HEAD), F32)], inputs="vv")(first, raw)
     return (
         query_grad.reshape(ROWS, QUERY_HEADS, HEAD),

time: 84 us -> 83.4 us (level)
  starting transfers between devices: 42.4 us -> 41.1 us
  waiting for transfers between devices: 24.9 us -> 25.9 us
    all_to_all x1, waiting for transfers between devices: 3.63 us -> 5.37 us  [body(): raw = lax.all_to_all(raw, FLAT, 0, 0)]
    pallas_call x2 -> x3, Pallas kernels: 4.82 us -> 4.82 us  [the longest x1 4.75 us: body(): call(far_kernel, [((axis_count(FLAT), 4 * KV_HEADS, HEAD), F32), ((2 * RO...]
  transfers between devices with their start and end apart: 9 -> 9, of which waited for: 5 -> 7; matrix products, arithmetic and copies ran while one was open for 3% -> 3% of each run, Pallas kernels for 5% -> 5%
where the time goes in v4:
time: 83.4 us; the launch traced here: 82.7 us
  starting transfers between devices  41.1 us (49%)
  waiting for transfers between devices  25.9 us (31%)
  Pallas kernels  11.5 us (14%)
  other arithmetic  2.3 us (3%)
  local copies, waits for them, and re-layouts  0.92 us (1%)
  between operations  0.87 us (1%)
    ppermute x7, starting transfers between devices, shift(): return lax.ppermute(value, TOK, pairs)  27.1 us
    ppermute x7, waiting for transfers between devices, shift(): return lax.ppermute(value, TOK, pairs)  20.6 us
    all_to_all x1, starting transfers between devices, body(): raw = lax.all_to_all(raw, FLAT, 0, 0)  7.44 us
    all_to_all x1, starting transfers between devices, body(): raw = lax.all_to_all(raw, 'z', 0, 0)  6.63 us
    all_to_all x1, waiting for transfers between devices, body(): raw = lax.all_to_all(raw, FLAT, 0, 0)  5.37 us
    pallas_call x1, Pallas kernels, body(): call(far_kernel, [((axis_count(FLAT), 4 * KV_HEADS, HEAD), F32), ((2 * RO...  4.75 us
    pallas_call x1, Pallas kernels, body(): call(near_kernel, [(wide, BF16), (wide, BF16), ((WIDE, NEAR_ROWS), BF16),...  2.8 us
    pallas_call x1, Pallas kernels, body(): call(pack_kernel, [(pack, BF16)], [((2,) + flat_codes, jnp.int32)], input...  1.72 us
  transfers between devices with their start and end apart: 9, of which 7 were waited for; matrix products, arithmetic and copies ran while one was open for 3% of the time, Pallas kernels for 5%

profile of v4, /device:TPU:1, one launch (start us, length us, event | category | flops | bytes accessed | tf_op | source)
XLA Modules:
  0.0 82.7 jit_solution(15665745366191831711)
XLA Ops:
  0.6 0.0 copy-start.2
  0.6 0.0 copy-start.3
  0.7 0.0 copy-start.4
  0.7 1.7 %shard_map.120.code0.code_ref = bf16[128,512]{1,0:T(8,128)(2,1)} custom-call(s32[256,128]{1,0:T(8,128)} %bitcast.17, s32[256,128]{1,0:T(8,128)} %bitcast.18), custom_call_target="tpu_custom_call" | custom-call | tf_op jit(solution)/shard_map/pallas_call | solution.py:417
  2.4 0.0 copy-start.1
  2.4 5.9 %collective-permute-start = (bf16[128,512]{1,0:T(8,128)(2,1)}, bf16[128,512]{1,0:T(8,128)(2,1)S(1)}, u32[]{:S(2)}, u32[]{:S(2)}) collective-permute-start(bf16[128,512]{1,0:T(8,128)(2,1)} %shard_map.120.code0.code_ref), channel_id=1, source_target_pairs={{0,2},{1,3},{2,4},{3,5},{4,6},{5,7},{6,8},{7,9},{8,10},{9,11},{10,... | collective-permute-start | bytes 393224 | tf_op jit(solution)/shard_map/ppermute | solution.py:44
  8.3 3.5 %collective-permute-start.3 = (bf16[128,512]{1,0:T(8,128)(2,1)}, bf16[128,512]{1,0:T(8,128)(2,1)S(1)}, u32[]{:S(2)}, u32[]{:S(2)}) collective-permute-start(bf16[128,512]{1,0:T(8,128)(2,1)} %shard_map.120.code0.code_ref), channel_id=1, source_target_pairs={{0,1},{1,2},{2,3},{3,4},{4,5},{5,6},{6,7},{7,8},{8,9},{9,10},{10,1... | collective-permute-start | bytes 393224 | tf_op jit(solution)/shard_map/ppermute | solution.py:44
  11.9 1.2 %fusion = (f32[640,64]{1,0:T(8,128)S(1)}, f32[640,64]{1,0:T(8,128)S(1)}, f32[640,64]{1,0:T(8,128)S(1)}) fusion(f32[64]{0:T(128)S(1)} %multiply_power_fusion, f32[640]{0:T(1024)S(1)} %add_convert_fusion), kind=kLoop, calls=%fused_computation.4 | loop fusion | flops 81920 | bytes 494336 | tf_op jit(solution)/shard_map/neg | solution.py:395
  13.1 0.1 fusion.4.had_ref
  13.2 8.6 %collective-permute-done.code2 = bf16[128,512]{1,0:T(8,128)(2,1)S(1)} collective-permute-done((bf16[128,512]{1,0:T(8,128)(2,1)}, bf16[128,512]{1,0:T(8,128)(2,1)S(1)}, u32[]{:S(2)}, u32[]{:S(2)}) %collective-permute-start) | collective-permute-done | bytes 131104 | tf_op jit(solution)/shard_map/ppermute | solution.py:44
  21.8 1.9 %collective-permute-start.1 = (bf16[128,512]{1,0:T(8,128)(2,1)S(1)}, bf16[128,512]{1,0:T(8,128)(2,1)S(1)}, u32[]{:S(2)}, u32[]{:S(2)}) collective-permute-start(bf16[128,512]{1,0:T(8,128)(2,1)S(1)} %collective-permute-done.code2), channel_id=1, source_target_pairs={{0,2},{1,3},{2,4},{3,5},{4,6},{5,7},{6,8},{7,9},{8,10},{9,11},{10,... | collective-permute-start | bytes 393224 | tf_op jit(solution)/shard_map/ppermute | solution.py:44
  23.7 4.1 %collective-permute-start.2 = (bf16[128,512]{1,0:T(8,128)(2,1)S(1)}, bf16[128,512]{1,0:T(8,128)(2,1)S(1)}, u32[]{:S(2)}, u32[]{:S(2)}) collective-permute-start(bf16[128,512]{1,0:T(8,128)(2,1)S(1)} %collective-permute-done.code2), channel_id=1, source_target_pairs={{0,1},{1,2},{2,3},{3,4},{4,5},{5,6},{6,7},{7,8},{8,9},{9,10},{10,1... | collective-permute-start | bytes 393224 | tf_op jit(solution)/shard_map/ppermute | solution.py:44
  27.8 0.7 pad_maximum_fusion.2.steps_ref
  28.5 0.2 pad_maximum_fusion
  28.8 0.0 collective-permute-done.3.code1
  28.8 0.0 copy-done.2
  28.8 0.0 copy-done.3
  28.8 0.0 copy-done.4
  28.8 0.0 copy-start
  28.8 0.9 %copy-done = bf16[128,512]{1,0:T(8,128)(2,1)S(1)} copy-done((bf16[128,512]{1,0:T(8,128)(2,1)S(1)}, bf16[128,512]{1,0:T(8,128)(2,1)}, u32[]{:S(2)}) %copy-start) | copy-done | bytes 131096
  29.7 2.8 %shard_map.121 = (bf16[2048,256]{1,0:T(8,128)(2,1)S(1)}, bf16[2048,256]{1,0:T(8,128)(2,1)S(1)}, bf16[256,384]{1,0:T(8,128)(2,1)S(1)}, f32[4,384,512]{2,1,0:T(8,1...) custom-call(s32[1]{0:T(128)} %bitcast.place_ref, bf16[2048,128]{1,0:T(8,128)(2,1)S(1)} %bitcast.14, ...), custom_call_target="tpu_custom_call" | custom-call | tf_op jit(solution)/shard_map/pallas_call | solution.py:433
  32.5 0.9 %collective-permute-done.1.code4 = bf16[128,512]{1,0:T(8,128)(2,1)S(1)} collective-permute-done((bf16[128,512]{1,0:T(8,128)(2,1)S(1)}, bf16[128,512]{1,0:T(8,128)(2,1)S(1)}, u32[]{:S(2)}, u32[]{:S(2)}) %collective-permute-start.1) | collective-permute-done | bytes 131104 | tf_op jit(solution)/shard_map/ppermute | solution.py:44
  33.5 4.5 %collective-permute-done.2.code3 = bf16[128,512]{1,0:T(8,128)(2,1)S(1)} collective-permute-done((bf16[128,512]{1,0:T(8,128)(2,1)S(1)}, bf16[128,512]{1,0:T(8,128)(2,1)S(1)}, u32[]{:S(2)}, u32[]{:S(2)}) %collective-permute-start.2) | collective-permute-done | bytes 131104 | tf_op jit(solution)/shard_map/ppermute | solution.py:44
  38.0 0.0 copy-done.1
  38.0 4.7 %shard_map.122 = (f32[32,8,128]{2,1,0:T(8,128)}, bf16[256,512]{1,0:T(8,128)(2,1)S(1)}, f32[384,512]{1,0:T(8,128)S(1)}, bf16[2048,128]{1,0:T(8,128)(2,1)}) custom-call(s32[1]{0:T(128)} %bitcast.place_ref, bf16[128,512]{1,0:T(8,128)(2,1)S(1)} %collective-permute-done.1.code4, bf16[128,512]{1,0:T(8,128)(2,1)S(1)} %collective-permute-done.2.code3, ...), custom_call_target="tpu_custom_call" | custom-call | tf_op jit(solution)/shard_map/pallas_call | solution.py:463
  42.8 7.4 %all-to-all-start = ((f32[32,8,128]{2,1,0:T(8,128)}), f32[32,8,128]{2,1,0:T(8,128)S(1)}, u32[]{:S(2)}, u32[]{:S(2)}) async-start(f32[32,8,128]{2,1,0:T(8,128)} %get-tuple-element.33), calls=%async_computation | async-start | bytes 262144 | tf_op jit(solution)/shard_map/all_to_all | solution.py:504
  50.2 2.2 %collective-permute-start.4 = (bf16[256,512]{1,0:T(8,128)(2,1)S(1)}, bf16[256,512]{1,0:T(8,128)(2,1)S(1)}, u32[]{:S(2)}, u32[]{:S(2)}) collective-permute-start(bf16[256,512]{1,0:T(8,128)(2,1)S(1)} %get-tuple-element.27), channel_id=1, source_target_pairs={{2,0},{3,1},{4,2},{5,3},{6,4},{7,5},{8,6},{9,7},{10,8},{11,9},{12,... | collective-permute-start | bytes 786440 | tf_op jit(solution)/shard_map/ppermute | solution.py:44
  52.4 5.4 %all-to-all-done.in_ref = f32[32,8,128]{2,1,0:T(8,128)S(1)} async-done(((f32[32,8,128]{2,1,0:T(8,128)}), f32[32,8,128]{2,1,0:T(8,128)S(1)}, u32[]{:S(2)}, u32[]{:S(2)}) %all-to-all-start) | async-done | bytes 131104 | tf_op jit(solution)/shard_map/all_to_all | solution.py:504
  57.8 0.7 shard_map.126
  58.5 6.6 %all-to-all-start.1 = ((f32[16,16,128]{2,1,0:T(8,128)}), f32[16,16,128]{2,1,0:T(8,128)S(1)}, u32[]{:S(2)}, u32[]{:S(2)}) async-start(f32[16,16,128]{2,1,0:T(8,128)} %shard_map.126), calls=%async_computation.1 | async-start | bytes 262144 | tf_op jit(solution)/shard_map/all_to_all | solution.py:510
  65.1 0.6 collective-permute-done.4.back_ref
  65.7 6.1 %collective-permute-start.5 = (bf16[128,512]{1,0:T(8,128)(2,1)S(1)}, bf16[128,512]{1,0:T(8,128)(2,1)S(1)}, u32[]{:S(2)}, u32[]{:S(2)}) collective-permute-start(bf16[128,512]{1,0:T(8,128)(2,1)S(1)} %get-tuple-element.28), channel_id=1, source_target_pairs={{2,0},{3,1},{4,2},{5,3},{6,4},{7,5},{8,6},{9,7},{10,8},{11,9},{12,... | collective-permute-start | bytes 393224 | tf_op jit(solution)/shard_map/ppermute | solution.py:44
  71.8 3.4 %collective-permute-start.6 = (bf16[128,512]{1,0:T(8,128)(2,1)S(1)}, bf16[128,512]{1,0:T(8,128)(2,1)S(1)}, u32[]{:S(2)}, u32[]{:S(2)}) collective-permute-start(bf16[128,512]{1,0:T(8,128)(2,1)S(1)} %get-tuple-element.29), channel_id=1, source_target_pairs={{1,0},{2,1},{3,2},{4,3},{5,4},{6,5},{7,6},{8,7},{9,8},{10,9},{11,1... | collective-permute-start | bytes 393224 | tf_op jit(solution)/shard_map/ppermute | solution.py:44
  75.2 4.8 %collective-permute-done.5.mid_ref = bf16[128,512]{1,0:T(8,128)(2,1)S(1)} collective-permute-done((bf16[128,512]{1,0:T(8,128)(2,1)S(1)}, bf16[128,512]{1,0:T(8,128)(2,1)S(1)}, u32[]{:S(2)}, u32[]{:S(2)}) %collective-permute-start.5) | collective-permute-done | bytes 131104 | tf_op jit(solution)/shard_map/ppermute | solution.py:44
  80.0 1.1 %collective-permute-done.6.near_ref = bf16[128,512]{1,0:T(8,128)(2,1)S(1)} collective-permute-done((bf16[128,512]{1,0:T(8,128)(2,1)S(1)}, bf16[128,512]{1,0:T(8,128)(2,1)S(1)}, u32[]{:S(2)}, u32[]{:S(2)}) %collective-permute-start.6) | collective-permute-done | bytes 131104 | tf_op jit(solution)/shard_map/ppermute | solution.py:44
  81.2 0.8 shard_map.125
  82.0 0.0 all-to-all-done.1.all_ref
  82.0 0.7 shard_map.127
  (5 shorter events, 0.1 us)
Async XLA Ops:
  0.6 28.2 %copy-start.2 = (bf16[128,16,128]{2,1,0:T(8,128)(2,1)S(1)}, bf16[128,16,128]{2,1,0:T(8,128)(2,1)}, u32[]{:S(2)}) copy-start(bf16[128,16,128]{2,1,0:T(8,128)(2,1)} %param.9) | copy-start | bytes 1572868
  0.6 28.2 %copy-start.3 = (bf16[128,16,128]{2,1,0:T(8,128)(2,1)S(1)}, bf16[128,16,128]{2,1,0:T(8,128)(2,1)}, u32[]{:S(2)}) copy-start(bf16[128,16,128]{2,1,0:T(8,128)(2,1)} %param.10) | copy-start | bytes 1572868
  0.7 28.2 %copy-start.4 = (bf16[128,16,128]{2,1,0:T(8,128)(2,1)S(1)}, bf16[128,16,128]{2,1,0:T(8,128)(2,1)}, u32[]{:S(2)}) copy-start(bf16[128,16,128]{2,1,0:T(8,128)(2,1)} %param.11) | copy-start | bytes 1572868
  2.4 35.6 %copy-start.1 = (bf16[128,512]{1,0:T(8,128)(2,1)S(1)}, bf16[128,512]{1,0:T(8,128)(2,1)}, u32[]{:S(2)}) copy-start(bf16[128,512]{1,0:T(8,128)(2,1)} %shard_map.120.code0.code_ref) | copy-start | bytes 393220
  2.4 19.4 %collective-permute-start = (bf16[128,512]{1,0:T(8,128)(2,1)}, bf16[128,512]{1,0:T(8,128)(2,1)S(1)}, u32[]{:S(2)}, u32[]{:S(2)}) collective-permute-start(bf16[128,512]{1,0:T(8,128)(2,1)} %shard_map.120.code0.code_ref), channel_id=1, source_target_pairs={{0,2},{1,3},{2,4},{3,5},{4,6},{5,7},{6,8},{7,9},{8,10},{9,11},{10,... | collective-permute-start | bytes 393224 | tf_op jit(solution)/shard_map/ppermute | solution.py:44
  8.3 20.5 %collective-permute-start.3 = (bf16[128,512]{1,0:T(8,128)(2,1)}, bf16[128,512]{1,0:T(8,128)(2,1)S(1)}, u32[]{:S(2)}, u32[]{:S(2)}) collective-permute-start(bf16[128,512]{1,0:T(8,128)(2,1)} %shard_map.120.code0.code_ref), channel_id=1, source_target_pairs={{0,1},{1,2},{2,3},{3,4},{4,5},{5,6},{6,7},{7,8},{8,9},{9,10},{10,1... | collective-permute-start | bytes 393224 | tf_op jit(solution)/shard_map/ppermute | solution.py:44
  21.8 11.7 %collective-permute-start.1 = (bf16[128,512]{1,0:T(8,128)(2,1)S(1)}, bf16[128,512]{1,0:T(8,128)(2,1)S(1)}, u32[]{:S(2)}, u32[]{:S(2)}) collective-permute-start(bf16[128,512]{1,0:T(8,128)(2,1)S(1)} %collective-permute-done.code2), channel_id=1, source_target_pairs={{0,2},{1,3},{2,4},{3,5},{4,6},{5,7},{6,8},{7,9},{8,10},{9,11},{10,... | collective-permute-start | bytes 393224 | tf_op jit(solution)/shard_map/ppermute | solution.py:44
  23.7 14.3 %collective-permute-start.2 = (bf16[128,512]{1,0:T(8,128)(2,1)S(1)}, bf16[128,512]{1,0:T(8,128)(2,1)S(1)}, u32[]{:S(2)}, u32[]{:S(2)}) collective-permute-start(bf16[128,512]{1,0:T(8,128)(2,1)S(1)} %collective-permute-done.code2), channel_id=1, source_target_pairs={{0,1},{1,2},{2,3},{3,4},{4,5},{5,6},{6,7},{7,8},{8,9},{9,10},{10,1... | collective-permute-start | bytes 393224 | tf_op jit(solution)/shard_map/ppermute | solution.py:44
  28.8 0.9 %copy-start = (bf16[128,512]{1,0:T(8,128)(2,1)S(1)}, bf16[128,512]{1,0:T(8,128)(2,1)}, u32[]{:S(2)}) copy-start(bf16[128,512]{1,0:T(8,128)(2,1)} %shard_map.120.code0.code_ref) | copy-start | bytes 393220
  42.8 15.0 %all-to-all-start = ((f32[32,8,128]{2,1,0:T(8,128)}), f32[32,8,128]{2,1,0:T(8,128)S(1)}, u32[]{:S(2)}, u32[]{:S(2)}) async-start(f32[32,8,128]{2,1,0:T(8,128)} %get-tuple-element.33), calls=%async_computation | async-start | bytes 262144 | tf_op jit(solution)/shard_map/all_to_all | solution.py:504
  50.2 15.5 %collective-permute-start.4 = (bf16[256,512]{1,0:T(8,128)(2,1)S(1)}, bf16[256,512]{1,0:T(8,128)(2,1)S(1)}, u32[]{:S(2)}, u32[]{:S(2)}) collective-permute-start(bf16[256,512]{1,0:T(8,128)(2,1)S(1)} %get-tuple-element.27), channel_id=1, source_target_pairs={{2,0},{3,1},{4,2},{5,3},{6,4},{7,5},{8,6},{9,7},{10,8},{11,9},{12,... | collective-permute-start | bytes 786440 | tf_op jit(solution)/shard_map/ppermute | solution.py:44
  58.5 23.5 %all-to-all-start.1 = ((f32[16,16,128]{2,1,0:T(8,128)}), f32[16,16,128]{2,1,0:T(8,128)S(1)}, u32[]{:S(2)}, u32[]{:S(2)}) async-start(f32[16,16,128]{2,1,0:T(8,128)} %shard_map.126), calls=%async_computation.1 | async-start | bytes 262144 | tf_op jit(solution)/shard_map/all_to_all | solution.py:510
  65.7 14.3 %collective-permute-start.5 = (bf16[128,512]{1,0:T(8,128)(2,1)S(1)}, bf16[128,512]{1,0:T(8,128)(2,1)S(1)}, u32[]{:S(2)}, u32[]{:S(2)}) collective-permute-start(bf16[128,512]{1,0:T(8,128)(2,1)S(1)} %get-tuple-element.28), channel_id=1, source_target_pairs={{2,0},{3,1},{4,2},{5,3},{6,4},{7,5},{8,6},{9,7},{10,8},{11,9},{12,... | collective-permute-start | bytes 393224 | tf_op jit(solution)/shard_map/ppermute | solution.py:44
  71.8 9.3 %collective-permute-start.6 = (bf16[128,512]{1,0:T(8,128)(2,1)S(1)}, bf16[128,512]{1,0:T(8,128)(2,1)S(1)}, u32[]{:S(2)}, u32[]{:S(2)}) collective-permute-start(bf16[128,512]{1,0:T(8,128)(2,1)S(1)} %get-tuple-element.29), channel_id=1, source_target_pairs={{1,0},{2,1},{3,2},{4,3},{5,4},{6,5},{7,6},{8,7},{9,8},{10,9},{11,1... | collective-permute-start | bytes 393224 | tf_op jit(solution)/shard_map/ppermute | solution.py:44

commit v5 on v4

--- a/solution.py
+++ b/solution.py
@@ -335,7 +335,8 @@
         raw_ref[:, head * terms : (head + 1) * terms, :] = jnp.broadcast_to(total[None], shape)
 
 
-def clip_kernel(first_ref, all_ref, quant_out):
+def clip_kernel(first_ref, all_ref, quant_out, mark_out):
+    mark_out[...] = first_ref[...]
     total = jnp.sum(all_ref[...], axis=0)
     squares = jnp.sum(total * total, keepdims=True)
     mine = jnp.where(first_ref[...] > 0.0, total[: 4 * KV_HEADS], total[4 * KV_HEADS :])
@@ -346,8 +347,7 @@
     sum_ref[...] = parts[2 * ROWS :, :] + mid_ref[...].astype(F32)
 
 
-def finish_kernel(first_ref, sum_ref, near_ref, code_ref, key_out, value_out, first_out, rows_ref):
-    first_out[...] = first_ref[...]
+def finish_kernel(mark_ref, sum_ref, near_ref, code_ref, key_out, value_out, rows_ref):
     total = sum_ref[...] + near_ref[...].astype(F32)
     code = code_ref[...].astype(F32)
     total = jnp.where((code > 0.0) & (code < 15.0), total, 0.0)
@@ -509,15 +509,15 @@
     near = shift(near, -1)
     raw = lax.all_to_all(raw, "z", 0, 0)
     first = jnp.where(lax.axis_index("head") == 0, jnp.ones((4 * KV_HEADS, HEAD), F32), 0.0)
+    quant, mark = call(clip_kernel, [((4 * KV_HEADS, HEAD), F32)] * 2, inputs="vv")(first, raw)
     (own_sum,) = call(add_kernel, [(pack, F32)], inputs="vv", flops=ADD_FLOPS)(parts, mid)
-    key_grad, value_grad, first = call(
+    key_grad, value_grad = call(
         finish_kernel,
-        [(flat_codes, BF16)] * 2 + [((4 * KV_HEADS, HEAD), F32)],
+        [(flat_codes, BF16)] * 2,
         scratch=[((2,) + flat_codes, F32)],
         inputs="vvvv",
         flops=FINISH_FLOPS,
-    )(first, own_sum, near, own)
-    (quant,) = call(clip_kernel, [((4 * KV_HEADS, HEAD), F32)], inputs="vv")(first, raw)
+    )(mark, own_sum, near, own)
     return (
         query_grad.reshape(ROWS, QUERY_HEADS, HEAD),
         key_grad.reshape(ROWS, KV_HEADS, HEAD),

time: 83.4 us -> 82.6 us (level)
  no operation moved by 1% of the time
where the time goes in v5:
time: 82.6 us; the launch traced here: 82 us
  starting transfers between devices  41.2 us (50%)
  waiting for transfers between devices  25.2 us (31%)
  Pallas kernels  11.5 us (14%)
  other arithmetic  2.3 us (3%)
  local copies, waits for them, and re-layouts  0.93 us (1%)
  between operations  0.88 us (1%)
    ppermute x7, starting transfers between devices, shift(): return lax.ppermute(value, TOK, pairs)  27.1 us
    ppermute x7, waiting for transfers between devices, shift(): return lax.ppermute(value, TOK, pairs)  19.8 us
    all_to_all x1, starting transfers between devices, body(): raw = lax.all_to_all(raw, FLAT, 0, 0)  7.44 us
    all_to_all x1, starting transfers between devices, body(): raw = lax.all_to_all(raw, 'z', 0, 0)  6.63 us
    all_to_all x1, waiting for transfers between devices, body(): raw = lax.all_to_all(raw, FLAT, 0, 0)  5.37 us
    pallas_call x1, Pallas kernels, body(): call(far_kernel, [((axis_count(FLAT), 4 * KV_HEADS, HEAD), F32), ((2 * RO...  4.75 us
    pallas_call x1, Pallas kernels, body(): call(near_kernel, [(wide, BF16), (wide, BF16), ((WIDE, NEAR_ROWS), BF16),...  2.8 us
    pallas_call x1, Pallas kernels, body(): call(pack_kernel, [(pack, BF16)], [((2,) + flat_codes, jnp.int32)], input...  1.72 us
  transfers between devices with their start and end apart: 9, of which 7 were waited for; matrix products, arithmetic and copies ran while one was open for 3% of the time, Pallas kernels for 5%

profile of v5, /device:TPU:1, one launch (start us, length us, event | category | flops | bytes accessed | tf_op | source)
XLA Modules:
  0.0 82.0 jit_solution(7996456713342057551)
XLA Ops:
  0.6 0.0 copy-start.2
  0.6 0.0 copy-start.3
  0.7 0.0 copy-start.4
  0.7 1.7 %shard_map.120.code0.code_ref = bf16[128,512]{1,0:T(8,128)(2,1)} custom-call(s32[256,128]{1,0:T(8,128)} %bitcast.17, s32[256,128]{1,0:T(8,128)} %bitcast.18), custom_call_target="tpu_custom_call" | custom-call | tf_op jit(solution)/shard_map/pallas_call | solution.py:417
  2.4 0.0 copy-start.1
  2.4 5.9 %collective-permute-start = (bf16[128,512]{1,0:T(8,128)(2,1)}, bf16[128,512]{1,0:T(8,128)(2,1)S(1)}, u32[]{:S(2)}, u32[]{:S(2)}) collective-permute-start(bf16[128,512]{1,0:T(8,128)(2,1)} %shard_map.120.code0.code_ref), channel_id=1, source_target_pairs={{0,2},{1,3},{2,4},{3,5},{4,6},{5,7},{6,8},{7,9},{8,10},{9,11},{10,... | collective-permute-start | bytes 393224 | tf_op jit(solution)/shard_map/ppermute | solution.py:44
  8.3 3.5 %collective-permute-start.3 = (bf16[128,512]{1,0:T(8,128)(2,1)}, bf16[128,512]{1,0:T(8,128)(2,1)S(1)}, u32[]{:S(2)}, u32[]{:S(2)}) collective-permute-start(bf16[128,512]{1,0:T(8,128)(2,1)} %shard_map.120.code0.code_ref), channel_id=1, source_target_pairs={{0,1},{1,2},{2,3},{3,4},{4,5},{5,6},{6,7},{7,8},{8,9},{9,10},{10,1... | collective-permute-start | bytes 393224 | tf_op jit(solution)/shard_map/ppermute | solution.py:44
  11.9 1.2 %fusion = (f32[640,64]{1,0:T(8,128)S(1)}, f32[640,64]{1,0:T(8,128)S(1)}, f32[640,64]{1,0:T(8,128)S(1)}) fusion(f32[64]{0:T(128)S(1)} %multiply_power_fusion, f32[640]{0:T(1024)S(1)} %add_convert_fusion), kind=kLoop, calls=%fused_computation.4 | loop fusion | flops 81920 | bytes 494336 | tf_op jit(solution)/shard_map/neg | solution.py:395
  13.1 0.1 fusion.4.had_ref
  13.2 8.6 %collective-permute-done.code2 = bf16[128,512]{1,0:T(8,128)(2,1)S(1)} collective-permute-done((bf16[128,512]{1,0:T(8,128)(2,1)}, bf16[128,512]{1,0:T(8,128)(2,1)S(1)}, u32[]{:S(2)}, u32[]{:S(2)}) %collective-permute-start) | collective-permute-done | bytes 131104 | tf_op jit(solution)/shard_map/ppermute | solution.py:44
  21.8 1.9 %collective-permute-start.1 = (bf16[128,512]{1,0:T(8,128)(2,1)S(1)}, bf16[128,512]{1,0:T(8,128)(2,1)S(1)}, u32[]{:S(2)}, u32[]{:S(2)}) collective-permute-start(bf16[128,512]{1,0:T(8,128)(2,1)S(1)} %collective-permute-done.code2), channel_id=1, source_target_pairs={{0,2},{1,3},{2,4},{3,5},{4,6},{5,7},{6,8},{7,9},{8,10},{9,11},{10,... | collective-permute-start | bytes 393224 | tf_op jit(solution)/shard_map/ppermute | solution.py:44
  23.7 4.1 %collective-permute-start.2 = (bf16[128,512]{1,0:T(8,128)(2,1)S(1)}, bf16[128,512]{1,0:T(8,128)(2,1)S(1)}, u32[]{:S(2)}, u32[]{:S(2)}) collective-permute-start(bf16[128,512]{1,0:T(8,128)(2,1)S(1)} %collective-permute-done.code2), channel_id=1, source_target_pairs={{0,1},{1,2},{2,3},{3,4},{4,5},{5,6},{6,7},{7,8},{8,9},{9,10},{10,1... | collective-permute-start | bytes 393224 | tf_op jit(solution)/shard_map/ppermute | solution.py:44
  27.8 0.7 pad_maximum_fusion.2.steps_ref
  28.5 0.2 pad_maximum_fusion
  28.8 0.0 collective-permute-done.3.code1
  28.8 0.0 copy-done.2
  28.8 0.0 copy-done.3
  28.8 0.0 copy-done.4
  28.8 0.0 copy-start
  28.8 0.9 %copy-done = bf16[128,512]{1,0:T(8,128)(2,1)S(1)} copy-done((bf16[128,512]{1,0:T(8,128)(2,1)S(1)}, bf16[128,512]{1,0:T(8,128)(2,1)}, u32[]{:S(2)}) %copy-start) | copy-done | bytes 131096
  29.7 2.8 %shard_map.121 = (bf16[2048,256]{1,0:T(8,128)(2,1)S(1)}, bf16[2048,256]{1,0:T(8,128)(2,1)S(1)}, bf16[256,384]{1,0:T(8,128)(2,1)S(1)}, f32[4,384,512]{2,1,0:T(8,1...) custom-call(s32[1]{0:T(128)} %bitcast.place_ref, bf16[2048,128]{1,0:T(8,128)(2,1)S(1)} %bitcast.14, ...), custom_call_target="tpu_custom_call" | custom-call | tf_op jit(solution)/shard_map/pallas_call | solution.py:433
  32.5 0.9 %collective-permute-done.1.code4 = bf16[128,512]{1,0:T(8,128)(2,1)S(1)} collective-permute-done((bf16[128,512]{1,0:T(8,128)(2,1)S(1)}, bf16[128,512]{1,0:T(8,128)(2,1)S(1)}, u32[]{:S(2)}, u32[]{:S(2)}) %collective-permute-start.1) | collective-permute-done | bytes 131104 | tf_op jit(solution)/shard_map/ppermute | solution.py:44
  33.5 4.5 %collective-permute-done.2.code3 = bf16[128,512]{1,0:T(8,128)(2,1)S(1)} collective-permute-done((bf16[128,512]{1,0:T(8,128)(2,1)S(1)}, bf16[128,512]{1,0:T(8,128)(2,1)S(1)}, u32[]{:S(2)}, u32[]{:S(2)}) %collective-permute-start.2) | collective-permute-done | bytes 131104 | tf_op jit(solution)/shard_map/ppermute | solution.py:44
  38.0 0.0 copy-done.1
  38.0 4.8 %shard_map.122 = (f32[32,8,128]{2,1,0:T(8,128)}, bf16[256,512]{1,0:T(8,128)(2,1)S(1)}, f32[384,512]{1,0:T(8,128)S(1)}, bf16[2048,128]{1,0:T(8,128)(2,1)}) custom-call(s32[1]{0:T(128)} %bitcast.place_ref, bf16[128,512]{1,0:T(8,128)(2,1)S(1)} %collective-permute-done.1.code4, bf16[128,512]{1,0:T(8,128)(2,1)S(1)} %collective-permute-done.2.code3, ...), custom_call_target="tpu_custom_call" | custom-call | tf_op jit(solution)/shard_map/pallas_call | solution.py:463
  42.8 7.4 %all-to-all-start = ((f32[32,8,128]{2,1,0:T(8,128)}), f32[32,8,128]{2,1,0:T(8,128)S(1)}, u32[]{:S(2)}, u32[]{:S(2)}) async-start(f32[32,8,128]{2,1,0:T(8,128)} %get-tuple-element.27), calls=%async_computation | async-start | bytes 262144 | tf_op jit(solution)/shard_map/all_to_all | solution.py:504
  50.2 2.2 %collective-permute-start.4 = (bf16[256,512]{1,0:T(8,128)(2,1)S(1)}, bf16[256,512]{1,0:T(8,128)(2,1)S(1)}, u32[]{:S(2)}, u32[]{:S(2)}) collective-permute-start(bf16[256,512]{1,0:T(8,128)(2,1)S(1)} %get-tuple-element.30), channel_id=1, source_target_pairs={{2,0},{3,1},{4,2},{5,3},{6,4},{7,5},{8,6},{9,7},{10,8},{11,9},{12,... | collective-permute-start | bytes 786440 | tf_op jit(solution)/shard_map/ppermute | solution.py:44
  52.4 5.4 %all-to-all-done.in_ref = f32[32,8,128]{2,1,0:T(8,128)S(1)} async-done(((f32[32,8,128]{2,1,0:T(8,128)}), f32[32,8,128]{2,1,0:T(8,128)S(1)}, u32[]{:S(2)}, u32[]{:S(2)}) %all-to-all-start) | async-done | bytes 131104 | tf_op jit(solution)/shard_map/all_to_all | solution.py:504
  57.8 0.7 shard_map.123
  58.5 6.6 %all-to-all-start.1 = ((f32[16,16,128]{2,1,0:T(8,128)}), f32[16,16,128]{2,1,0:T(8,128)S(1)}, u32[]{:S(2)}, u32[]{:S(2)}) async-start(f32[16,16,128]{2,1,0:T(8,128)} %shard_map.123), calls=%async_computation.1 | async-start | bytes 262144 | tf_op jit(solution)/shard_map/all_to_all | solution.py:510
  65.1 0.6 collective-permute-done.4.back_ref
  65.7 6.1 %collective-permute-start.5 = (bf16[128,512]{1,0:T(8,128)(2,1)S(1)}, bf16[128,512]{1,0:T(8,128)(2,1)S(1)}, u32[]{:S(2)}, u32[]{:S(2)}) collective-permute-start(bf16[128,512]{1,0:T(8,128)(2,1)S(1)} %get-tuple-element.31), channel_id=1, source_target_pairs={{2,0},{3,1},{4,2},{5,3},{6,4},{7,5},{8,6},{9,7},{10,8},{11,9},{12,... | collective-permute-start | bytes 393224 | tf_op jit(solution)/shard_map/ppermute | solution.py:44
  71.8 3.4 %collective-permute-start.6 = (bf16[128,512]{1,0:T(8,128)(2,1)S(1)}, bf16[128,512]{1,0:T(8,128)(2,1)S(1)}, u32[]{:S(2)}, u32[]{:S(2)}) collective-permute-start(bf16[128,512]{1,0:T(8,128)(2,1)S(1)} %get-tuple-element.32), channel_id=1, source_target_pairs={{1,0},{2,1},{3,2},{4,3},{5,4},{6,5},{7,6},{8,7},{9,8},{10,9},{11,1... | collective-permute-start | bytes 393224 | tf_op jit(solution)/shard_map/ppermute | solution.py:44
  75.2 4.8 %collective-permute-done.5.mid_ref = bf16[128,512]{1,0:T(8,128)(2,1)S(1)} collective-permute-done((bf16[128,512]{1,0:T(8,128)(2,1)S(1)}, bf16[128,512]{1,0:T(8,128)(2,1)S(1)}, u32[]{:S(2)}, u32[]{:S(2)}) %collective-permute-start.5) | collective-permute-done | bytes 131104 | tf_op jit(solution)/shard_map/ppermute | solution.py:44
  80.0 0.0 all-to-all-done.1.all_ref
  80.1 0.7 shard_map.124
  80.8 0.4 collective-permute-done.6.near_ref
  81.2 0.8 shard_map.127
  (5 shorter events, 0.1 us)
Async XLA Ops:
  0.6 28.2 %copy-start.2 = (bf16[128,16,128]{2,1,0:T(8,128)(2,1)S(1)}, bf16[128,16,128]{2,1,0:T(8,128)(2,1)}, u32[]{:S(2)}) copy-start(bf16[128,16,128]{2,1,0:T(8,128)(2,1)} %param.9) | copy-start | bytes 1572868
  0.6 28.2 %copy-start.3 = (bf16[128,16,128]{2,1,0:T(8,128)(2,1)S(1)}, bf16[128,16,128]{2,1,0:T(8,128)(2,1)}, u32[]{:S(2)}) copy-start(bf16[128,16,128]{2,1,0:T(8,128)(2,1)} %param.10) | copy-start | bytes 1572868
  0.7 28.2 %copy-start.4 = (bf16[128,16,128]{2,1,0:T(8,128)(2,1)S(1)}, bf16[128,16,128]{2,1,0:T(8,128)(2,1)}, u32[]{:S(2)}) copy-start(bf16[128,16,128]{2,1,0:T(8,128)(2,1)} %param.11) | copy-start | bytes 1572868
  2.4 35.6 %copy-start.1 = (bf16[128,512]{1,0:T(8,128)(2,1)S(1)}, bf16[128,512]{1,0:T(8,128)(2,1)}, u32[]{:S(2)}) copy-start(bf16[128,512]{1,0:T(8,128)(2,1)} %shard_map.120.code0.code_ref) | copy-start | bytes 393220
  2.4 19.4 %collective-permute-start = (bf16[128,512]{1,0:T(8,128)(2,1)}, bf16[128,512]{1,0:T(8,128)(2,1)S(1)}, u32[]{:S(2)}, u32[]{:S(2)}) collective-permute-start(bf16[128,512]{1,0:T(8,128)(2,1)} %shard_map.120.code0.code_ref), channel_id=1, source_target_pairs={{0,2},{1,3},{2,4},{3,5},{4,6},{5,7},{6,8},{7,9},{8,10},{9,11},{10,... | collective-permute-start | bytes 393224 | tf_op jit(solution)/shard_map/ppermute | solution.py:44
  8.3 20.5 %collective-permute-start.3 = (bf16[128,512]{1,0:T(8,128)(2,1)}, bf16[128,512]{1,0:T(8,128)(2,1)S(1)}, u32[]{:S(2)}, u32[]{:S(2)}) collective-permute-start(bf16[128,512]{1,0:T(8,128)(2,1)} %shard_map.120.code0.code_ref), channel_id=1, source_target_pairs={{0,1},{1,2},{2,3},{3,4},{4,5},{5,6},{6,7},{7,8},{8,9},{9,10},{10,1... | collective-permute-start | bytes 393224 | tf_op jit(solution)/shard_map/ppermute | solution.py:44
  21.8 11.7 %collective-permute-start.1 = (bf16[128,512]{1,0:T(8,128)(2,1)S(1)}, bf16[128,512]{1,0:T(8,128)(2,1)S(1)}, u32[]{:S(2)}, u32[]{:S(2)}) collective-permute-start(bf16[128,512]{1,0:T(8,128)(2,1)S(1)} %collective-permute-done.code2), channel_id=1, source_target_pairs={{0,2},{1,3},{2,4},{3,5},{4,6},{5,7},{6,8},{7,9},{8,10},{9,11},{10,... | collective-permute-start | bytes 393224 | tf_op jit(solution)/shard_map/ppermute | solution.py:44
  23.7 14.3 %collective-permute-start.2 = (bf16[128,512]{1,0:T(8,128)(2,1)S(1)}, bf16[128,512]{1,0:T(8,128)(2,1)S(1)}, u32[]{:S(2)}, u32[]{:S(2)}) collective-permute-start(bf16[128,512]{1,0:T(8,128)(2,1)S(1)} %collective-permute-done.code2), channel_id=1, source_target_pairs={{0,1},{1,2},{2,3},{3,4},{4,5},{5,6},{6,7},{7,8},{8,9},{9,10},{10,1... | collective-permute-start | bytes 393224 | tf_op jit(solution)/shard_map/ppermute | solution.py:44
  28.8 0.9 %copy-start = (bf16[128,512]{1,0:T(8,128)(2,1)S(1)}, bf16[128,512]{1,0:T(8,128)(2,1)}, u32[]{:S(2)}) copy-start(bf16[128,512]{1,0:T(8,128)(2,1)} %shard_map.120.code0.code_ref) | copy-start | bytes 393220
  42.8 15.0 %all-to-all-start = ((f32[32,8,128]{2,1,0:T(8,128)}), f32[32,8,128]{2,1,0:T(8,128)S(1)}, u32[]{:S(2)}, u32[]{:S(2)}) async-start(f32[32,8,128]{2,1,0:T(8,128)} %get-tuple-element.27), calls=%async_computation | async-start | bytes 262144 | tf_op jit(solution)/shard_map/all_to_all | solution.py:504
  50.2 15.5 %collective-permute-start.4 = (bf16[256,512]{1,0:T(8,128)(2,1)S(1)}, bf16[256,512]{1,0:T(8,128)(2,1)S(1)}, u32[]{:S(2)}, u32[]{:S(2)}) collective-permute-start(bf16[256,512]{1,0:T(8,128)(2,1)S(1)} %get-tuple-element.30), channel_id=1, source_target_pairs={{2,0},{3,1},{4,2},{5,3},{6,4},{7,5},{8,6},{9,7},{10,8},{11,9},{12,... | collective-permute-start | bytes 786440 | tf_op jit(solution)/shard_map/ppermute | solution.py:44
  58.5 21.6 %all-to-all-start.1 = ((f32[16,16,128]{2,1,0:T(8,128)}), f32[16,16,128]{2,1,0:T(8,128)S(1)}, u32[]{:S(2)}, u32[]{:S(2)}) async-start(f32[16,16,128]{2,1,0:T(8,128)} %shard_map.123), calls=%async_computation.1 | async-start | bytes 262144 | tf_op jit(solution)/shard_map/all_to_all | solution.py:510
  65.7 14.3 %collective-permute-start.5 = (bf16[128,512]{1,0:T(8,128)(2,1)S(1)}, bf16[128,512]{1,0:T(8,128)(2,1)S(1)}, u32[]{:S(2)}, u32[]{:S(2)}) collective-permute-start(bf16[128,512]{1,0:T(8,128)(2,1)S(1)} %get-tuple-element.31), channel_id=1, source_target_pairs={{2,0},{3,1},{4,2},{5,3},{6,4},{7,5},{8,6},{9,7},{10,8},{11,9},{12,... | collective-permute-start | bytes 393224 | tf_op jit(solution)/shard_map/ppermute | solution.py:44
  71.8 9.3 %collective-permute-start.6 = (bf16[128,512]{1,0:T(8,128)(2,1)S(1)}, bf16[128,512]{1,0:T(8,128)(2,1)S(1)}, u32[]{:S(2)}, u32[]{:S(2)}) collective-permute-start(bf16[128,512]{1,0:T(8,128)(2,1)S(1)} %get-tuple-element.32), channel_id=1, source_target_pairs={{1,0},{2,1},{3,2},{4,3},{5,4},{6,5},{7,6},{8,7},{9,8},{10,9},{11,1... | collective-permute-start | bytes 393224 | tf_op jit(solution)/shard_map/ppermute | solution.py:44

commit v6 on v5

--- a/solution.py
+++ b/solution.py
@@ -251,9 +251,6 @@
         for chunk in range(CHUNKS):
             scores[chunk] = jnp.where(row < missing, FLOOR, scores[chunk])
 
-    key_acc[...] = jnp.zeros_like(key_acc)
-    value_acc[...] = jnp.zeros_like(value_acc)
-    grads[...] = jnp.zeros_like(grads)
     low_lane = (
         lax.broadcasted_iota(jnp.int32, (HEAD, COLS), 1) % QUERY_HEADS < QUERY_HEADS // KV_HEADS
     )
@@ -276,8 +273,20 @@
         lows[chunk, FAR_ROWS:last, :] = near.astype(BF16)
         grads[chunk, first:FAR_ROWS, :] = (far * upstream).astype(BF16)
         grads[chunk, FAR_ROWS:last, :] = (near * near_u[chunk, :count, :]).astype(BF16)
-        value_acc[first:last, :] += matmul(lows[chunk, first:last, :], wide_g[picked, :])
-        key_acc[first:last, :] += matmul(grads[chunk, first:last, :], wide_q[picked, :])
+        if first > 0:
+            grads[chunk, :first, :] = jnp.zeros((first, COLS), BF16)
+        if last < SPAN:
+            grads[chunk, last:, :] = jnp.zeros((SPAN - last, COLS), BF16)
+        value_part = matmul(lows[chunk, first:last, :], wide_g[picked, :])
+        key_part = matmul(grads[chunk, first:last, :], wide_q[picked, :])
+        if chunk == 0:
+            value_acc[:last, :] = value_part
+            key_acc[:last, :] = key_part
+            value_acc[last:, :] = jnp.zeros((SPAN - last, WIDE), F32)
+            key_acc[last:, :] = jnp.zeros((SPAN - last, WIDE), F32)
+        else:
+            value_acc[first:last, :] += value_part
+            key_acc[first:last, :] += key_part
         both = matmul(keys_t[...], grads[chunk, :FAR_ROWS, :])
         both = both + matmul(near_t[...], grads[chunk, FAR_ROWS:, :])
         query_grad = jnp.where(low_lane, both[:HEAD], both[HEAD:]) * SCALE
@@ -291,6 +300,7 @@
     code_refs = (code4, code3, code2, code1, code0)
     outs = [back_out.at[:ROWS], back_out.at[ROWS:]]
     outs = outs + [parts.at[block * ROWS : (block + 1) * ROWS] for block in range(3)]
+    terms = []
     for head in range(KV_HEADS):
         cols = head_cols(head)
         value_cols = head_cols(KV_HEADS + head)
@@ -312,10 +322,9 @@
             code = code_refs[block][:, value_cols].astype(F32)
             sums[2] = sums[2] + jnp.sum(part * code, axis=0, keepdims=True)
             sums[3] = sums[3] - jnp.sum(part, axis=0, keepdims=True)
-        for term in range(4):
-            row = term * KV_HEADS + head
-            for copy in range(raw_ref.shape[0]):
-                raw_ref[copy, row : row + 1, :] = sums[term]
+        terms.append(sums)
+    tile = jnp.concatenate([terms[i % KV_HEADS][i // KV_HEADS] for i in range(4 * KV_HEADS)], axis=0)
+    raw_ref[...] = jnp.broadcast_to(tile[None], raw_ref.shape)
     for copy in copies:
         copy.wait()
 

time: 82.6 us -> 82.6 us (level)
  no operation moved by 1% of the time
where the time goes in v6:
time: 82.6 us; the launch traced here: 81.9 us
  starting transfers between devices  41.2 us (50%)
  waiting for transfers between devices  25.2 us (31%)
  Pallas kernels  11.5 us (14%)
  other arithmetic  2.3 us (3%)
  local copies, waits for them, and re-layouts  0.93 us (1%)
  between operations  0.88 us (1%)
    ppermute x7, starting transfers between devices, shift(): return lax.ppermute(value, TOK, pairs)  27.1 us
    ppermute x7, waiting for transfers between devices, shift(): return lax.ppermute(value, TOK, pairs)  19.8 us
    all_to_all x1, starting transfers between devices, body(): raw = lax.all_to_all(raw, FLAT, 0, 0)  7.44 us
    all_to_all x1, starting transfers between devices, body(): raw = lax.all_to_all(raw, 'z', 0, 0)  6.63 us
    all_to_all x1, waiting for transfers between devices, body(): raw = lax.all_to_all(raw, FLAT, 0, 0)  5.37 us
    pallas_call x1, Pallas kernels, body(): call(far_kernel, [((axis_count(FLAT), 4 * KV_HEADS, HEAD), F32), ((2 * RO...  4.74 us
    pallas_call x1, Pallas kernels, body(): call(near_kernel, [(wide, BF16), (wide, BF16), ((WIDE, NEAR_ROWS), BF16),...  2.8 us
    pallas_call x1, Pallas kernels, body(): call(pack_kernel, [(pack, BF16)], [((2,) + flat_codes, jnp.int32)], input...  1.72 us
  transfers between devices with their start and end apart: 9, of which 7 were waited for; matrix products, arithmetic and copies ran while one was open for 3% of the time, Pallas kernels for 5%

profile of v6, /device:TPU:1, one launch (start us, length us, event | category | flops | bytes accessed | tf_op | source)
XLA Modules:
  0.0 81.9 jit_solution(7652565588653317640)
XLA Ops:
  0.6 0.0 copy-start.2
  0.6 0.0 copy-start.3
  0.7 0.0 copy-start.4
  0.7 1.7 %shard_map.120.code0.code_ref = bf16[128,512]{1,0:T(8,128)(2,1)} custom-call(s32[256,128]{1,0:T(8,128)} %bitcast.17, s32[256,128]{1,0:T(8,128)} %bitcast.18), custom_call_target="tpu_custom_call" | custom-call | tf_op jit(solution)/shard_map/pallas_call | solution.py:426
  2.4 0.0 copy-start.1
  2.4 5.9 %collective-permute-start = (bf16[128,512]{1,0:T(8,128)(2,1)}, bf16[128,512]{1,0:T(8,128)(2,1)S(1)}, u32[]{:S(2)}, u32[]{:S(2)}) collective-permute-start(bf16[128,512]{1,0:T(8,128)(2,1)} %shard_map.120.code0.code_ref), channel_id=1, source_target_pairs={{0,2},{1,3},{2,4},{3,5},{4,6},{5,7},{6,8},{7,9},{8,10},{9,11},{10,... | collective-permute-start | bytes 393224 | tf_op jit(solution)/shard_map/ppermute | solution.py:44
  8.3 3.5 %collective-permute-start.3 = (bf16[128,512]{1,0:T(8,128)(2,1)}, bf16[128,512]{1,0:T(8,128)(2,1)S(1)}, u32[]{:S(2)}, u32[]{:S(2)}) collective-permute-start(bf16[128,512]{1,0:T(8,128)(2,1)} %shard_map.120.code0.code_ref), channel_id=1, source_target_pairs={{0,1},{1,2},{2,3},{3,4},{4,5},{5,6},{6,7},{7,8},{8,9},{9,10},{10,1... | collective-permute-start | bytes 393224 | tf_op jit(solution)/shard_map/ppermute | solution.py:44
  11.9 1.2 %fusion = (f32[640,64]{1,0:T(8,128)S(1)}, f32[640,64]{1,0:T(8,128)S(1)}, f32[640,64]{1,0:T(8,128)S(1)}) fusion(f32[64]{0:T(128)S(1)} %multiply_power_fusion, f32[640]{0:T(1024)S(1)} %add_convert_fusion), kind=kLoop, calls=%fused_computation.4 | loop fusion | flops 81920 | bytes 494336 | tf_op jit(solution)/shard_map/neg | solution.py:404
  13.1 0.1 fusion.4.had_ref
  13.2 8.6 %collective-permute-done.code2 = bf16[128,512]{1,0:T(8,128)(2,1)S(1)} collective-permute-done((bf16[128,512]{1,0:T(8,128)(2,1)}, bf16[128,512]{1,0:T(8,128)(2,1)S(1)}, u32[]{:S(2)}, u32[]{:S(2)}) %collective-permute-start) | collective-permute-done | bytes 131104 | tf_op jit(solution)/shard_map/ppermute | solution.py:44
  21.8 1.9 %collective-permute-start.1 = (bf16[128,512]{1,0:T(8,128)(2,1)S(1)}, bf16[128,512]{1,0:T(8,128)(2,1)S(1)}, u32[]{:S(2)}, u32[]{:S(2)}) collective-permute-start(bf16[128,512]{1,0:T(8,128)(2,1)S(1)} %collective-permute-done.code2), channel_id=1, source_target_pairs={{0,2},{1,3},{2,4},{3,5},{4,6},{5,7},{6,8},{7,9},{8,10},{9,11},{10,... | collective-permute-start | bytes 393224 | tf_op jit(solution)/shard_map/ppermute | solution.py:44
  23.7 4.1 %collective-permute-start.2 = (bf16[128,512]{1,0:T(8,128)(2,1)S(1)}, bf16[128,512]{1,0:T(8,128)(2,1)S(1)}, u32[]{:S(2)}, u32[]{:S(2)}) collective-permute-start(bf16[128,512]{1,0:T(8,128)(2,1)S(1)} %collective-permute-done.code2), channel_id=1, source_target_pairs={{0,1},{1,2},{2,3},{3,4},{4,5},{5,6},{6,7},{7,8},{8,9},{9,10},{10,1... | collective-permute-start | bytes 393224 | tf_op jit(solution)/shard_map/ppermute | solution.py:44
  27.8 0.7 pad_maximum_fusion.2.steps_ref
  28.5 0.2 pad_maximum_fusion
  28.8 0.0 collective-permute-done.3.code1
  28.8 0.0 copy-done.2
  28.8 0.0 copy-done.3
  28.8 0.0 copy-done.4
  28.8 0.0 copy-start
  28.8 0.9 %copy-done = bf16[128,512]{1,0:T(8,128)(2,1)S(1)} copy-done((bf16[128,512]{1,0:T(8,128)(2,1)S(1)}, bf16[128,512]{1,0:T(8,128)(2,1)}, u32[]{:S(2)}) %copy-start) | copy-done | bytes 131096
  29.7 2.8 %shard_map.121 = (bf16[2048,256]{1,0:T(8,128)(2,1)S(1)}, bf16[2048,256]{1,0:T(8,128)(2,1)S(1)}, bf16[256,384]{1,0:T(8,128)(2,1)S(1)}, f32[4,384,512]{2,1,0:T(8,1...) custom-call(s32[1]{0:T(128)} %bitcast.place_ref, bf16[2048,128]{1,0:T(8,128)(2,1)S(1)} %bitcast.14, ...), custom_call_target="tpu_custom_call" | custom-call | tf_op jit(solution)/shard_map/pallas_call | solution.py:442
  32.5 0.9 %collective-permute-done.1.code4 = bf16[128,512]{1,0:T(8,128)(2,1)S(1)} collective-permute-done((bf16[128,512]{1,0:T(8,128)(2,1)S(1)}, bf16[128,512]{1,0:T(8,128)(2,1)S(1)}, u32[]{:S(2)}, u32[]{:S(2)}) %collective-permute-start.1) | collective-permute-done | bytes 131104 | tf_op jit(solution)/shard_map/ppermute | solution.py:44
  33.5 4.5 %collective-permute-done.2.code3 = bf16[128,512]{1,0:T(8,128)(2,1)S(1)} collective-permute-done((bf16[128,512]{1,0:T(8,128)(2,1)S(1)}, bf16[128,512]{1,0:T(8,128)(2,1)S(1)}, u32[]{:S(2)}, u32[]{:S(2)}) %collective-permute-start.2) | collective-permute-done | bytes 131104 | tf_op jit(solution)/shard_map/ppermute | solution.py:44
  38.0 0.0 copy-done.1
  38.0 4.7 %shard_map.122 = (f32[32,8,128]{2,1,0:T(8,128)}, bf16[256,512]{1,0:T(8,128)(2,1)S(1)}, f32[384,512]{1,0:T(8,128)S(1)}, bf16[2048,128]{1,0:T(8,128)(2,1)}) custom-call(s32[1]{0:T(128)} %bitcast.place_ref, bf16[128,512]{1,0:T(8,128)(2,1)S(1)} %collective-permute-done.1.code4, bf16[128,512]{1,0:T(8,128)(2,1)S(1)} %collective-permute-done.2.code3, ...), custom_call_target="tpu_custom_call" | custom-call | tf_op jit(solution)/shard_map/pallas_call | solution.py:472
  42.8 7.4 %all-to-all-start = ((f32[32,8,128]{2,1,0:T(8,128)}), f32[32,8,128]{2,1,0:T(8,128)S(1)}, u32[]{:S(2)}, u32[]{:S(2)}) async-start(f32[32,8,128]{2,1,0:T(8,128)} %get-tuple-element.27), calls=%async_computation | async-start | bytes 262144 | tf_op jit(solution)/shard_map/all_to_all | solution.py:513
  50.2 2.2 %collective-permute-start.4 = (bf16[256,512]{1,0:T(8,128)(2,1)S(1)}, bf16[256,512]{1,0:T(8,128)(2,1)S(1)}, u32[]{:S(2)}, u32[]{:S(2)}) collective-permute-start(bf16[256,512]{1,0:T(8,128)(2,1)S(1)} %get-tuple-element.30), channel_id=1, source_target_pairs={{2,0},{3,1},{4,2},{5,3},{6,4},{7,5},{8,6},{9,7},{10,8},{11,9},{12,... | collective-permute-start | bytes 786440 | tf_op jit(solution)/shard_map/ppermute | solution.py:44
  52.4 5.4 %all-to-all-done.in_ref = f32[32,8,128]{2,1,0:T(8,128)S(1)} async-done(((f32[32,8,128]{2,1,0:T(8,128)}), f32[32,8,128]{2,1,0:T(8,128)S(1)}, u32[]{:S(2)}, u32[]{:S(2)}) %all-to-all-start) | async-done | bytes 131104 | tf_op jit(solution)/shard_map/all_to_all | solution.py:513
  57.8 0.7 shard_map.123
  58.5 6.6 %all-to-all-start.1 = ((f32[16,16,128]{2,1,0:T(8,128)}), f32[16,16,128]{2,1,0:T(8,128)S(1)}, u32[]{:S(2)}, u32[]{:S(2)}) async-start(f32[16,16,128]{2,1,0:T(8,128)} %shard_map.123), calls=%async_computation.1 | async-start | bytes 262144 | tf_op jit(solution)/shard_map/all_to_all | solution.py:519
  65.1 0.6 collective-permute-done.4.back_ref
  65.7 6.1 %collective-permute-start.5 = (bf16[128,512]{1,0:T(8,128)(2,1)S(1)}, bf16[128,512]{1,0:T(8,128)(2,1)S(1)}, u32[]{:S(2)}, u32[]{:S(2)}) collective-permute-start(bf16[128,512]{1,0:T(8,128)(2,1)S(1)} %get-tuple-element.31), channel_id=1, source_target_pairs={{2,0},{3,1},{4,2},{5,3},{6,4},{7,5},{8,6},{9,7},{10,8},{11,9},{12,... | collective-permute-start | bytes 393224 | tf_op jit(solution)/shard_map/ppermute | solution.py:44
  71.8 3.4 %collective-permute-start.6 = (bf16[128,512]{1,0:T(8,128)(2,1)S(1)}, bf16[128,512]{1,0:T(8,128)(2,1)S(1)}, u32[]{:S(2)}, u32[]{:S(2)}) collective-permute-start(bf16[128,512]{1,0:T(8,128)(2,1)S(1)} %get-tuple-element.32), channel_id=1, source_target_pairs={{1,0},{2,1},{3,2},{4,3},{5,4},{6,5},{7,6},{8,7},{9,8},{10,9},{11,1... | collective-permute-start | bytes 393224 | tf_op jit(solution)/shard_map/ppermute | solution.py:44
  75.2 4.8 %collective-permute-done.5.mid_ref = bf16[128,512]{1,0:T(8,128)(2,1)S(1)} collective-permute-done((bf16[128,512]{1,0:T(8,128)(2,1)S(1)}, bf16[128,512]{1,0:T(8,128)(2,1)S(1)}, u32[]{:S(2)}, u32[]{:S(2)}) %collective-permute-start.5) | collective-permute-done | bytes 131104 | tf_op jit(solution)/shard_map/ppermute | solution.py:44
  80.0 0.0 all-to-all-done.1.all_ref
  80.0 0.7 shard_map.124
  80.8 0.4 collective-permute-done.6.near_ref
  81.2 0.8 shard_map.127
  (5 shorter events, 0.1 us)
Async XLA Ops:
  0.6 28.2 %copy-start.2 = (bf16[128,16,128]{2,1,0:T(8,128)(2,1)S(1)}, bf16[128,16,128]{2,1,0:T(8,128)(2,1)}, u32[]{:S(2)}) copy-start(bf16[128,16,128]{2,1,0:T(8,128)(2,1)} %param.9) | copy-start | bytes 1572868
  0.6 28.2 %copy-start.3 = (bf16[128,16,128]{2,1,0:T(8,128)(2,1)S(1)}, bf16[128,16,128]{2,1,0:T(8,128)(2,1)}, u32[]{:S(2)}) copy-start(bf16[128,16,128]{2,1,0:T(8,128)(2,1)} %param.10) | copy-start | bytes 1572868
  0.7 28.2 %copy-start.4 = (bf16[128,16,128]{2,1,0:T(8,128)(2,1)S(1)}, bf16[128,16,128]{2,1,0:T(8,128)(2,1)}, u32[]{:S(2)}) copy-start(bf16[128,16,128]{2,1,0:T(8,128)(2,1)} %param.11) | copy-start | bytes 1572868
  2.4 35.6 %copy-start.1 = (bf16[128,512]{1,0:T(8,128)(2,1)S(1)}, bf16[128,512]{1,0:T(8,128)(2,1)}, u32[]{:S(2)}) copy-start(bf16[128,512]{1,0:T(8,128)(2,1)} %shard_map.120.code0.code_ref) | copy-start | bytes 393220
  2.4 19.4 %collective-permute-start = (bf16[128,512]{1,0:T(8,128)(2,1)}, bf16[128,512]{1,0:T(8,128)(2,1)S(1)}, u32[]{:S(2)}, u32[]{:S(2)}) collective-permute-start(bf16[128,512]{1,0:T(8,128)(2,1)} %shard_map.120.code0.code_ref), channel_id=1, source_target_pairs={{0,2},{1,3},{2,4},{3,5},{4,6},{5,7},{6,8},{7,9},{8,10},{9,11},{10,... | collective-permute-start | bytes 393224 | tf_op jit(solution)/shard_map/ppermute | solution.py:44
  8.3 20.5 %collective-permute-start.3 = (bf16[128,512]{1,0:T(8,128)(2,1)}, bf16[128,512]{1,0:T(8,128)(2,1)S(1)}, u32[]{:S(2)}, u32[]{:S(2)}) collective-permute-start(bf16[128,512]{1,0:T(8,128)(2,1)} %shard_map.120.code0.code_ref), channel_id=1, source_target_pairs={{0,1},{1,2},{2,3},{3,4},{4,5},{5,6},{6,7},{7,8},{8,9},{9,10},{10,1... | collective-permute-start | bytes 393224 | tf_op jit(solution)/shard_map/ppermute | solution.py:44
  21.8 11.7 %collective-permute-start.1 = (bf16[128,512]{1,0:T(8,128)(2,1)S(1)}, bf16[128,512]{1,0:T(8,128)(2,1)S(1)}, u32[]{:S(2)}, u32[]{:S(2)}) collective-permute-start(bf16[128,512]{1,0:T(8,128)(2,1)S(1)} %collective-permute-done.code2), channel_id=1, source_target_pairs={{0,2},{1,3},{2,4},{3,5},{4,6},{5,7},{6,8},{7,9},{8,10},{9,11},{10,... | collective-permute-start | bytes 393224 | tf_op jit(solution)/shard_map/ppermute | solution.py:44
  23.7 14.3 %collective-permute-start.2 = (bf16[128,512]{1,0:T(8,128)(2,1)S(1)}, bf16[128,512]{1,0:T(8,128)(2,1)S(1)}, u32[]{:S(2)}, u32[]{:S(2)}) collective-permute-start(bf16[128,512]{1,0:T(8,128)(2,1)S(1)} %collective-permute-done.code2), channel_id=1, source_target_pairs={{0,1},{1,2},{2,3},{3,4},{4,5},{5,6},{6,7},{7,8},{8,9},{9,10},{10,1... | collective-permute-start | bytes 393224 | tf_op jit(solution)/shard_map/ppermute | solution.py:44
  28.8 0.9 %copy-start = (bf16[128,512]{1,0:T(8,128)(2,1)S(1)}, bf16[128,512]{1,0:T(8,128)(2,1)}, u32[]{:S(2)}) copy-start(bf16[128,512]{1,0:T(8,128)(2,1)} %shard_map.120.code0.code_ref) | copy-start | bytes 393220
  42.8 15.0 %all-to-all-start = ((f32[32,8,128]{2,1,0:T(8,128)}), f32[32,8,128]{2,1,0:T(8,128)S(1)}, u32[]{:S(2)}, u32[]{:S(2)}) async-start(f32[32,8,128]{2,1,0:T(8,128)} %get-tuple-element.27), calls=%async_computation | async-start | bytes 262144 | tf_op jit(solution)/shard_map/all_to_all | solution.py:513
  50.2 15.5 %collective-permute-start.4 = (bf16[256,512]{1,0:T(8,128)(2,1)S(1)}, bf16[256,512]{1,0:T(8,128)(2,1)S(1)}, u32[]{:S(2)}, u32[]{:S(2)}) collective-permute-start(bf16[256,512]{1,0:T(8,128)(2,1)S(1)} %get-tuple-element.30), channel_id=1, source_target_pairs={{2,0},{3,1},{4,2},{5,3},{6,4},{7,5},{8,6},{9,7},{10,8},{11,9},{12,... | collective-permute-start | bytes 786440 | tf_op jit(solution)/shard_map/ppermute | solution.py:44
  58.5 21.6 %all-to-all-start.1 = ((f32[16,16,128]{2,1,0:T(8,128)}), f32[16,16,128]{2,1,0:T(8,128)S(1)}, u32[]{:S(2)}, u32[]{:S(2)}) async-start(f32[16,16,128]{2,1,0:T(8,128)} %shard_map.123), calls=%async_computation.1 | async-start | bytes 262144 | tf_op jit(solution)/shard_map/all_to_all | solution.py:519
  65.7 14.3 %collective-permute-start.5 = (bf16[128,512]{1,0:T(8,128)(2,1)S(1)}, bf16[128,512]{1,0:T(8,128)(2,1)S(1)}, u32[]{:S(2)}, u32[]{:S(2)}) collective-permute-start(bf16[128,512]{1,0:T(8,128)(2,1)S(1)} %get-tuple-element.31), channel_id=1, source_target_pairs={{2,0},{3,1},{4,2},{5,3},{6,4},{7,5},{8,6},{9,7},{10,8},{11,9},{12,... | collective-permute-start | bytes 393224 | tf_op jit(solution)/shard_map/ppermute | solution.py:44
  71.8 9.3 %collective-permute-start.6 = (bf16[128,512]{1,0:T(8,128)(2,1)S(1)}, bf16[128,512]{1,0:T(8,128)(2,1)S(1)}, u32[]{:S(2)}, u32[]{:S(2)}) collective-permute-start(bf16[128,512]{1,0:T(8,128)(2,1)S(1)} %get-tuple-element.32), channel_id=1, source_target_pairs={{1,0},{2,1},{3,2},{4,3},{5,4},{6,5},{7,6},{8,7},{9,8},{10,9},{11,1... | collective-permute-start | bytes 393224 | tf_op jit(solution)/shard_map/ppermute | solution.py:44
